TPU v7x, 32 devices: a whole 2x2x4 slice. The times are simulated.
32 devices in a mesh: groups: 2 (over x), hid: 16 (over z, y, core).
Axes of the slice: x: 2, y: 2, z: 4, core: 2. Of those that a mesh axis runs over, the one named last changes fastest.
Arguments:
- tokens: bfloat16 [8, 32, 6144], P('groups', 'hid'), parts along dimension 0, may hold values from -6 to 6
- w_gate: bfloat16 [4, 6144, 8192], P(None, None, 'hid'), may hold values from -0.078125 to 0.078125
- w_up: bfloat16 [4, 6144, 8192], P(None, None, 'hid'), may hold values from -0.078125 to 0.078125
- w_down: bfloat16 [4, 8192, 6144], P(None, 'hid'), may hold values from -0.0625 to 0.0625
- expert_ids: int32 [8, 32, 2], P('groups'), parts along dimension 0, may hold values from 0 to 3, all different within a row
- gate_weights: bfloat16 [8, 32, 2], P('groups'), parts along dimension 0, may hold values from 0.099609375 to 0.8984375
- return_order: int32 [8, 32], P('groups'), parts along dimension 0, may hold values from 0 to 31, each once within a row
Outputs:
- expert_out: bfloat16 [8, 32, 6144], P('groups', 'hid'), parts along dimension 0
There are 2 independent parts, one for each index of `groups`. A program takes and returns all parts, laid end to end along the dimension named above; an argument that names none is the same for every part. Nothing has to cross between parts.
Inputs may be any that keep to these rules, and one draw needn't show every extreme that they name: `expert_ids`: each row names 2 different experts. `return_order`: each step's row is a permutation of the 32 rows.
All inputs are finite; a program needn't handle non-finite values.
Results may differ from a plain program's by a relative error of at most 0.0049.
Values may be sent and summed in bfloat16 or wider, within the bound.
No kernel may reach another device: no remote copies, remote signals or barrier semaphores. Data moves between devices by JAX's collectives and lax.ppermute only.
A program may use at most 192 MiB of HBM per device.

v0:
```python
import jax
import jax.numpy as jnp
from jax import lax
from jax.sharding import PartitionSpec as P


def route_table(expert_ids, gate_weights, num_experts):
    labels = jnp.arange(num_experts, dtype=jnp.int32)
    chosen = expert_ids[..., None] == labels
    return jnp.sum(
        jnp.where(chosen, gate_weights[..., None].astype(jnp.float32), jnp.float32(0.0)), axis=-2
    )


def hidden_of(token_rows, route_rows, w_gate, w_up):
    gate_part = jnp.einsum("nd,edf->nef", token_rows, w_gate, preferred_element_type=jnp.float32)
    up_part = jnp.einsum("nd,edf->nef", token_rows, w_up, preferred_element_type=jnp.float32)
    hidden = jax.nn.silu(gate_part) * up_part * route_rows[:, :, None]
    return hidden.reshape(token_rows.shape[0], -1).astype(jnp.bfloat16)


def run_block(block_tokens, block_route, block_order, w_gate, w_up, down_flat):
    step_count, own_rows, model_width = block_tokens.shape
    total_rows = block_order.shape[1]
    num_experts = block_route.shape[2]
    gathered = lax.all_gather(block_tokens, "hid", axis=1, tiled=True)
    gathered = jnp.take_along_axis(gathered, block_order[:, :, None], axis=1)
    routed = jnp.take_along_axis(block_route, block_order[:, :, None], axis=1)
    hidden = hidden_of(
        gathered.reshape(-1, model_width), routed.reshape(-1, num_experts), w_gate, w_up
    )
    hidden = hidden.reshape(step_count, total_rows, -1)
    by_row = jnp.transpose(hidden, (1, 0, 2))
    row_count = own_rows * lax.axis_size("hid")
    summed = jnp.dot(
        by_row.reshape(row_count * step_count, -1), down_flat, preferred_element_type=jnp.float32
    )
    shares = lax.psum_scatter(
        summed.reshape(row_count, step_count * model_width), "hid", scatter_dimension=0, tiled=True
    )
    return jnp.transpose(shares.reshape(own_rows, step_count, model_width), (1, 0, 2)).astype(
        jnp.bfloat16
    )


def body(tokens, w_gate, w_up, w_down, expert_ids, gate_weights, return_order):
    num_experts = w_gate.shape[0]
    routing = route_table(expert_ids, gate_weights, num_experts)
    down_flat = w_down.reshape(-1, w_down.shape[2])
    return run_block(tokens, routing, return_order, w_gate, w_up, down_flat)


def solution(mesh):
    in_specs = (
        P("groups", "hid", None),
        P(None, None, "hid"),
        P(None, None, "hid"),
        P(None, "hid", None),
        P("groups", None, None),
        P("groups", None, None),
        P("groups", None),
    )
    out_specs = P("groups", "hid", None)
    return jax.shard_map(body, mesh=mesh, in_specs=in_specs, out_specs=out_specs, check_vma=False)
```

profile of v0, /device:TPU:0, one launch (start us, length us, event | category | flops | bytes accessed | tf_op | source)
XLA Modules:
  0.0 183.8 jit_solution(7139665983004370129)
XLA Ops:
  6.5 1.6 copy.24
  8.2 0.7 bitcast_or_fusion
  8.8 0.1 reshape.50
  8.9 0.7 compare_and_fusion
  9.6 0.1 broadcast_in_dim.35
  9.7 0.7 convert_element_type.20
  10.4 0.7 select_reduce_fusion
  11.1 0.1 copy.26
  11.2 1.2 gather_fusion.1
  12.4 0.1 broadcast_select_fusion.3
  12.6 1.3 dynamic-slice
  14.5 37.6 %all-gather.2.cloned.1.call-done = bf16[4,32,6144]{2,0,1:T(4,128)(2,1)} async-done(((bf16[4,2,6144]{2,0,1:T(4,128)(2,1)}), bf16[4,32,6144]{2,0,1:T(4,128)(2,1)}) %all-gather.2.cloned.1.call-update) | async-done | bytes 1572880 | tf_op jit(solution)/shard_map/all_gather | solution.py:26
  52.0 2.3 %copy.25 = bf16[4,32,6144]{2,1,0:T(8,128)(2,1)S(1)} copy(bf16[4,32,6144]{2,0,1:T(4,128)(2,1)} %all-gather.2.cloned.1.call-done) | data formatting | bytes 3145728 | tf_op jit(solution)/shard_map/all_gather | solution.py:26
  54.3 5.4 %gather_fusion = bf16[128,6144]{1,0:T(8,128)(2,1)S(1)} fusion(bf16[4,32,6144]{2,1,0:T(8,128)(2,1)S(1)} %copy.25, s32[128]{0:T(128)S(1)} %reshape.50), kind=kCustom, calls=%fused_computation | custom fusion | bytes 3146752 | tf_op jit(solution)/shard_map/jit(take_along_axis)/gather | solution.py:27
  59.7 10.2 %fusion.2 = f32[128,4,512]{2,0,1:T(8,128)S(1)} fusion(bf16[4,6144,512]{2,1,0:T(8,128)(2,1)} %param.8, bf16[128,6144]{1,0:T(8,128)(2,1)S(1)} %gather_fusion, pred[128]{0:T(512)(128)(4,1)S(1)} %broadcast_in_dim.35), kind=kOutput, calls=%fused_computation.4 | convolution fusion | flops 3222011904 | bytes 27787392 | tf_op jit(solution)/shard_map/nd,edf->nef/dot_general | solution.py:16
  70.0 11.9 %fusion.10 = bf16[128,4,512]{2,0,1:T(8,128)(2,1)S(1)} fusion(bf16[4,6144,512]{2,1,0:T(8,128)(2,1)} %param.9, f32[128,4,512]{2,0,1:T(8,128)S(1)} %fusion.2, bf16[128,6144]{1,0:T(8,128)(2,1)S(1)} %gather_fusion, pred[128]{0:T(512)(128)(4,1)S(1)} %broadcast_in_dim.35, f32[128,4]{0,1:T(4,128)S(1)} %copy.27), kind=kOutput, calls=%fused_computation.9 | convolution fusion | flops 3223846912 | bytes 28313728 | tf_op jit(solution)/shard_map/nd,edf->nef/dot_general | solution.py:17
  81.9 0.4 copy.28
  82.3 0.4 convert_element_type.22
  82.7 0.4 copy.29
  83.1 0.1 reshape.47
  83.3 13.3 %fusion.15 = f32[128,6144]{1,0:T(8,128)} fusion(bf16[128,2048]{1,0:T(8,128)(2,1)S(1)} %reshape.47, bf16[2048,6144]{1,0:T(8,128)(2,1)} %bitcast.25), kind=kOutput, calls=%fused_computation.19 | convolution fusion | flops 3221225472 | bytes 28835840 | tf_op jit(solution)/shard_map/dot_general | solution.py:35
  96.5 2.9 %reshape.49 = f32[32,24576]{1,0:T(8,128)S(1)} reshape(f32[128,6144]{1,0:T(8,128)} %fusion.15) | data formatting | bytes 6291456 | tf_op jit(solution)/shard_map/reshape | solution.py:39
  99.4 75.9 %all-reduce.2 = bf16[32,24576]{1,0:T(8,128)(2,1)} all-reduce(f32[32,24576]{1,0:T(8,128)S(1)} %reshape.49), channel_id=2, replica_groups=mesh['groups'=2,'hid'=16] {'hid'}, use_global_device_ids=true, to_apply=%region_1.2.clone | all-reduce | flops 786432 | bytes 4718592
  175.3 1.7 dynamic-slice_convert_fusion
  (3 shorter events, 0.1 us)
Async XLA Ops:
  6.5 45.5 %all-gather.2.cloned.1.call-start = ((), (), s32[]{:S(2)}) async-start(), calls=%async_computation | async-start | bytes 1671168 | tf_op jit(solution)/shard_map/all_gather | solution.py:26
Sparse Core Ops, SparseCore 0:
  9.6 42.3 all-gather.1
where the time goes:
time: 184 us
  blocking collectives  75.9 us (41%)
  waiting for transfers between devices  37.6 us (20%)
  matrix products  35.4 us (19%)
  local copies, waits for them, and re-layouts  18 us (10%)
  between operations  14.1 us (8%)
  other arithmetic  2.85 us (2%)
    unnamed x1, blocking collectives  75.9 us
    all_gather x1, waiting for transfers between devices, run_block(): gathered = lax.all_gather(block_tokens, 'hid', axis=1, tiled=True)  37.6 us
    dot_general x1, matrix products, run_block(): jnp.dot(by_row.reshape(row_count * step_count, -1), down_flat, preferred_...  13.3 us
    dot_general x1, matrix products, hidden_of(): jnp.einsum('nd,edf->nef', token_rows, w_up, preferred_element_type=jnp.fl...  11.9 us
    dot_general x1, matrix products, hidden_of(): jnp.einsum('nd,edf->nef', token_rows, w_gate, preferred_element_type=jnp....  10.2 us
    gather x2, local copies, waits for them, and re-layouts, run_block(): gathered = jnp.take_along_axis(gathered, block_order[:, :, None], axis=1)  5.48 us
  transfers between devices with their start and end apart: 1, of which 1 were waited for; matrix products, arithmetic and copies ran while one was open for 3% of the time, Pallas kernels for 0%

commit v1 on v0

v1 whole, which is shorter than its diff:
```python
import functools

import jax
import jax.numpy as jnp
from jax import lax
from jax.experimental import pallas as pl
from jax.experimental.pallas import tpu as pltpu
from jax.sharding import PartitionSpec as P

MIB = 1 << 20
ARENA = 30 * MIB
SCOPED = 24
VMEM = pl.BlockSpec(memory_space=pltpu.VMEM)
ANY = pl.BlockSpec(memory_space=pl.ANY)
BF16, F32 = jnp.bfloat16, jnp.float32


def in_vmem(x):
    return pltpu.with_memory_space_constraint(x, pltpu.VMEM)


def in_hbm(x):
    return pltpu.with_memory_space_constraint(x, pltpu.HBM)


def cost(flops, size):
    return pl.CostEstimate(flops=flops, bytes_accessed=size, transcendentals=0)


def swap(x, mask):
    n = lax.axis_size("hid")
    return lax.ppermute(x, "hid", [(i, i ^ mask) for i in range(n)])


def split_kernel(tokens_ref, *out_refs):
    steps, own, _ = tokens_ref.shape
    first = 0
    for out_ref in out_refs:
        columns = out_ref.shape[1]
        for s in range(steps):
            out_ref[s * own : (s + 1) * own] = tokens_ref[s, :, first : first + columns]
        first += columns


def split(tokens, widths):
    steps, own, _ = tokens.shape
    return pl.pallas_call(
        split_kernel,
        in_specs=[VMEM],
        out_specs=[VMEM] * len(widths),
        out_shape=[pltpu.VMEM((steps * own, w), tokens.dtype) for w in widths],
        compiler_params=pltpu.CompilerParams(vmem_limit_bytes=2 * MIB),
        cost_estimate=cost(0, 4 * tokens.size),
        name="split",
    )(in_vmem(tokens))


def stack_kernel(places, *refs):
    *part_refs, out_ref = refs[: len(places)] + refs[-1:]
    for part_ref, (column, rows) in zip(part_refs, places):
        columns = part_ref.shape[1]
        per = part_ref.shape[0] // len(rows)
        for i, row in enumerate(rows):
            out_ref[row * per : (row + 1) * per, column : column + columns] = part_ref[i * per : (i + 1) * per]


def stack(parts, places, shape, after):
    return pl.pallas_call(
        functools.partial(stack_kernel, places),
        in_specs=[VMEM] * len(parts) + [ANY],
        out_specs=VMEM,
        out_shape=pltpu.VMEM(shape, parts[0].dtype),
        compiler_params=pltpu.CompilerParams(vmem_limit_bytes=2 * MIB),
        cost_estimate=cost(0, 4 * shape[0] * shape[1]),
        name="stack",
    )(*[in_vmem(part) for part in parts], after)


def load_kernel(pieces, gate_ref, up_ref, after_ref, out_ref, token_ref, sem):
    width = gate_ref.shape[1]
    copies = []
    for i, piece in enumerate(pieces):
        source = up_ref if piece % 2 else gate_ref
        copies.append(pltpu.make_async_copy(source.at[piece // 2], out_ref.at[pl.ds(i * width, width)], sem.at[i]))
    for copy in copies:
        copy.start()
    token_ref[...] = jnp.zeros_like(token_ref)
    for copy in copies:
        copy.wait()


def load(w_gate, w_up, after, pieces):
    _, width, units = w_gate.shape
    return pl.pallas_call(
        functools.partial(load_kernel, pieces),
        in_specs=[ANY, ANY, ANY],
        out_specs=[VMEM, VMEM],
        out_shape=[pltpu.VMEM((len(pieces) * width, units), w_gate.dtype), pltpu.VMEM((8, 128), F32)],
        scratch_shapes=[pltpu.SemaphoreType.DMA((len(pieces),))],
        compiler_params=pltpu.CompilerParams(vmem_limit_bytes=2 * MIB),
        cost_estimate=cost(0, 2 * len(pieces) * width * units),
        name="load",
    )(in_hbm(w_gate), in_hbm(w_up), after)


def place_of(row, n, steps, own, me):
    per = steps * own
    slot, rest = row // per, row % per
    far = n // 4
    mask = slot // (2 * far) + 2 * ((slot // far) % 2) + 4 * (slot % far)
    return (rest // own) * (n * own) + (me ^ mask) * own + rest % own


def experts_kernel(
    n, steps, own, loads, blocks, half_ref, other_ref, table_ref, gate_ref, up_ref, down_ref, *refs
):
    refs = refs[loads:]
    (h_ref, keep_ref, send_ref), arena_refs = refs[:3], refs[3 : 3 + loads]
    x_ref, rest_ref, route, order, rest_sem, down_sem = refs[3 + loads :]
    half, width = half_ref.shape
    rows = 2 * half
    experts, units, _ = down_ref.shape
    depth = experts * units
    homes = [ref.at[pl.ds(i, width)] for ref in arena_refs for i in range(0, ref.shape[0], width)]
    count = len(homes)
    spares = [rest_ref.at[pl.ds(i, width)] for i in range(0, rest_ref.shape[0], width)]
    late = []
    for p in range(count, 2 * experts):
        at = p - count
        home = spares[at] if at < len(spares) else homes[at - len(spares)]
        source = (up_ref if p % 2 else gate_ref).at[p // 2]
        late.append((home, pltpu.make_async_copy(source, home, rest_sem.at[at])))
    taken = max(len(late) - len(spares), 0)
    for _, copy in late[:2]:
        copy.start()
    x_ref[:half] = half_ref[...]
    x_ref[half:] = other_ref[...]

    me = lax.axis_index("hid")
    shape = (rows, rows)
    down = lax.broadcasted_iota(jnp.int32, shape, 0)
    across = lax.broadcasted_iota(jnp.int32, shape, 1)
    pick = (place_of(down, n, steps, own, me) == across).astype(BF16)
    mine = jnp.dot(pick, table_ref[...].astype(BF16), preferred_element_type=F32)
    step = (lax.broadcasted_iota(jnp.int32, (rows, 1), 0) % (steps * own)) // own
    source = mine[:, 4:5].astype(jnp.int32) + step * (n * own)
    order[...] = (place_of(across, n, steps, own, me) == source).astype(BF16)
    for e in range(experts):
        route[e] = jnp.where(mine[:, 0:1] == e, mine[:, 2:3], 0.0) + jnp.where(
            mine[:, 1:2] == e, mine[:, 3:4], 0.0
        )

    fit = width // depth

    def block_home(b):
        return homes[taken + b // fit].at[pl.ds(b % fit * depth, depth)]

    def block_copies(b):
        return [
            pltpu.make_async_copy(
                down_ref.at[e, :, pl.ds(b * units, units)],
                block_home(b).at[pl.ds(e * units, units)],
                down_sem.at[b, e],
            )
            for e in range(experts)
        ]

    def piece(p):
        if p < count:
            return homes[p][...]
        home, copy = late[p - count]
        copy.wait()
        return home[...]

    begun = 0
    for e in range(experts):
        gate = jnp.dot(x_ref[...], piece(2 * e), preferred_element_type=F32)
        up = jnp.dot(x_ref[...], piece(2 * e + 1), preferred_element_type=F32)
        if e == 0:
            for _, copy in late[2:]:
                copy.start()
        free = (min(2 * (e + 1), count) - taken) * fit
        until = blocks if e == experts - 1 else min(-(-blocks * e // experts), free)
        for b in range(begun, until):
            for copy in block_copies(b):
                copy.start()
        begun = until
        hidden = gate / (1.0 + jnp.exp(-gate)) * up * route[e]
        hidden = jnp.dot(order[...], hidden.astype(BF16), preferred_element_type=F32)
        h_ref[:, e * units : (e + 1) * units] = hidden.astype(BF16)
    for b in range(blocks):
        for copy in block_copies(b):
            copy.wait()
        total = jnp.dot(h_ref[...], block_home(b)[...], preferred_element_type=F32)
        keep_ref[:, b * units : (b + 1) * units] = total[:half]
        send_ref[:, b * units : (b + 1) * units] = total[half:].astype(BF16)


def experts_of(half, other, table, w_gate, w_up, w_down, arena, blocks, n, steps, own):
    experts, units, width = w_down.shape
    rows = 2 * half.shape[0]
    columns = blocks * units
    rest = max(2 * experts - sum(buffer.shape[0] for buffer in arena) // width, 1)
    h, keep, send, *_ = pl.pallas_call(
        functools.partial(experts_kernel, n, steps, own, len(arena), blocks),
        in_specs=[VMEM] * 3 + [ANY] * 3 + [VMEM] * len(arena),
        out_specs=[VMEM] * (3 + len(arena)),
        out_shape=[
            pltpu.VMEM((rows, experts * units), BF16),
            pltpu.VMEM((rows // 2, columns), F32),
            pltpu.VMEM((rows // 2, columns), BF16),
        ]
        + [pltpu.VMEM(buffer.shape, buffer.dtype) for buffer in arena],
        scratch_shapes=[
            pltpu.VMEM((rows, width), BF16),
            pltpu.VMEM((max(rest - 1, 1) * width, units), BF16),
            pltpu.VMEM((experts, rows, 1), F32),
            pltpu.VMEM((rows, rows), BF16),
            pltpu.SemaphoreType.DMA((rest,)),
            pltpu.SemaphoreType.DMA((blocks, experts)),
        ],
        input_output_aliases={6 + i: 3 + i for i in range(len(arena))},
        compiler_params=pltpu.CompilerParams(vmem_limit_bytes=SCOPED * MIB),
        cost_estimate=cost(6 * rows * w_down.size, 2 * w_down.size),
        name="experts",
    )(
        in_vmem(half), in_vmem(other), in_vmem(table), in_hbm(w_gate), in_hbm(w_up), in_hbm(w_down),
        *[in_vmem(buffer) for buffer in arena],
    )
    return h, keep, send


def down_kernel(first, h_ref, down_ref, keep_ref, send_ref, w_ref, sem):
    half = keep_ref.shape[0]
    experts, units, _ = down_ref.shape
    blocks = w_ref.shape[0]
    copies = [
        [
            pltpu.make_async_copy(
                down_ref.at[e, :, pl.ds((first + b) * units, units)], w_ref.at[b, pl.ds(e * units, units)], sem.at[b, e]
            )
            for e in range(experts)
        ]
        for b in range(blocks)
    ]
    for block in copies:
        for copy in block:
            copy.start()
    for b, block in enumerate(copies):
        for copy in block:
            copy.wait()
        total = jnp.dot(h_ref[...], w_ref[b], preferred_element_type=F32)
        keep_ref[:, b * units : (b + 1) * units] = total[:half]
        send_ref[:, b * units : (b + 1) * units] = total[half:].astype(BF16)


def down(h, w_down, first, blocks):
    experts, units, _ = w_down.shape
    rows, depth = h.shape
    half, columns = rows // 2, blocks * units
    return pl.pallas_call(
        functools.partial(down_kernel, first),
        in_specs=[VMEM, ANY],
        out_specs=[VMEM] * 2,
        out_shape=[pltpu.VMEM((half, columns), F32), pltpu.VMEM((half, columns), BF16)],
        scratch_shapes=[pltpu.VMEM((blocks, depth, units), BF16), pltpu.SemaphoreType.DMA((blocks, experts))],
        compiler_params=pltpu.CompilerParams(vmem_limit_bytes=16 * MIB),
        cost_estimate=cost(2 * rows * depth * columns, 2 * depth * columns),
        name="down",
    )(in_vmem(h), in_hbm(w_down))


def add_kernel(groups, keep_ref, got_ref, *out_refs):
    count = sum(len(group) for group in groups)
    per = keep_ref.shape[0] // count
    for group, out_ref in zip(groups, out_refs):
        for i, block in enumerate(group):
            rows = slice(block * per, (block + 1) * per)
            total = keep_ref[rows] + got_ref[rows].astype(F32)
            out_ref[i * per : (i + 1) * per] = total.astype(out_ref.dtype)


def add(keep, got, groups):
    per = keep.shape[0] // sum(len(group) for group in groups)
    columns = keep.shape[1]
    return pl.pallas_call(
        functools.partial(add_kernel, groups),
        in_specs=[VMEM, VMEM],
        out_specs=[VMEM] * len(groups),
        out_shape=[pltpu.VMEM((per * len(g), columns), BF16 if i else F32) for i, g in enumerate(groups)],
        compiler_params=pltpu.CompilerParams(vmem_limit_bytes=2 * MIB),
        cost_estimate=cost(0, 8 * keep.size),
        name="add",
    )(in_vmem(keep), in_vmem(got))


def sum_kernel(far, *refs):
    *part_refs, out_ref = refs
    first = 0
    steps, own, _ = out_ref.shape
    for keep_ref, got_refs in ((part_refs[0], part_refs[1:far]), (part_refs[far], part_refs[far + 1 :])):
        total = keep_ref[...]
        for got_ref in got_refs:
            total = total + got_ref[...].astype(F32)
        total = total.astype(out_ref.dtype)
        columns = keep_ref.shape[1]
        for s in range(steps):
            out_ref[s, :, first : first + columns] = total[s * own : (s + 1) * own]
        first += columns


def body(tokens, w_gate, w_up, w_down, expert_ids, gate_weights, return_order):
    steps, own, width = tokens.shape
    experts, _, units = w_gate.shape
    n = lax.axis_size("hid")
    far = n // 4
    per = steps * own
    rows = per * n
    table = jnp.concatenate(
        [expert_ids.astype(F32), gate_weights.astype(F32), return_order[..., None].astype(F32)], axis=-1
    ).reshape(rows, 5)

    blocks = width // units
    lead = (2 * blocks + 2) // 3
    a = lead * units
    b = width - a
    count = min(2 * experts, ARENA // (2 * width * units))
    cuts = [count // 4, 3 * count // 4, count]
    pieces = [range(0, cuts[0]), range(cuts[0], cuts[1]), range(cuts[1], cuts[2])]
    xa, xb = split(tokens, [a, b])
    za = [swap(xa, 4 * z) for z in range(1, far)]
    yb = swap(xb, 2)
    arena0, ready = load(w_gate, w_up, table, pieces[0])
    xb = stack([xb, yb], [(0, [0]), (0, [1])], (2 * per, b), ready)
    zb = [swap(xb, 4 * z) for z in range(1, far)]
    arena1, ready = load(w_gate, w_up, xb, pieces[1])
    xa = stack([xa] + za, [(0, [z]) for z in range(far)], (far * per, a), ready)
    ya = swap(xa, 2)
    arena2, ready = load(w_gate, w_up, xa, pieces[2])
    half = stack(
        [xa, ya, xb] + zb,
        [(0, [0]), (0, [1])] + [(a, [z, far + z]) for z in range(far)],
        (2 * far * per, width),
        ready,
    )
    other = swap(half, 1)
    h, keep_a, send_a = experts_of(half, other, table, w_gate, w_up, w_down, [arena0, arena1, arena2], lead, n, steps, own)
    got_a = swap(send_a, 1)
    keep_b, send_b = down(h, w_down, lead, blocks - lead)
    got_b = swap(send_b, 1)
    keep_a, send_a = add(keep_a, got_a, [list(range(far)), list(range(far, 2 * far))])
    got_a = swap(send_a, 2)
    keep_b, *send_b = add(keep_b, got_b, [[z, far + z] for z in range(far)])
    got_b = [swap(send, 4 * (z + 1)) for z, send in enumerate(send_b)]
    keep_a, *send_a = add(keep_a, got_a, [[z] for z in range(far)])
    got_a = [swap(send, 4 * (z + 1)) for z, send in enumerate(send_a)]
    total_b = keep_b
    for got in got_b:
        total_b = total_b + got.astype(F32)
    keep_b, send_b = total_b[:per], total_b[per:].astype(BF16)
    parts = [keep_a, *got_a, keep_b, swap(send_b, 2)]
    return pl.pallas_call(
        functools.partial(sum_kernel, far),
        in_specs=[VMEM] * len(parts),
        out_specs=VMEM,
        out_shape=jax.ShapeDtypeStruct(tokens.shape, tokens.dtype),
        compiler_params=pltpu.CompilerParams(vmem_limit_bytes=4 * MIB),
        cost_estimate=cost(0, 4 * tokens.size),
        name="sum",
    )(*[in_vmem(part) for part in parts])


def solution(mesh):
    in_specs = (
        P("groups", "hid", None),
        P(None, None, "hid"),
        P(None, None, "hid"),
        P(None, "hid", None),
        P("groups", None, None),
        P("groups", None, None),
        P("groups", None),
    )
    out_specs = P("groups", "hid", None)
    return jax.shard_map(body, mesh=mesh, in_specs=in_specs, out_specs=out_specs, check_vma=False)
```

time: 184 us -> 70.1 us (0.38)
  blocking collectives: 75.9 us -> 0 us
  matrix products: 35.4 us -> 0 us
  Pallas kernels: 0 us -> 32.3 us
  waiting for transfers between devices: 37.6 us -> 8.66 us
  starting transfers between devices: 0.01 us -> 25.3 us
  local copies, waits for them, and re-layouts: 18 us -> 1.96 us
  between operations: 14.1 us -> 0.18 us
    unnamed x1 -> x0, blocking collectives: 75.9 us -> none
    all_gather x1 -> x0, waiting for transfers between devices: 37.6 us -> none  [run_block(): gathered = lax.all_gather(block_tokens, 'hid', axis=1, tiled=True)]
    dot_general x3 -> x0, matrix products: 35.4 us -> none  [the longest x1 13.3 us: run_block(): jnp.dot(by_row.reshape(row_count * step_count, -1), down_flat, preferred_...]
    pallas_call x0 -> x13, Pallas kernels: none -> 32.3 us  [the longest x1 15.1 us: experts_of(): pl.pallas_call(functools.partial(experts_kernel, n, steps, own, len(arena...]
    ppermute x0 -> x19, starting transfers between devices: none -> 25.3 us  [swap(): return lax.ppermute(x, 'hid', [(i, i ^ mask) for i in range(n)])]
    ppermute x0 -> x19, waiting for transfers between devices: none -> 8.66 us  [swap(): return lax.ppermute(x, 'hid', [(i, i ^ mask) for i in range(n)])]
    gather x3 -> x0, local copies, waits for them, and re-layouts: 6.71 us -> none  [the longest x2 5.48 us: run_block(): gathered = jnp.take_along_axis(gathered, block_order[:, :, None], axis=1)]
    reshape x2 -> x0, local copies, waits for them, and re-layouts: 2.98 us -> none  [the longest x1 2.85 us: run_block(): summed.reshape(row_count, step_count * model_width)]
  transfers between devices with their start and end apart: 1 -> 19, of which waited for: 1 -> 4; matrix products, arithmetic and copies ran while one was open for 3% -> 4% of each run, Pallas kernels for 0% -> 23%
where the time goes in v1:
time: 70.1 us; the launch traced here: 69.8 us
  Pallas kernels  32.3 us (46%)
  starting transfers between devices  25.3 us (36%)
  waiting for transfers between devices  8.66 us (12%)
  local copies, waits for them, and re-layouts  1.96 us (3%)
  other arithmetic  1.42 us (2%)
    ppermute x19, starting transfers between devices, swap(): return lax.ppermute(x, 'hid', [(i, i ^ mask) for i in range(n)])  25.3 us
    pallas_call x1, Pallas kernels, experts_of(): pl.pallas_call(functools.partial(experts_kernel, n, steps, own, len(arena...  15.1 us
    pallas_call x3, Pallas kernels, load(): pl.pallas_call(functools.partial(load_kernel, pieces), in_specs=[ANY, ANY...  12.1 us
    ppermute x19, waiting for transfers between devices, swap(): return lax.ppermute(x, 'hid', [(i, i ^ mask) for i in range(n)])  8.66 us
    pallas_call x1, Pallas kernels, down(): pl.pallas_call(functools.partial(down_kernel, first), in_specs=[VMEM, ANY...  4.02 us
  transfers between devices with their start and end apart: 19, of which 4 were waited for; matrix products, arithmetic and copies ran while one was open for 4% of the time, Pallas kernels for 23%

profile of v1, /device:TPU:0, one launch (start us, length us, event | category | flops | bytes accessed | tf_op | source)
XLA Modules:
  0.0 69.8 jit_solution(15260516608505805035)
XLA Ops:
  0.0 0.9 %copy-done = bf16[4,2,6144]{2,1,0:T(2,128)(2,1)S(1)} copy-done((bf16[4,2,6144]{2,1,0:T(2,128)(2,1)S(1)}, bf16[4,2,6144]{2,1,0:T(2,128)(2,1)}, u32[]{:S(2)}) %copy-start) | copy-done | bytes 98328
  1.0 5.1 %collective-permute-start.2 = (bf16[8,4096]{1,0:T(8,128)(2,1)S(1)}, bf16[8,4096]{1,0:T(8,128)(2,1)S(1)}, u32[]{:S(2)}, u32[]{:S(2)}) collective-permute-start(bf16[8,4096]{1,0:T(8,128)(2,1)S(1)} %get-tuple-element.28.refs_0_), channel_id=1, source_target_pairs={{0,12},{1,13},{2,14},{3,15},{4,8},{5,9},{6,10},{7,11},{8,4},{9,5},... | collective-permute-start | bytes 196616 | tf_op jit(solution)/shard_map/ppermute | solution.py:32
  6.7 1.7 %collective-permute-start.3 = (bf16[8,2048]{1,0:T(8,128)(2,1)S(1)}, bf16[8,2048]{1,0:T(8,128)(2,1)S(1)}, u32[]{:S(2)}, u32[]{:S(2)}) collective-permute-start(bf16[8,2048]{1,0:T(8,128)(2,1)S(1)} %get-tuple-element.29.refs_0_), channel_id=1, source_target_pairs={{0,2},{1,3},{2,0},{3,1},{4,6},{5,7},{6,4},{7,5},{8,10},{9,11},{10,... | collective-permute-start | bytes 98312 | tf_op jit(solution)/shard_map/ppermute | solution.py:32
  8.4 0.7 convert_element_type.19
  9.1 0.7 convert_element_type.18
  9.9 0.7 copy.15
  10.8 2.8 %load.3 = (bf16[6144,512]{1,0:T(8,128)(2,1)S(1)}, f32[8,128]{1,0:T(8,128)S(1)}) custom-call(bf16[4,6144,512]{2,1,0:T(8,128)(2,1)} %gate_ref.7, bf16[4,6144,512]{2,1,0:T(8,128)(2,1)} %up_ref.7, f32[128,5]{1,0:T(8,128)S(1)} %copy.16.after_ref.table_ref), custom_call_target="tpu_custom_call" | custom-call | bytes 6291456 | tf_op jit(solution)/shard_map/load/pallas_call | solution.py:94
  13.7 4.6 %load.4 = (bf16[12288,512]{1,0:T(8,128)(2,1)S(1)}, f32[8,128]{1,0:T(8,128)S(1)}) custom-call(bf16[4,6144,512]{2,1,0:T(8,128)(2,1)} %gate_ref.7, bf16[4,6144,512]{2,1,0:T(8,128)(2,1)} %up_ref.7, bf16[16,2048]{1,0:T(8,128)(2,1)S(1)} %stack.3.after_ref.refs_2_), custom_call_target="tpu_custom_call" | custom-call | bytes 12582912 | tf_op jit(solution)/shard_map/load/pallas_call | solution.py:94
  18.8 3.7 %collective-permute-start.7 = (bf16[16,2048]{1,0:T(8,128)(2,1)S(1)}, bf16[16,2048]{1,0:T(8,128)(2,1)S(1)}, u32[]{:S(2)}, u32[]{:S(2)}) collective-permute-start(bf16[16,2048]{1,0:T(8,128)(2,1)S(1)} %stack.3.after_ref.refs_2_), channel_id=1, source_target_pairs={{0,12},{1,13},{2,14},{3,15},{4,8},{5,9},{6,10},{7,11},{8,4},{9,5},... | collective-permute-start | bytes 196616 | tf_op jit(solution)/shard_map/ppermute | solution.py:32
  22.5 0.6 collective-permute-start.5
  23.2 4.7 %load.5 = (bf16[12288,512]{1,0:T(8,128)(2,1)S(1)}, f32[8,128]{1,0:T(8,128)S(1)}) custom-call(bf16[4,6144,512]{2,1,0:T(8,128)(2,1)} %gate_ref.7, bf16[4,6144,512]{2,1,0:T(8,128)(2,1)} %up_ref.7, bf16[32,4096]{1,0:T(8,128)(2,1)S(1)} %stack.4.after_ref.refs_0_), custom_call_target="tpu_custom_call" | custom-call | bytes 12582912 | tf_op jit(solution)/shard_map/load/pallas_call | solution.py:94
  28.0 2.3 %collective-permute-done.8.other_ref = bf16[64,6144]{1,0:T(8,128)(2,1)S(1)} collective-permute-done((bf16[64,6144]{1,0:T(8,128)(2,1)S(1)}, bf16[64,6144]{1,0:T(8,128)(2,1)S(1)}, u32[]{:S(2)}, u32[]{:S(2)}) %collective-permute-start.8) | collective-permute-done | bytes 786464 | tf_op jit(solution)/shard_map/ppermute | solution.py:32
  30.3 15.1 %experts.1 = (bf16[128,2048]{1,0:T(8,128)(2,1)S(1)}, f32[64,4096]{1,0:T(8,128)S(1)}, bf16[64,4096]{1,0:T(8,128)(2,1)S(1)}, bf16[6144,512]{1,0:T(8,128)(2,1)S(1)}...) custom-call(bf16[64,6144]{1,0:T(8,128)(2,1)S(1)} %stack.5.half_ref, ...), custom_call_target="tpu_custom_call", output_to_operand_aliasing={{3}: (6, {}), {4}: (7, {}), {5}: (8, {})} | custom-call | flops 9663676416 | bytes 25165824 | tf_op jit(solution)/shard_map/experts/pallas_call | solution.py:204
  45.6 4.0 %down.1 = (f32[64,2048]{1,0:T(8,128)S(1)}, bf16[64,2048]{1,0:T(8,128)(2,1)S(1)}) custom-call(bf16[128,2048]{1,0:T(8,128)(2,1)S(1)} %get-tuple-element.44.h_ref, bf16[4,512,6144]{2,1,0:T(8,128)(2,1)} %down_ref.3), custom_call_target="tpu_custom_call" | custom-call | flops 1073741824 | bytes 8388608 | tf_op jit(solution)/shard_map/down/pallas_call | solution.py:261
  50.2 1.7 %collective-permute-start.10 = (bf16[32,4096]{1,0:T(8,128)(2,1)S(1)}, bf16[32,4096]{1,0:T(8,128)(2,1)S(1)}, u32[]{:S(2)}, u32[]{:S(2)}) collective-permute-start(bf16[32,4096]{1,0:T(8,128)(2,1)S(1)} %get-tuple-element.39), channel_id=1, source_target_pairs={{0,2},{1,3},{2,0},{3,1},{4,6},{5,7},{6,4},{7,5},{8,10},{9,11},{10,... | collective-permute-start | bytes 786440 | tf_op jit(solution)/shard_map/ppermute | solution.py:32
  52.0 1.3 %collective-permute-start.15 = (bf16[16,2048]{1,0:T(8,128)(2,1)S(1)}, bf16[16,2048]{1,0:T(8,128)(2,1)S(1)}, u32[]{:S(2)}, u32[]{:S(2)}) collective-permute-start(bf16[16,2048]{1,0:T(8,128)(2,1)S(1)} %get-tuple-element.48), channel_id=1, source_target_pairs={{0,4},{1,5},{2,6},{3,7},{4,0},{5,1},{6,2},{7,3},{8,12},{9,13},{10,... | collective-permute-start | bytes 196616 | tf_op jit(solution)/shard_map/ppermute | solution.py:32
  53.3 2.9 %collective-permute-start.16 = (bf16[16,2048]{1,0:T(8,128)(2,1)S(1)}, bf16[16,2048]{1,0:T(8,128)(2,1)S(1)}, u32[]{:S(2)}, u32[]{:S(2)}) collective-permute-start(bf16[16,2048]{1,0:T(8,128)(2,1)S(1)} %get-tuple-element.49), channel_id=1, source_target_pairs={{0,8},{1,9},{2,10},{3,11},{4,12},{5,13},{6,14},{7,15},{8,0},{9,1},... | collective-permute-start | bytes 196616 | tf_op jit(solution)/shard_map/ppermute | solution.py:32
  56.5 2.2 %collective-permute-done.10.got_ref = bf16[32,4096]{1,0:T(8,128)(2,1)S(1)} collective-permute-done((bf16[32,4096]{1,0:T(8,128)(2,1)S(1)}, bf16[32,4096]{1,0:T(8,128)(2,1)S(1)}, u32[]{:S(2)}, u32[]{:S(2)}) %collective-permute-start.10) | collective-permute-done | bytes 262176 | tf_op jit(solution)/shard_map/ppermute | solution.py:32
  58.7 1.5 %collective-permute-start.11 = (bf16[8,4096]{1,0:T(8,128)(2,1)S(1)}, bf16[8,4096]{1,0:T(8,128)(2,1)S(1)}, u32[]{:S(2)}, u32[]{:S(2)}) collective-permute-start(bf16[8,4096]{1,0:T(8,128)(2,1)S(1)} %get-tuple-element.41), channel_id=1, source_target_pairs={{0,4},{1,5},{2,6},{3,7},{4,0},{5,1},{6,2},{7,3},{8,12},{9,13},{10,... | collective-permute-start | bytes 196616 | tf_op jit(solution)/shard_map/ppermute | solution.py:32
  60.1 2.9 %collective-permute-start.12 = (bf16[8,4096]{1,0:T(8,128)(2,1)S(1)}, bf16[8,4096]{1,0:T(8,128)(2,1)S(1)}, u32[]{:S(2)}, u32[]{:S(2)}) collective-permute-start(bf16[8,4096]{1,0:T(8,128)(2,1)S(1)} %get-tuple-element.42), channel_id=1, source_target_pairs={{0,8},{1,9},{2,10},{3,11},{4,12},{5,13},{6,14},{7,15},{8,0},{9,1},... | collective-permute-start | bytes 196616 | tf_op jit(solution)/shard_map/ppermute | solution.py:32
  63.2 1.7 %collective-permute-start.18 = (bf16[8,2048]{1,0:T(8,128)(2,1)S(1)}, bf16[8,2048]{1,0:T(8,128)(2,1)S(1)}, u32[]{:S(2)}, u32[]{:S(2)}) collective-permute-start(bf16[8,2048]{1,0:T(8,128)(2,1)S(1)} %slice.12), channel_id=1, source_target_pairs={{0,2},{1,3},{2,0},{3,1},{4,6},{5,7},{6,4},{7,5},{8,10},{9,11},{10,... | collective-permute-start | bytes 98312 | tf_op jit(solution)/shard_map/ppermute | solution.py:32
  64.9 2.2 %collective-permute-done.18.refs_5_ = bf16[8,2048]{1,0:T(8,128)(2,1)S(1)} collective-permute-done((bf16[8,2048]{1,0:T(8,128)(2,1)S(1)}, bf16[8,2048]{1,0:T(8,128)(2,1)S(1)}, u32[]{:S(2)}, u32[]{:S(2)}) %collective-permute-start.18) | collective-permute-done | bytes 32800 | tf_op jit(solution)/shard_map/ppermute | solution.py:32
  67.2 2.0 %collective-permute-done.13.refs_3_ = bf16[8,4096]{1,0:T(8,128)(2,1)S(1)} collective-permute-done((bf16[8,4096]{1,0:T(8,128)(2,1)S(1)}, bf16[8,4096]{1,0:T(8,128)(2,1)S(1)}, u32[]{:S(2)}, u32[]{:S(2)}) %collective-permute-start.13) | collective-permute-done | bytes 65568 | tf_op jit(solution)/shard_map/ppermute | solution.py:32
  69.1 0.7 sum.1
  (41 shorter events, 2.9 us)
Async XLA Ops:
  0.0 0.9 %copy-start = (bf16[4,2,6144]{2,1,0:T(2,128)(2,1)S(1)}, bf16[4,2,6144]{2,1,0:T(2,128)(2,1)}, u32[]{:S(2)}) copy-start(bf16[4,2,6144]{2,1,0:T(2,128)(2,1)} %tokens_ref.1) | copy-start | bytes 294916
  1.0 17.3 %collective-permute-start.2 = (bf16[8,4096]{1,0:T(8,128)(2,1)S(1)}, bf16[8,4096]{1,0:T(8,128)(2,1)S(1)}, u32[]{:S(2)}, u32[]{:S(2)}) collective-permute-start(bf16[8,4096]{1,0:T(8,128)(2,1)S(1)} %get-tuple-element.28.refs_0_), channel_id=1, source_target_pairs={{0,12},{1,13},{2,14},{3,15},{4,8},{5,9},{6,10},{7,11},{8,4},{9,5},... | collective-permute-start | bytes 196616 | tf_op jit(solution)/shard_map/ppermute | solution.py:32
  6.1 12.2 %collective-permute-start.1 = (bf16[8,4096]{1,0:T(8,128)(2,1)S(1)}, bf16[8,4096]{1,0:T(8,128)(2,1)S(1)}, u32[]{:S(2)}, u32[]{:S(2)}) collective-permute-start(bf16[8,4096]{1,0:T(8,128)(2,1)S(1)} %get-tuple-element.28.refs_0_), channel_id=1, source_target_pairs={{0,8},{1,9},{2,10},{3,11},{4,12},{5,13},{6,14},{7,15},{8,0},{9,1},... | collective-permute-start | bytes 196616 | tf_op jit(solution)/shard_map/ppermute | solution.py:32
  6.1 12.2 %collective-permute-start = (bf16[8,4096]{1,0:T(8,128)(2,1)S(1)}, bf16[8,4096]{1,0:T(8,128)(2,1)S(1)}, u32[]{:S(2)}, u32[]{:S(2)}) collective-permute-start(bf16[8,4096]{1,0:T(8,128)(2,1)S(1)} %get-tuple-element.28.refs_0_), channel_id=1, source_target_pairs={{0,4},{1,5},{2,6},{3,7},{4,0},{5,1},{6,2},{7,3},{8,12},{9,13},{10,... | collective-permute-start | bytes 196616 | tf_op jit(solution)/shard_map/ppermute | solution.py:32
  6.7 6.9 %collective-permute-start.3 = (bf16[8,2048]{1,0:T(8,128)(2,1)S(1)}, bf16[8,2048]{1,0:T(8,128)(2,1)S(1)}, u32[]{:S(2)}, u32[]{:S(2)}) collective-permute-start(bf16[8,2048]{1,0:T(8,128)(2,1)S(1)} %get-tuple-element.29.refs_0_), channel_id=1, source_target_pairs={{0,2},{1,3},{2,0},{3,1},{4,6},{5,7},{6,4},{7,5},{8,10},{9,11},{10,... | collective-permute-start | bytes 98312 | tf_op jit(solution)/shard_map/ppermute | solution.py:32
  18.3 9.5 %collective-permute-start.4 = (bf16[32,4096]{1,0:T(8,128)(2,1)S(1)}, bf16[32,4096]{1,0:T(8,128)(2,1)S(1)}, u32[]{:S(2)}, u32[]{:S(2)}) collective-permute-start(bf16[32,4096]{1,0:T(8,128)(2,1)S(1)} %stack.4.after_ref.refs_0_), channel_id=1, source_target_pairs={{0,2},{1,3},{2,0},{3,1},{4,6},{5,7},{6,4},{7,5},{8,10},{9,11},{10,... | collective-permute-start | bytes 786440 | tf_op jit(solution)/shard_map/ppermute | solution.py:32
  18.8 9.1 %collective-permute-start.7 = (bf16[16,2048]{1,0:T(8,128)(2,1)S(1)}, bf16[16,2048]{1,0:T(8,128)(2,1)S(1)}, u32[]{:S(2)}, u32[]{:S(2)}) collective-permute-start(bf16[16,2048]{1,0:T(8,128)(2,1)S(1)} %stack.3.after_ref.refs_2_), channel_id=1, source_target_pairs={{0,12},{1,13},{2,14},{3,15},{4,8},{5,9},{6,10},{7,11},{8,4},{9,5},... | collective-permute-start | bytes 196616 | tf_op jit(solution)/shard_map/ppermute | solution.py:32
  22.5 5.4 %collective-permute-start.6 = (bf16[16,2048]{1,0:T(8,128)(2,1)S(1)}, bf16[16,2048]{1,0:T(8,128)(2,1)S(1)}, u32[]{:S(2)}, u32[]{:S(2)}) collective-permute-start(bf16[16,2048]{1,0:T(8,128)(2,1)S(1)} %stack.3.after_ref.refs_2_), channel_id=1, source_target_pairs={{0,8},{1,9},{2,10},{3,11},{4,12},{5,13},{6,14},{7,15},{8,0},{9,1},... | collective-permute-start | bytes 196616 | tf_op jit(solution)/shard_map/ppermute | solution.py:32
  22.5 5.4 %collective-permute-start.5 = (bf16[16,2048]{1,0:T(8,128)(2,1)S(1)}, bf16[16,2048]{1,0:T(8,128)(2,1)S(1)}, u32[]{:S(2)}, u32[]{:S(2)}) collective-permute-start(bf16[16,2048]{1,0:T(8,128)(2,1)S(1)} %stack.3.after_ref.refs_2_), channel_id=1, source_target_pairs={{0,4},{1,5},{2,6},{3,7},{4,0},{5,1},{6,2},{7,3},{8,12},{9,13},{10,... | collective-permute-start | bytes 196616 | tf_op jit(solution)/shard_map/ppermute | solution.py:32
  28.0 2.4 %collective-permute-start.8 = (bf16[64,6144]{1,0:T(8,128)(2,1)S(1)}, bf16[64,6144]{1,0:T(8,128)(2,1)S(1)}, u32[]{:S(2)}, u32[]{:S(2)}) collective-permute-start(bf16[64,6144]{1,0:T(8,128)(2,1)S(1)} %stack.5.half_ref), channel_id=1, source_target_pairs={{0,1},{1,0},{2,3},{3,2},{4,5},{5,4},{6,7},{7,6},{8,9},{9,8},{10,11... | collective-permute-start | bytes 2359304 | tf_op jit(solution)/shard_map/ppermute | solution.py:32
  45.4 4.7 %collective-permute-start.9 = (bf16[64,4096]{1,0:T(8,128)(2,1)S(1)}, bf16[64,4096]{1,0:T(8,128)(2,1)S(1)}, u32[]{:S(2)}, u32[]{:S(2)}) collective-permute-start(bf16[64,4096]{1,0:T(8,128)(2,1)S(1)} %get-tuple-element.37), channel_id=1, source_target_pairs={{0,1},{1,0},{2,3},{3,2},{4,5},{5,4},{6,7},{7,6},{8,9},{9,8},{10,11... | collective-permute-start | bytes 1572872 | tf_op jit(solution)/shard_map/ppermute | solution.py:32
  49.7 2.3 %collective-permute-start.14 = (bf16[64,2048]{1,0:T(8,128)(2,1)S(1)}, bf16[64,2048]{1,0:T(8,128)(2,1)S(1)}, u32[]{:S(2)}, u32[]{:S(2)}) collective-permute-start(bf16[64,2048]{1,0:T(8,128)(2,1)S(1)} %get-tuple-element.46), channel_id=1, source_target_pairs={{0,1},{1,0},{2,3},{3,2},{4,5},{5,4},{6,7},{7,6},{8,9},{9,8},{10,11... | collective-permute-start | bytes 786440 | tf_op jit(solution)/shard_map/ppermute | solution.py:32
  50.2 8.4 %collective-permute-start.10 = (bf16[32,4096]{1,0:T(8,128)(2,1)S(1)}, bf16[32,4096]{1,0:T(8,128)(2,1)S(1)}, u32[]{:S(2)}, u32[]{:S(2)}) collective-permute-start(bf16[32,4096]{1,0:T(8,128)(2,1)S(1)} %get-tuple-element.39), channel_id=1, source_target_pairs={{0,2},{1,3},{2,0},{3,1},{4,6},{5,7},{6,4},{7,5},{8,10},{9,11},{10,... | collective-permute-start | bytes 786440 | tf_op jit(solution)/shard_map/ppermute | solution.py:32
  52.0 11.1 %collective-permute-start.15 = (bf16[16,2048]{1,0:T(8,128)(2,1)S(1)}, bf16[16,2048]{1,0:T(8,128)(2,1)S(1)}, u32[]{:S(2)}, u32[]{:S(2)}) collective-permute-start(bf16[16,2048]{1,0:T(8,128)(2,1)S(1)} %get-tuple-element.48), channel_id=1, source_target_pairs={{0,4},{1,5},{2,6},{3,7},{4,0},{5,1},{6,2},{7,3},{8,12},{9,13},{10,... | collective-permute-start | bytes 196616 | tf_op jit(solution)/shard_map/ppermute | solution.py:32
  53.3 9.8 %collective-permute-start.16 = (bf16[16,2048]{1,0:T(8,128)(2,1)S(1)}, bf16[16,2048]{1,0:T(8,128)(2,1)S(1)}, u32[]{:S(2)}, u32[]{:S(2)}) collective-permute-start(bf16[16,2048]{1,0:T(8,128)(2,1)S(1)} %get-tuple-element.49), channel_id=1, source_target_pairs={{0,8},{1,9},{2,10},{3,11},{4,12},{5,13},{6,14},{7,15},{8,0},{9,1},... | collective-permute-start | bytes 196616 | tf_op jit(solution)/shard_map/ppermute | solution.py:32
  56.2 6.9 %collective-permute-start.17 = (bf16[16,2048]{1,0:T(8,128)(2,1)S(1)}, bf16[16,2048]{1,0:T(8,128)(2,1)S(1)}, u32[]{:S(2)}, u32[]{:S(2)}) collective-permute-start(bf16[16,2048]{1,0:T(8,128)(2,1)S(1)} %get-tuple-element.50), channel_id=1, source_target_pairs={{0,12},{1,13},{2,14},{3,15},{4,8},{5,9},{6,10},{7,11},{8,4},{9,5},... | collective-permute-start | bytes 196616 | tf_op jit(solution)/shard_map/ppermute | solution.py:32
  58.7 8.5 %collective-permute-start.11 = (bf16[8,4096]{1,0:T(8,128)(2,1)S(1)}, bf16[8,4096]{1,0:T(8,128)(2,1)S(1)}, u32[]{:S(2)}, u32[]{:S(2)}) collective-permute-start(bf16[8,4096]{1,0:T(8,128)(2,1)S(1)} %get-tuple-element.41), channel_id=1, source_target_pairs={{0,4},{1,5},{2,6},{3,7},{4,0},{5,1},{6,2},{7,3},{8,12},{9,13},{10,... | collective-permute-start | bytes 196616 | tf_op jit(solution)/shard_map/ppermute | solution.py:32
  60.1 7.0 %collective-permute-start.12 = (bf16[8,4096]{1,0:T(8,128)(2,1)S(1)}, bf16[8,4096]{1,0:T(8,128)(2,1)S(1)}, u32[]{:S(2)}, u32[]{:S(2)}) collective-permute-start(bf16[8,4096]{1,0:T(8,128)(2,1)S(1)} %get-tuple-element.42), channel_id=1, source_target_pairs={{0,8},{1,9},{2,10},{3,11},{4,12},{5,13},{6,14},{7,15},{8,0},{9,1},... | collective-permute-start | bytes 196616 | tf_op jit(solution)/shard_map/ppermute | solution.py:32
  63.1 6.1 %collective-permute-start.13 = (bf16[8,4096]{1,0:T(8,128)(2,1)S(1)}, bf16[8,4096]{1,0:T(8,128)(2,1)S(1)}, u32[]{:S(2)}, u32[]{:S(2)}) collective-permute-start(bf16[8,4096]{1,0:T(8,128)(2,1)S(1)} %get-tuple-element.43), channel_id=1, source_target_pairs={{0,12},{1,13},{2,14},{3,15},{4,8},{5,9},{6,10},{7,11},{8,4},{9,5},... | collective-permute-start | bytes 196616 | tf_op jit(solution)/shard_map/ppermute | solution.py:32
  63.2 4.0 %collective-permute-start.18 = (bf16[8,2048]{1,0:T(8,128)(2,1)S(1)}, bf16[8,2048]{1,0:T(8,128)(2,1)S(1)}, u32[]{:S(2)}, u32[]{:S(2)}) collective-permute-start(bf16[8,2048]{1,0:T(8,128)(2,1)S(1)} %slice.12), channel_id=1, source_target_pairs={{0,2},{1,3},{2,0},{3,1},{4,6},{5,7},{6,4},{7,5},{8,10},{9,11},{10,... | collective-permute-start | bytes 98312 | tf_op jit(solution)/shard_map/ppermute | solution.py:32

commit v2 on v1

--- a/solution.py
+++ b/solution.py
@@ -8,8 +8,7 @@
 from jax.sharding import PartitionSpec as P
 
 MIB = 1 << 20
-ARENA = 30 * MIB
-SCOPED = 24
+SCOPED = 18
 VMEM = pl.BlockSpec(memory_space=pltpu.VMEM)
 ANY = pl.BlockSpec(memory_space=pl.ANY)
 BF16, F32 = jnp.bfloat16, jnp.float32
@@ -76,31 +75,24 @@
     )(*[in_vmem(part) for part in parts], after)
 
 
-def load_kernel(pieces, gate_ref, up_ref, after_ref, out_ref, token_ref, sem):
-    width = gate_ref.shape[1]
-    copies = []
-    for i, piece in enumerate(pieces):
-        source = up_ref if piece % 2 else gate_ref
-        copies.append(pltpu.make_async_copy(source.at[piece // 2], out_ref.at[pl.ds(i * width, width)], sem.at[i]))
-    for copy in copies:
-        copy.start()
+def load_kernel(w_ref, after_ref, out_ref, token_ref, sem):
+    copy = pltpu.make_async_copy(w_ref.at[0], out_ref, sem)
+    copy.start()
     token_ref[...] = jnp.zeros_like(token_ref)
-    for copy in copies:
-        copy.wait()
-
-
-def load(w_gate, w_up, after, pieces):
-    _, width, units = w_gate.shape
-    return pl.pallas_call(
-        functools.partial(load_kernel, pieces),
-        in_specs=[ANY, ANY, ANY],
+    copy.wait()
+
+
+def load(w, after):
+    return pl.pallas_call(
+        load_kernel,
+        in_specs=[ANY, ANY],
         out_specs=[VMEM, VMEM],
-        out_shape=[pltpu.VMEM((len(pieces) * width, units), w_gate.dtype), pltpu.VMEM((8, 128), F32)],
-        scratch_shapes=[pltpu.SemaphoreType.DMA((len(pieces),))],
+        out_shape=[pltpu.VMEM(w.shape[1:], w.dtype), pltpu.VMEM((8, 128), F32)],
+        scratch_shapes=[pltpu.SemaphoreType.DMA],
         compiler_params=pltpu.CompilerParams(vmem_limit_bytes=2 * MIB),
-        cost_estimate=cost(0, 2 * len(pieces) * width * units),
+        cost_estimate=cost(0, 2 * w.size // w.shape[0]),
         name="load",
-    )(in_hbm(w_gate), in_hbm(w_up), after)
+    )(in_hbm(w), after)
 
 
 def place_of(row, n, steps, own, me):
@@ -111,121 +103,116 @@
     return (rest // own) * (n * own) + (me ^ mask) * own + rest % own
 
 
+def plan_kernel(n, own, ids_ref, weights_ref, return_ref, after_ref, route_ref, order_ref):
+    steps, total = return_ref.shape
+    rows = steps * total
+    me = lax.axis_index("hid")
+    down = lax.broadcasted_iota(jnp.int32, (rows, total), 0)
+    place = place_of(down, n, steps, own, me)
+    across = lax.broadcasted_iota(jnp.int32, (rows, total), 1)
+    picked = [jnp.zeros((rows, total), F32)] * 5
+    for s in range(steps):
+        here = place == across + s * total
+        values = [ids_ref[s, 0:1], ids_ref[s, 1:2], weights_ref[s, 0:1], weights_ref[s, 1:2], return_ref[s : s + 1]]
+        picked = [jnp.where(here, value.astype(F32), old) for value, old in zip(values, picked)]
+    first, second, first_weight, second_weight, source = [jnp.sum(p, axis=1, keepdims=True) for p in picked]
+    for e in range(route_ref.shape[0]):
+        route_ref[e] = jnp.where(first == e, first_weight, 0.0) + jnp.where(second == e, second_weight, 0.0)
+    shape = (rows, rows)
+    step = (lax.broadcasted_iota(jnp.int32, (rows, 1), 0) % (steps * own)) // own
+    across = lax.broadcasted_iota(jnp.int32, shape, 1)
+    order_ref[...] = (place_of(across, n, steps, own, me) == source.astype(jnp.int32) + step * total).astype(BF16)
+
+
+def plan(expert_ids, gate_weights, return_order, experts, n, own, after):
+    steps, total = return_order.shape
+    rows = steps * total
+    return pl.pallas_call(
+        functools.partial(plan_kernel, n, own),
+        in_specs=[VMEM] * 3 + [ANY],
+        out_specs=[VMEM, VMEM],
+        out_shape=[pltpu.VMEM((experts, rows, 1), F32), pltpu.VMEM((rows, rows), BF16)],
+        compiler_params=pltpu.CompilerParams(vmem_limit_bytes=8 * MIB),
+        cost_estimate=cost(0, 4 * rows * rows),
+        name="plan",
+    )(jnp.swapaxes(expert_ids, 1, 2), jnp.swapaxes(gate_weights, 1, 2), return_order, after)
+
+
 def experts_kernel(
-    n, steps, own, loads, blocks, half_ref, other_ref, table_ref, gate_ref, up_ref, down_ref, *refs
+    blocks, half_ref, other_ref, route_ref, order_ref, gate_ref, up_ref, down_ref, old_ref,
+    h_ref, keep_ref, send_ref, first_ref, x_ref, up_buf, up_sem, down_sem,
 ):
-    refs = refs[loads:]
-    (h_ref, keep_ref, send_ref), arena_refs = refs[:3], refs[3 : 3 + loads]
-    x_ref, rest_ref, route, order, rest_sem, down_sem = refs[3 + loads :]
     half, width = half_ref.shape
-    rows = 2 * half
     experts, units, _ = down_ref.shape
     depth = experts * units
-    homes = [ref.at[pl.ds(i, width)] for ref in arena_refs for i in range(0, ref.shape[0], width)]
-    count = len(homes)
-    spares = [rest_ref.at[pl.ds(i, width)] for i in range(0, rest_ref.shape[0], width)]
-    late = []
-    for p in range(count, 2 * experts):
-        at = p - count
-        home = spares[at] if at < len(spares) else homes[at - len(spares)]
-        source = (up_ref if p % 2 else gate_ref).at[p // 2]
-        late.append((home, pltpu.make_async_copy(source, home, rest_sem.at[at])))
-    taken = max(len(late) - len(spares), 0)
-    for _, copy in late[:2]:
+    up_homes = [first_ref] + [up_buf.at[e % 2] for e in range(1, experts - 1)] + [first_ref]
+    up_copies = [None] + [pltpu.make_async_copy(up_ref.at[e], up_homes[e], up_sem.at[e]) for e in range(1, experts)]
+    fit = width // depth
+    homes = [ref.at[pl.ds(at * experts, experts)] for ref in (up_buf.at[1], up_buf.at[0], first_ref) for at in range(fit)]
+
+    def block_copy(b):
+        return pltpu.make_async_copy(down_ref.at[:, :, pl.ds(b * units, units)], homes[b], down_sem.at[b])
+
+    def start_blocks(first, last):
+        for b in range(first, min(last, blocks)):
+            block_copy(b).start()
+
+    for copy in up_copies[1:3]:
         copy.start()
     x_ref[:half] = half_ref[...]
     x_ref[half:] = other_ref[...]
-
-    me = lax.axis_index("hid")
-    shape = (rows, rows)
-    down = lax.broadcasted_iota(jnp.int32, shape, 0)
-    across = lax.broadcasted_iota(jnp.int32, shape, 1)
-    pick = (place_of(down, n, steps, own, me) == across).astype(BF16)
-    mine = jnp.dot(pick, table_ref[...].astype(BF16), preferred_element_type=F32)
-    step = (lax.broadcasted_iota(jnp.int32, (rows, 1), 0) % (steps * own)) // own
-    source = mine[:, 4:5].astype(jnp.int32) + step * (n * own)
-    order[...] = (place_of(across, n, steps, own, me) == source).astype(BF16)
     for e in range(experts):
-        route[e] = jnp.where(mine[:, 0:1] == e, mine[:, 2:3], 0.0) + jnp.where(
-            mine[:, 1:2] == e, mine[:, 3:4], 0.0
-        )
-
-    fit = width // depth
-
-    def block_home(b):
-        return homes[taken + b // fit].at[pl.ds(b % fit * depth, depth)]
-
-    def block_copies(b):
-        return [
-            pltpu.make_async_copy(
-                down_ref.at[e, :, pl.ds(b * units, units)],
-                block_home(b).at[pl.ds(e * units, units)],
-                down_sem.at[b, e],
-            )
-            for e in range(experts)
-        ]
-
-    def piece(p):
-        if p < count:
-            return homes[p][...]
-        home, copy = late[p - count]
-        copy.wait()
-        return home[...]
-
-    begun = 0
-    for e in range(experts):
-        gate = jnp.dot(x_ref[...], piece(2 * e), preferred_element_type=F32)
-        up = jnp.dot(x_ref[...], piece(2 * e + 1), preferred_element_type=F32)
+        gate = jnp.dot(x_ref[...], gate_ref[e], preferred_element_type=F32)
+        if e:
+            up_copies[e].wait()
+        up = jnp.dot(x_ref[...], up_homes[e].reshape(width, units)[...], preferred_element_type=F32)
         if e == 0:
-            for _, copy in late[2:]:
+            for copy in up_copies[3:]:
                 copy.start()
-        free = (min(2 * (e + 1), count) - taken) * fit
-        until = blocks if e == experts - 1 else min(-(-blocks * e // experts), free)
-        for b in range(begun, until):
-            for copy in block_copies(b):
-                copy.start()
-        begun = until
-        hidden = gate / (1.0 + jnp.exp(-gate)) * up * route[e]
-        hidden = jnp.dot(order[...], hidden.astype(BF16), preferred_element_type=F32)
+        elif e == 1:
+            start_blocks(0, fit)
+        elif e == 2:
+            start_blocks(fit, 2 * fit)
+        else:
+            start_blocks(2 * fit, blocks)
+        hidden = gate / (1.0 + jnp.exp(-gate)) * up * route_ref[e]
+        hidden = jnp.dot(order_ref[...], hidden.astype(BF16), preferred_element_type=F32)
         h_ref[:, e * units : (e + 1) * units] = hidden.astype(BF16)
     for b in range(blocks):
-        for copy in block_copies(b):
-            copy.wait()
-        total = jnp.dot(h_ref[...], block_home(b)[...], preferred_element_type=F32)
+        block_copy(b).wait()
+        total = jnp.dot(h_ref[...], homes[b].reshape(depth, units)[...], preferred_element_type=F32)
         keep_ref[:, b * units : (b + 1) * units] = total[:half]
         send_ref[:, b * units : (b + 1) * units] = total[half:].astype(BF16)
 
 
-def experts_of(half, other, table, w_gate, w_up, w_down, arena, blocks, n, steps, own):
+def experts_of(half, other, route, order, w_gate, w_up, w_down, first_up, blocks):
     experts, units, width = w_down.shape
     rows = 2 * half.shape[0]
     columns = blocks * units
-    rest = max(2 * experts - sum(buffer.shape[0] for buffer in arena) // width, 1)
-    h, keep, send, *_ = pl.pallas_call(
-        functools.partial(experts_kernel, n, steps, own, len(arena), blocks),
-        in_specs=[VMEM] * 3 + [ANY] * 3 + [VMEM] * len(arena),
-        out_specs=[VMEM] * (3 + len(arena)),
+    depth = experts * units
+    h, keep, send, _ = pl.pallas_call(
+        functools.partial(experts_kernel, blocks),
+        in_specs=[VMEM] * 5 + [ANY] * 2 + [VMEM],
+        out_specs=[VMEM] * 4,
         out_shape=[
-            pltpu.VMEM((rows, experts * units), BF16),
+            pltpu.VMEM((rows, depth), BF16),
             pltpu.VMEM((rows // 2, columns), F32),
             pltpu.VMEM((rows // 2, columns), BF16),
-        ]
-        + [pltpu.VMEM(buffer.shape, buffer.dtype) for buffer in arena],
+            pltpu.VMEM(first_up.shape, first_up.dtype),
+        ],
         scratch_shapes=[
             pltpu.VMEM((rows, width), BF16),
-            pltpu.VMEM((max(rest - 1, 1) * width, units), BF16),
-            pltpu.VMEM((experts, rows, 1), F32),
-            pltpu.VMEM((rows, rows), BF16),
-            pltpu.SemaphoreType.DMA((rest,)),
-            pltpu.SemaphoreType.DMA((blocks, experts)),
+            pltpu.VMEM((2, width // units, units, units), BF16),
+            pltpu.SemaphoreType.DMA((experts,)),
+            pltpu.SemaphoreType.DMA((blocks,)),
         ],
-        input_output_aliases={6 + i: 3 + i for i in range(len(arena))},
+        input_output_aliases={7: 3},
         compiler_params=pltpu.CompilerParams(vmem_limit_bytes=SCOPED * MIB),
-        cost_estimate=cost(6 * rows * w_down.size, 2 * w_down.size),
+        cost_estimate=cost(0, 8 * w_down.size),
         name="experts",
     )(
-        in_vmem(half), in_vmem(other), in_vmem(table), in_hbm(w_gate), in_hbm(w_up), in_hbm(w_down),
-        *[in_vmem(buffer) for buffer in arena],
+        in_vmem(half), in_vmem(other), in_vmem(route), in_vmem(order),
+        in_vmem(w_gate), in_hbm(w_up), in_hbm(w_down), in_vmem(first_up),
     )
     return h, keep, send
 
@@ -316,35 +303,28 @@
     far = n // 4
     per = steps * own
     rows = per * n
-    table = jnp.concatenate(
-        [expert_ids.astype(F32), gate_weights.astype(F32), return_order[..., None].astype(F32)], axis=-1
-    ).reshape(rows, 5)
-
     blocks = width // units
     lead = (2 * blocks + 2) // 3
     a = lead * units
     b = width - a
-    count = min(2 * experts, ARENA // (2 * width * units))
-    cuts = [count // 4, 3 * count // 4, count]
-    pieces = [range(0, cuts[0]), range(cuts[0], cuts[1]), range(cuts[1], cuts[2])]
     xa, xb = split(tokens, [a, b])
     za = [swap(xa, 4 * z) for z in range(1, far)]
     yb = swap(xb, 2)
-    arena0, ready = load(w_gate, w_up, table, pieces[0])
+    w_up = w_up.reshape(experts, blocks, units, units)
+    first_up, ready = load(w_up, xa)
     xb = stack([xb, yb], [(0, [0]), (0, [1])], (2 * per, b), ready)
     zb = [swap(xb, 4 * z) for z in range(1, far)]
-    arena1, ready = load(w_gate, w_up, xb, pieces[1])
-    xa = stack([xa] + za, [(0, [z]) for z in range(far)], (far * per, a), ready)
+    xa = stack([xa] + za, [(0, [z]) for z in range(far)], (far * per, a), xb)
     ya = swap(xa, 2)
-    arena2, ready = load(w_gate, w_up, xa, pieces[2])
+    route, order = plan(expert_ids, gate_weights, return_order, experts, n, own, xa)
     half = stack(
         [xa, ya, xb] + zb,
         [(0, [0]), (0, [1])] + [(a, [z, far + z]) for z in range(far)],
         (2 * far * per, width),
-        ready,
+        order,
     )
     other = swap(half, 1)
-    h, keep_a, send_a = experts_of(half, other, table, w_gate, w_up, w_down, [arena0, arena1, arena2], lead, n, steps, own)
+    h, keep_a, send_a = experts_of(half, other, route, order, w_gate, w_up, w_down, first_up, lead)
     got_a = swap(send_a, 1)
     keep_b, send_b = down(h, w_down, lead, blocks - lead)
     got_b = swap(send_b, 1)

time: 70.1 us -> 59.3 us (0.85)
  Pallas kernels: 32.3 us -> 20.2 us
  waiting for transfers between devices: 8.66 us -> 13.3 us
  other arithmetic: 1.42 us -> 0.03 us
  local copies, waits for them, and re-layouts: 1.96 us -> 0.92 us
    pallas_call x4 -> x3, Pallas kernels: 27.2 us -> 15.2 us  [the longest x1 12.1 us: experts_of(): pl.pallas_call(functools.partial(experts_kernel, blocks), in_specs=[VMEM]...]
    ppermute x19, waiting for transfers between devices: 8.66 us -> 13.3 us  [swap(): return lax.ppermute(x, 'hid', [(i, i ^ mask) for i in range(n)])]
    convert_element_type x2 -> x0, other arithmetic: 1.37 us -> none  [the longest x1 0.69 us: body(): expert_ids.astype(F32)]
    concatenate x5 -> x0, local copies, waits for them, and re-layouts: 1.06 us -> none  [body(): jnp.concatenate([expert_ids.astype(F32), gate_weights.astype(F32), return...]
    ppermute x19, starting transfers between devices: 25.3 us -> 24.6 us  [swap(): return lax.ppermute(x, 'hid', [(i, i ^ mask) for i in range(n)])]
  transfers between devices with their start and end apart: 19 -> 19, of which waited for: 4 -> 8; matrix products, arithmetic and copies ran while one was open for 4% -> 0% of each run, Pallas kernels for 23% -> 12%
where the time goes in v2:
time: 59.3 us; the launch traced here: 59.2 us
  starting transfers between devices  24.6 us (41%)
  Pallas kernels  20.2 us (34%)
  waiting for transfers between devices  13.3 us (22%)
  local copies, waits for them, and re-layouts  0.92 us (2%)
    ppermute x19, starting transfers between devices, swap(): return lax.ppermute(x, 'hid', [(i, i ^ mask) for i in range(n)])  24.6 us
    ppermute x19, waiting for transfers between devices, swap(): return lax.ppermute(x, 'hid', [(i, i ^ mask) for i in range(n)])  13.3 us
    pallas_call x1, Pallas kernels, experts_of(): pl.pallas_call(functools.partial(experts_kernel, blocks), in_specs=[VMEM]...  12.1 us
    pallas_call x1, Pallas kernels, down(): pl.pallas_call(functools.partial(down_kernel, first), in_specs=[VMEM, ANY...  4.02 us
    pallas_call x1, Pallas kernels, load(): pl.pallas_call(load_kernel, in_specs=[ANY, ANY], out_specs=[VMEM, VMEM],...  2.79 us
  transfers between devices with their start and end apart: 19, of which 8 were waited for; matrix products, arithmetic and copies ran while one was open for 0% of the time, Pallas kernels for 12%

profile of v2, /device:TPU:0, one launch (start us, length us, event | category | flops | bytes accessed | tf_op | source)
XLA Modules:
  0.0 59.2 jit_solution(12884676643416970147)
XLA Ops:
  0.0 0.9 %copy-done.1 = bf16[4,2,6144]{2,1,0:T(2,128)(2,1)S(1)} copy-done((bf16[4,2,6144]{2,1,0:T(2,128)(2,1)S(1)}, bf16[4,2,6144]{2,1,0:T(2,128)(2,1)}, u32[]{:S(2)}) %copy-start.1) | copy-done | bytes 98328
  1.0 5.1 %collective-permute-start.2 = (bf16[8,4096]{1,0:T(8,128)(2,1)S(1)}, bf16[8,4096]{1,0:T(8,128)(2,1)S(1)}, u32[]{:S(2)}, u32[]{:S(2)}) collective-permute-start(bf16[8,4096]{1,0:T(8,128)(2,1)S(1)} %get-tuple-element.26.after_ref.refs_0_), channel_id=1, source_target_pairs={{0,12},{1,13},{2,14},{3,15},{4,8},{5,9},{6,10},{7,11},{8,4},{9,5},... | collective-permute-start | bytes 196616 | tf_op jit(solution)/shard_map/ppermute | solution.py:31
  6.1 0.6 %collective-permute-start = (bf16[8,4096]{1,0:T(8,128)(2,1)S(1)}, bf16[8,4096]{1,0:T(8,128)(2,1)S(1)}, u32[]{:S(2)}, u32[]{:S(2)}) collective-permute-start(bf16[8,4096]{1,0:T(8,128)(2,1)S(1)} %get-tuple-element.26.after_ref.refs_0_), channel_id=1, source_target_pairs={{0,4},{1,5},{2,6},{3,7},{4,0},{5,1},{6,2},{7,3},{8,12},{9,13},{10,... | collective-permute-start | bytes 196616 | tf_op jit(solution)/shard_map/ppermute | solution.py:31
  6.7 1.7 %collective-permute-start.3 = (bf16[8,2048]{1,0:T(8,128)(2,1)S(1)}, bf16[8,2048]{1,0:T(8,128)(2,1)S(1)}, u32[]{:S(2)}, u32[]{:S(2)}) collective-permute-start(bf16[8,2048]{1,0:T(8,128)(2,1)S(1)} %get-tuple-element.27.refs_0_), channel_id=1, source_target_pairs={{0,2},{1,3},{2,0},{3,1},{4,6},{5,7},{6,4},{7,5},{8,10},{9,11},{10,... | collective-permute-start | bytes 98312 | tf_op jit(solution)/shard_map/ppermute | solution.py:31
  8.4 2.8 %load.1 = (bf16[12,512,512]{2,1,0:T(8,128)(2,1)S(1)}, f32[8,128]{1,0:T(8,128)S(1)}) custom-call(bf16[4,12,512,512]{3,2,1,0:T(8,128)(2,1)} %bitcast.5, bf16[8,4096]{1,0:T(8,128)(2,1)S(1)} %get-tuple-element.26.after_ref.refs_0_), custom_call_target="tpu_custom_call" | custom-call | bytes 6291456 | tf_op jit(solution)/shard_map/load/pallas_call | solution.py:86
  11.2 0.5 collective-permute-done.1.refs_2_
  11.7 1.6 %collective-permute-start.4 = (bf16[32,4096]{1,0:T(8,128)(2,1)S(1)}, bf16[32,4096]{1,0:T(8,128)(2,1)S(1)}, u32[]{:S(2)}, u32[]{:S(2)}) collective-permute-start(bf16[32,4096]{1,0:T(8,128)(2,1)S(1)} %stack.4.after_ref.refs_0_), channel_id=1, source_target_pairs={{0,2},{1,3},{2,0},{3,1},{4,6},{5,7},{6,4},{7,5},{8,10},{9,11},{10,... | collective-permute-start | bytes 786440 | tf_op jit(solution)/shard_map/ppermute | solution.py:31
  13.3 2.9 %collective-permute-start.7 = (bf16[16,2048]{1,0:T(8,128)(2,1)S(1)}, bf16[16,2048]{1,0:T(8,128)(2,1)S(1)}, u32[]{:S(2)}, u32[]{:S(2)}) collective-permute-start(bf16[16,2048]{1,0:T(8,128)(2,1)S(1)} %stack.3.refs_4_.refs_2_), channel_id=1, source_target_pairs={{0,12},{1,13},{2,14},{3,15},{4,8},{5,9},{6,10},{7,11},{8,4},{9,5},... | collective-permute-start | bytes 196616 | tf_op jit(solution)/shard_map/ppermute | solution.py:31
  16.2 1.5 %collective-permute-start.5 = (bf16[16,2048]{1,0:T(8,128)(2,1)S(1)}, bf16[16,2048]{1,0:T(8,128)(2,1)S(1)}, u32[]{:S(2)}, u32[]{:S(2)}) collective-permute-start(bf16[16,2048]{1,0:T(8,128)(2,1)S(1)} %stack.3.refs_4_.refs_2_), channel_id=1, source_target_pairs={{0,4},{1,5},{2,6},{3,7},{4,0},{5,1},{6,2},{7,3},{8,12},{9,13},{10,... | collective-permute-start | bytes 196616 | tf_op jit(solution)/shard_map/ppermute | solution.py:31
  18.0 1.8 %collective-permute-done.7.refs_5_ = bf16[16,2048]{1,0:T(8,128)(2,1)S(1)} collective-permute-done((bf16[16,2048]{1,0:T(8,128)(2,1)S(1)}, bf16[16,2048]{1,0:T(8,128)(2,1)S(1)}, u32[]{:S(2)}, u32[]{:S(2)}) %collective-permute-start.7) | collective-permute-done | bytes 65568 | tf_op jit(solution)/shard_map/ppermute | solution.py:31
  19.8 2.3 %collective-permute-done.6.refs_4_ = bf16[16,2048]{1,0:T(8,128)(2,1)S(1)} collective-permute-done((bf16[16,2048]{1,0:T(8,128)(2,1)S(1)}, bf16[16,2048]{1,0:T(8,128)(2,1)S(1)}, u32[]{:S(2)}, u32[]{:S(2)}) %collective-permute-start.6) | collective-permute-done | bytes 65568 | tf_op jit(solution)/shard_map/ppermute | solution.py:31
  22.3 2.3 %collective-permute-done.8.other_ref = bf16[64,6144]{1,0:T(8,128)(2,1)S(1)} collective-permute-done((bf16[64,6144]{1,0:T(8,128)(2,1)S(1)}, bf16[64,6144]{1,0:T(8,128)(2,1)S(1)}, u32[]{:S(2)}, u32[]{:S(2)}) %collective-permute-start.8) | collective-permute-done | bytes 786464 | tf_op jit(solution)/shard_map/ppermute | solution.py:31
  24.6 12.1 %experts.1 = (bf16[128,2048]{1,0:T(8,128)(2,1)S(1)}, f32[64,4096]{1,0:T(8,128)S(1)}, bf16[64,4096]{1,0:T(8,128)(2,1)S(1)}, bf16[12,512,512]{2,1,0:T(8,128)(2,1)S(1)}) custom-call(bf16[64,6144]{1,0:T(8,128)(2,1)S(1)} %stack.5.half_ref, bf16[64,6144]{1,0:T(8,128)(2,1)S(1)} %collective-permute-done.8.other_ref, ...), custom_call_target="tpu_custom_call", output_to_operand_aliasing={{3}: (7, {})} | custom-call | bytes 100663296 | tf_op jit(solution)/shard_map/experts/pallas_call | solution.py:193
  36.9 4.0 %down.1 = (f32[64,2048]{1,0:T(8,128)S(1)}, bf16[64,2048]{1,0:T(8,128)(2,1)S(1)}) custom-call(bf16[128,2048]{1,0:T(8,128)(2,1)S(1)} %get-tuple-element.40.h_ref, bf16[4,512,6144]{2,1,0:T(8,128)(2,1)} %down_ref.3), custom_call_target="tpu_custom_call" | custom-call | flops 1073741824 | bytes 8388608 | tf_op jit(solution)/shard_map/down/pallas_call | solution.py:248
  40.9 0.4 collective-permute-start.14
  41.4 0.8 %collective-permute-start.10 = (bf16[32,4096]{1,0:T(8,128)(2,1)S(1)}, bf16[32,4096]{1,0:T(8,128)(2,1)S(1)}, u32[]{:S(2)}, u32[]{:S(2)}) collective-permute-start(bf16[32,4096]{1,0:T(8,128)(2,1)S(1)} %get-tuple-element.35), channel_id=1, source_target_pairs={{0,2},{1,3},{2,0},{3,1},{4,6},{5,7},{6,4},{7,5},{8,10},{9,11},{10,... | collective-permute-start | bytes 786440 | tf_op jit(solution)/shard_map/ppermute | solution.py:31
  42.9 2.3 %collective-permute-start.16 = (bf16[16,2048]{1,0:T(8,128)(2,1)S(1)}, bf16[16,2048]{1,0:T(8,128)(2,1)S(1)}, u32[]{:S(2)}, u32[]{:S(2)}) collective-permute-start(bf16[16,2048]{1,0:T(8,128)(2,1)S(1)} %get-tuple-element.45), channel_id=1, source_target_pairs={{0,8},{1,9},{2,10},{3,11},{4,12},{5,13},{6,14},{7,15},{8,0},{9,1},... | collective-permute-start | bytes 196616 | tf_op jit(solution)/shard_map/ppermute | solution.py:31
  45.2 1.8 %collective-permute-start.17 = (bf16[16,2048]{1,0:T(8,128)(2,1)S(1)}, bf16[16,2048]{1,0:T(8,128)(2,1)S(1)}, u32[]{:S(2)}, u32[]{:S(2)}) collective-permute-start(bf16[16,2048]{1,0:T(8,128)(2,1)S(1)} %get-tuple-element.46), channel_id=1, source_target_pairs={{0,12},{1,13},{2,14},{3,15},{4,8},{5,9},{6,10},{7,11},{8,4},{9,5},... | collective-permute-start | bytes 196616 | tf_op jit(solution)/shard_map/ppermute | solution.py:31
  47.0 2.8 %collective-permute-done.10.got_ref = bf16[32,4096]{1,0:T(8,128)(2,1)S(1)} collective-permute-done((bf16[32,4096]{1,0:T(8,128)(2,1)S(1)}, bf16[32,4096]{1,0:T(8,128)(2,1)S(1)}, u32[]{:S(2)}, u32[]{:S(2)}) %collective-permute-start.10) | collective-permute-done | bytes 262176 | tf_op jit(solution)/shard_map/ppermute | solution.py:31
  50.0 2.3 %collective-permute-start.12 = (bf16[8,4096]{1,0:T(8,128)(2,1)S(1)}, bf16[8,4096]{1,0:T(8,128)(2,1)S(1)}, u32[]{:S(2)}, u32[]{:S(2)}) collective-permute-start(bf16[8,4096]{1,0:T(8,128)(2,1)S(1)} %get-tuple-element.38), channel_id=1, source_target_pairs={{0,8},{1,9},{2,10},{3,11},{4,12},{5,13},{6,14},{7,15},{8,0},{9,1},... | collective-permute-start | bytes 196616 | tf_op jit(solution)/shard_map/ppermute | solution.py:31
  52.3 2.1 %collective-permute-start.13 = (bf16[8,4096]{1,0:T(8,128)(2,1)S(1)}, bf16[8,4096]{1,0:T(8,128)(2,1)S(1)}, u32[]{:S(2)}, u32[]{:S(2)}) collective-permute-start(bf16[8,4096]{1,0:T(8,128)(2,1)S(1)} %get-tuple-element.39), channel_id=1, source_target_pairs={{0,12},{1,13},{2,14},{3,15},{4,8},{5,9},{6,10},{7,11},{8,4},{9,5},... | collective-permute-start | bytes 196616 | tf_op jit(solution)/shard_map/ppermute | solution.py:31
  54.4 0.8 %collective-permute-start.18 = (bf16[8,2048]{1,0:T(8,128)(2,1)S(1)}, bf16[8,2048]{1,0:T(8,128)(2,1)S(1)}, u32[]{:S(2)}, u32[]{:S(2)}) collective-permute-start(bf16[8,2048]{1,0:T(8,128)(2,1)S(1)} %slice.12), channel_id=1, source_target_pairs={{0,2},{1,3},{2,0},{3,1},{4,6},{5,7},{6,4},{7,5},{8,10},{9,11},{10,... | collective-permute-start | bytes 98312 | tf_op jit(solution)/shard_map/ppermute | solution.py:31
  55.2 3.2 %collective-permute-done.18.refs_5_ = bf16[8,2048]{1,0:T(8,128)(2,1)S(1)} collective-permute-done((bf16[8,2048]{1,0:T(8,128)(2,1)S(1)}, bf16[8,2048]{1,0:T(8,128)(2,1)S(1)}, u32[]{:S(2)}, u32[]{:S(2)}) %collective-permute-start.18) | collective-permute-done | bytes 32800 | tf_op jit(solution)/shard_map/ppermute | solution.py:31
  58.5 0.7 %sum.1 = bf16[4,2,6144]{2,1,0:T(2,128)(2,1)} custom-call(f32[8,4096]{1,0:T(8,128)S(1)} %get-tuple-element.36.refs_0_, bf16[8,4096]{1,0:T(8,128)(2,1)S(1)} %collective-permute-done.11.refs_1_, bf16[8,4096]{1,0:T(8,128)(2,1)S(1)} %collective-permute-done.12.refs_2_, bf16[8,4096]{1,0:T(8,128)(2,1)S(1)} %collective-permute-done.13.refs_3_, ...), custom_call_target="tpu_custom_call" | custom-call | bytes 196608 | tf_op jit(solution)/shard_map/sum/pallas_call | solution.py:342
  (39 shorter events, 1.7 us)
Async XLA Ops:
  0.0 0.9 %copy-start.1 = (bf16[4,2,6144]{2,1,0:T(2,128)(2,1)S(1)}, bf16[4,2,6144]{2,1,0:T(2,128)(2,1)}, u32[]{:S(2)}) copy-start(bf16[4,2,6144]{2,1,0:T(2,128)(2,1)} %tokens_ref.1) | copy-start | bytes 294916
  0.9 16.8 %copy-start.2 = (s32[4,32,2]{1,2,0:T(2,128)S(1)}, s32[4,32,2]{1,2,0:T(2,128)}, u32[]{:S(2)}) copy-start(s32[4,32,2]{1,2,0:T(2,128)} %param.11) | copy-start | bytes 3076
  0.9 16.8 %copy-start.3 = (bf16[4,32,2]{1,2,0:T(2,128)(2,1)S(1)}, bf16[4,32,2]{1,2,0:T(2,128)(2,1)}, u32[]{:S(2)}) copy-start(bf16[4,32,2]{1,2,0:T(2,128)(2,1)} %param.12) | copy-start | bytes 1540
  0.9 16.8 %copy-start.4 = (s32[4,32]{1,0:T(4,128)S(1)}, s32[4,32]{1,0:T(4,128)}, u32[]{:S(2)}) copy-start(s32[4,32]{1,0:T(4,128)} %return_ref.1) | copy-start | bytes 1540
  0.9 23.7 %copy-start = (bf16[4,6144,512]{2,1,0:T(8,128)(2,1)S(1)}, bf16[4,6144,512]{2,1,0:T(8,128)(2,1)}, u32[]{:S(2)}) copy-start(bf16[4,6144,512]{2,1,0:T(8,128)(2,1)} %gate_ref.1) | copy-start | bytes 75497472
  1.0 10.3 %collective-permute-start.2 = (bf16[8,4096]{1,0:T(8,128)(2,1)S(1)}, bf16[8,4096]{1,0:T(8,128)(2,1)S(1)}, u32[]{:S(2)}, u32[]{:S(2)}) collective-permute-start(bf16[8,4096]{1,0:T(8,128)(2,1)S(1)} %get-tuple-element.26.after_ref.refs_0_), channel_id=1, source_target_pairs={{0,12},{1,13},{2,14},{3,15},{4,8},{5,9},{6,10},{7,11},{8,4},{9,5},... | collective-permute-start | bytes 196616 | tf_op jit(solution)/shard_map/ppermute | solution.py:31
  6.1 5.6 %collective-permute-start.1 = (bf16[8,4096]{1,0:T(8,128)(2,1)S(1)}, bf16[8,4096]{1,0:T(8,128)(2,1)S(1)}, u32[]{:S(2)}, u32[]{:S(2)}) collective-permute-start(bf16[8,4096]{1,0:T(8,128)(2,1)S(1)} %get-tuple-element.26.after_ref.refs_0_), channel_id=1, source_target_pairs={{0,8},{1,9},{2,10},{3,11},{4,12},{5,13},{6,14},{7,15},{8,0},{9,1},... | collective-permute-start | bytes 196616 | tf_op jit(solution)/shard_map/ppermute | solution.py:31
  6.1 5.6 %collective-permute-start = (bf16[8,4096]{1,0:T(8,128)(2,1)S(1)}, bf16[8,4096]{1,0:T(8,128)(2,1)S(1)}, u32[]{:S(2)}, u32[]{:S(2)}) collective-permute-start(bf16[8,4096]{1,0:T(8,128)(2,1)S(1)} %get-tuple-element.26.after_ref.refs_0_), channel_id=1, source_target_pairs={{0,4},{1,5},{2,6},{3,7},{4,0},{5,1},{6,2},{7,3},{8,12},{9,13},{10,... | collective-permute-start | bytes 196616 | tf_op jit(solution)/shard_map/ppermute | solution.py:31
  6.7 4.5 %collective-permute-start.3 = (bf16[8,2048]{1,0:T(8,128)(2,1)S(1)}, bf16[8,2048]{1,0:T(8,128)(2,1)S(1)}, u32[]{:S(2)}, u32[]{:S(2)}) collective-permute-start(bf16[8,2048]{1,0:T(8,128)(2,1)S(1)} %get-tuple-element.27.refs_0_), channel_id=1, source_target_pairs={{0,2},{1,3},{2,0},{3,1},{4,6},{5,7},{6,4},{7,5},{8,10},{9,11},{10,... | collective-permute-start | bytes 98312 | tf_op jit(solution)/shard_map/ppermute | solution.py:31
  11.7 10.5 %collective-permute-start.4 = (bf16[32,4096]{1,0:T(8,128)(2,1)S(1)}, bf16[32,4096]{1,0:T(8,128)(2,1)S(1)}, u32[]{:S(2)}, u32[]{:S(2)}) collective-permute-start(bf16[32,4096]{1,0:T(8,128)(2,1)S(1)} %stack.4.after_ref.refs_0_), channel_id=1, source_target_pairs={{0,2},{1,3},{2,0},{3,1},{4,6},{5,7},{6,4},{7,5},{8,10},{9,11},{10,... | collective-permute-start | bytes 786440 | tf_op jit(solution)/shard_map/ppermute | solution.py:31
  13.3 6.5 %collective-permute-start.7 = (bf16[16,2048]{1,0:T(8,128)(2,1)S(1)}, bf16[16,2048]{1,0:T(8,128)(2,1)S(1)}, u32[]{:S(2)}, u32[]{:S(2)}) collective-permute-start(bf16[16,2048]{1,0:T(8,128)(2,1)S(1)} %stack.3.refs_4_.refs_2_), channel_id=1, source_target_pairs={{0,12},{1,13},{2,14},{3,15},{4,8},{5,9},{6,10},{7,11},{8,4},{9,5},... | collective-permute-start | bytes 196616 | tf_op jit(solution)/shard_map/ppermute | solution.py:31
  16.2 6.0 %collective-permute-start.6 = (bf16[16,2048]{1,0:T(8,128)(2,1)S(1)}, bf16[16,2048]{1,0:T(8,128)(2,1)S(1)}, u32[]{:S(2)}, u32[]{:S(2)}) collective-permute-start(bf16[16,2048]{1,0:T(8,128)(2,1)S(1)} %stack.3.refs_4_.refs_2_), channel_id=1, source_target_pairs={{0,8},{1,9},{2,10},{3,11},{4,12},{5,13},{6,14},{7,15},{8,0},{9,1},... | collective-permute-start | bytes 196616 | tf_op jit(solution)/shard_map/ppermute | solution.py:31
  16.2 6.0 %collective-permute-start.5 = (bf16[16,2048]{1,0:T(8,128)(2,1)S(1)}, bf16[16,2048]{1,0:T(8,128)(2,1)S(1)}, u32[]{:S(2)}, u32[]{:S(2)}) collective-permute-start(bf16[16,2048]{1,0:T(8,128)(2,1)S(1)} %stack.3.refs_4_.refs_2_), channel_id=1, source_target_pairs={{0,4},{1,5},{2,6},{3,7},{4,0},{5,1},{6,2},{7,3},{8,12},{9,13},{10,... | collective-permute-start | bytes 196616 | tf_op jit(solution)/shard_map/ppermute | solution.py:31
  22.2 2.4 %collective-permute-start.8 = (bf16[64,6144]{1,0:T(8,128)(2,1)S(1)}, bf16[64,6144]{1,0:T(8,128)(2,1)S(1)}, u32[]{:S(2)}, u32[]{:S(2)}) collective-permute-start(bf16[64,6144]{1,0:T(8,128)(2,1)S(1)} %stack.5.half_ref), channel_id=1, source_target_pairs={{0,1},{1,0},{2,3},{3,2},{4,5},{5,4},{6,7},{7,6},{8,9},{9,8},{10,11... | collective-permute-start | bytes 2359304 | tf_op jit(solution)/shard_map/ppermute | solution.py:31
  36.7 4.7 %collective-permute-start.9 = (bf16[64,4096]{1,0:T(8,128)(2,1)S(1)}, bf16[64,4096]{1,0:T(8,128)(2,1)S(1)}, u32[]{:S(2)}, u32[]{:S(2)}) collective-permute-start(bf16[64,4096]{1,0:T(8,128)(2,1)S(1)} %get-tuple-element.33), channel_id=1, source_target_pairs={{0,1},{1,0},{2,3},{3,2},{4,5},{5,4},{6,7},{7,6},{8,9},{9,8},{10,11... | collective-permute-start | bytes 1572872 | tf_op jit(solution)/shard_map/ppermute | solution.py:31
  40.9 1.6 %collective-permute-start.14 = (bf16[64,2048]{1,0:T(8,128)(2,1)S(1)}, bf16[64,2048]{1,0:T(8,128)(2,1)S(1)}, u32[]{:S(2)}, u32[]{:S(2)}) collective-permute-start(bf16[64,2048]{1,0:T(8,128)(2,1)S(1)} %get-tuple-element.42), channel_id=1, source_target_pairs={{0,1},{1,0},{2,3},{3,2},{4,5},{5,4},{6,7},{7,6},{8,9},{9,8},{10,11... | collective-permute-start | bytes 786440 | tf_op jit(solution)/shard_map/ppermute | solution.py:31
  41.4 8.4 %collective-permute-start.10 = (bf16[32,4096]{1,0:T(8,128)(2,1)S(1)}, bf16[32,4096]{1,0:T(8,128)(2,1)S(1)}, u32[]{:S(2)}, u32[]{:S(2)}) collective-permute-start(bf16[32,4096]{1,0:T(8,128)(2,1)S(1)} %get-tuple-element.35), channel_id=1, source_target_pairs={{0,2},{1,3},{2,0},{3,1},{4,6},{5,7},{6,4},{7,5},{8,10},{9,11},{10,... | collective-permute-start | bytes 786440 | tf_op jit(solution)/shard_map/ppermute | solution.py:31
  42.6 9.8 %collective-permute-start.15 = (bf16[16,2048]{1,0:T(8,128)(2,1)S(1)}, bf16[16,2048]{1,0:T(8,128)(2,1)S(1)}, u32[]{:S(2)}, u32[]{:S(2)}) collective-permute-start(bf16[16,2048]{1,0:T(8,128)(2,1)S(1)} %get-tuple-element.44), channel_id=1, source_target_pairs={{0,4},{1,5},{2,6},{3,7},{4,0},{5,1},{6,2},{7,3},{8,12},{9,13},{10,... | collective-permute-start | bytes 196616 | tf_op jit(solution)/shard_map/ppermute | solution.py:31
  42.9 11.5 %collective-permute-start.16 = (bf16[16,2048]{1,0:T(8,128)(2,1)S(1)}, bf16[16,2048]{1,0:T(8,128)(2,1)S(1)}, u32[]{:S(2)}, u32[]{:S(2)}) collective-permute-start(bf16[16,2048]{1,0:T(8,128)(2,1)S(1)} %get-tuple-element.45), channel_id=1, source_target_pairs={{0,8},{1,9},{2,10},{3,11},{4,12},{5,13},{6,14},{7,15},{8,0},{9,1},... | collective-permute-start | bytes 196616 | tf_op jit(solution)/shard_map/ppermute | solution.py:31
  45.2 9.2 %collective-permute-start.17 = (bf16[16,2048]{1,0:T(8,128)(2,1)S(1)}, bf16[16,2048]{1,0:T(8,128)(2,1)S(1)}, u32[]{:S(2)}, u32[]{:S(2)}) collective-permute-start(bf16[16,2048]{1,0:T(8,128)(2,1)S(1)} %get-tuple-element.46), channel_id=1, source_target_pairs={{0,12},{1,13},{2,14},{3,15},{4,8},{5,9},{6,10},{7,11},{8,4},{9,5},... | collective-permute-start | bytes 196616 | tf_op jit(solution)/shard_map/ppermute | solution.py:31
  49.9 8.5 %collective-permute-start.11 = (bf16[8,4096]{1,0:T(8,128)(2,1)S(1)}, bf16[8,4096]{1,0:T(8,128)(2,1)S(1)}, u32[]{:S(2)}, u32[]{:S(2)}) collective-permute-start(bf16[8,4096]{1,0:T(8,128)(2,1)S(1)} %get-tuple-element.37), channel_id=1, source_target_pairs={{0,4},{1,5},{2,6},{3,7},{4,0},{5,1},{6,2},{7,3},{8,12},{9,13},{10,... | collective-permute-start | bytes 196616 | tf_op jit(solution)/shard_map/ppermute | solution.py:31
  50.0 8.4 %collective-permute-start.12 = (bf16[8,4096]{1,0:T(8,128)(2,1)S(1)}, bf16[8,4096]{1,0:T(8,128)(2,1)S(1)}, u32[]{:S(2)}, u32[]{:S(2)}) collective-permute-start(bf16[8,4096]{1,0:T(8,128)(2,1)S(1)} %get-tuple-element.38), channel_id=1, source_target_pairs={{0,8},{1,9},{2,10},{3,11},{4,12},{5,13},{6,14},{7,15},{8,0},{9,1},... | collective-permute-start | bytes 196616 | tf_op jit(solution)/shard_map/ppermute | solution.py:31
  52.3 6.2 %collective-permute-start.13 = (bf16[8,4096]{1,0:T(8,128)(2,1)S(1)}, bf16[8,4096]{1,0:T(8,128)(2,1)S(1)}, u32[]{:S(2)}, u32[]{:S(2)}) collective-permute-start(bf16[8,4096]{1,0:T(8,128)(2,1)S(1)} %get-tuple-element.39), channel_id=1, source_target_pairs={{0,12},{1,13},{2,14},{3,15},{4,8},{5,9},{6,10},{7,11},{8,4},{9,5},... | collective-permute-start | bytes 196616 | tf_op jit(solution)/shard_map/ppermute | solution.py:31
  54.4 4.0 %collective-permute-start.18 = (bf16[8,2048]{1,0:T(8,128)(2,1)S(1)}, bf16[8,2048]{1,0:T(8,128)(2,1)S(1)}, u32[]{:S(2)}, u32[]{:S(2)}) collective-permute-start(bf16[8,2048]{1,0:T(8,128)(2,1)S(1)} %slice.12), channel_id=1, source_target_pairs={{0,2},{1,3},{2,0},{3,1},{4,6},{5,7},{6,4},{7,5},{8,10},{9,11},{10,... | collective-permute-start | bytes 98312 | tf_op jit(solution)/shard_map/ppermute | solution.py:31

commit v3 on v2

--- a/solution.py
+++ b/solution.py
@@ -8,7 +8,7 @@
 from jax.sharding import PartitionSpec as P
 
 MIB = 1 << 20
-SCOPED = 18
+SCOPED = 10
 VMEM = pl.BlockSpec(memory_space=pltpu.VMEM)
 ANY = pl.BlockSpec(memory_space=pl.ANY)
 BF16, F32 = jnp.bfloat16, jnp.float32
@@ -75,16 +75,16 @@
     )(*[in_vmem(part) for part in parts], after)
 
 
-def load_kernel(w_ref, after_ref, out_ref, token_ref, sem):
-    copy = pltpu.make_async_copy(w_ref.at[0], out_ref, sem)
+def load_kernel(e, w_ref, after_ref, out_ref, token_ref, sem):
+    copy = pltpu.make_async_copy(w_ref.at[e], out_ref, sem)
     copy.start()
     token_ref[...] = jnp.zeros_like(token_ref)
     copy.wait()
 
 
-def load(w, after):
-    return pl.pallas_call(
-        load_kernel,
+def load(w, e, after):
+    return pl.pallas_call(
+        functools.partial(load_kernel, e),
         in_specs=[ANY, ANY],
         out_specs=[VMEM, VMEM],
         out_shape=[pltpu.VMEM(w.shape[1:], w.dtype), pltpu.VMEM((8, 128), F32)],
@@ -139,146 +139,109 @@
 
 
 def experts_kernel(
-    blocks, half_ref, other_ref, route_ref, order_ref, gate_ref, up_ref, down_ref, old_ref,
-    h_ref, keep_ref, send_ref, first_ref, x_ref, up_buf, up_sem, down_sem,
+    half_ref, other_ref, route_ref, order_ref, gate_ref, up_ref, down_ref, *refs
 ):
+    early = len(refs) // 2 - 3
+    keep_ref, send_ref = refs[early : early + 2]
+    homes = list(refs[early + 2 : 2 * early + 2])
+    x_ref, h_ref, up_buf, up_sem, down_sem = refs[2 * early + 2 :]
     half, width = half_ref.shape
     experts, units, _ = down_ref.shape
     depth = experts * units
-    up_homes = [first_ref] + [up_buf.at[e % 2] for e in range(1, experts - 1)] + [first_ref]
-    up_copies = [None] + [pltpu.make_async_copy(up_ref.at[e], up_homes[e], up_sem.at[e]) for e in range(1, experts)]
+    blocks = width // units
     fit = width // depth
-    homes = [ref.at[pl.ds(at * experts, experts)] for ref in (up_buf.at[1], up_buf.at[0], first_ref) for at in range(fit)]
+    homes.append(up_buf)
+    homes += homes[: experts - early - 1]
+    up_copies = {e: pltpu.make_async_copy(up_ref.at[e], homes[e], up_sem.at[e]) for e in range(early, experts)}
+    down_homes = homes[experts - early - 1 : experts]
+    down_homes = [ref.at[pl.ds(i * experts, experts)] for ref in down_homes for i in range(fit)]
+    slots = len(down_homes)
 
     def block_copy(b):
-        return pltpu.make_async_copy(down_ref.at[:, :, pl.ds(b * units, units)], homes[b], down_sem.at[b])
+        return pltpu.make_async_copy(
+            down_ref.at[:, :, pl.ds(b * units, units)], down_homes[b % slots], down_sem.at[b % slots]
+        )
 
     def start_blocks(first, last):
         for b in range(first, min(last, blocks)):
             block_copy(b).start()
 
-    for copy in up_copies[1:3]:
-        copy.start()
+    up_copies[early].start()
     x_ref[:half] = half_ref[...]
     x_ref[half:] = other_ref[...]
     for e in range(experts):
         gate = jnp.dot(x_ref[...], gate_ref[e], preferred_element_type=F32)
-        if e:
+        if e in up_copies:
             up_copies[e].wait()
-        up = jnp.dot(x_ref[...], up_homes[e].reshape(width, units)[...], preferred_element_type=F32)
-        if e == 0:
-            for copy in up_copies[3:]:
-                copy.start()
-        elif e == 1:
-            start_blocks(0, fit)
-        elif e == 2:
-            start_blocks(fit, 2 * fit)
+        up = jnp.dot(x_ref[...], homes[e].reshape(width, units)[...], preferred_element_type=F32)
+        if e + early + 1 < experts:
+            up_copies[e + early + 1].start()
         else:
-            start_blocks(2 * fit, blocks)
+            first = (e + early + 1 - experts) * fit
+            start_blocks(first, min(first + fit, slots))
         hidden = gate / (1.0 + jnp.exp(-gate)) * up * route_ref[e]
         hidden = jnp.dot(order_ref[...], hidden.astype(BF16), preferred_element_type=F32)
         h_ref[:, e * units : (e + 1) * units] = hidden.astype(BF16)
     for b in range(blocks):
         block_copy(b).wait()
-        total = jnp.dot(h_ref[...], homes[b].reshape(depth, units)[...], preferred_element_type=F32)
+        w = down_homes[b % slots].reshape(depth, units)
+        total = jnp.dot(h_ref[...], w[...], preferred_element_type=F32)
+        start_blocks(b + slots, b + slots + 1)
         keep_ref[:, b * units : (b + 1) * units] = total[:half]
         send_ref[:, b * units : (b + 1) * units] = total[half:].astype(BF16)
 
 
-def experts_of(half, other, route, order, w_gate, w_up, w_down, first_up, blocks):
+def experts_of(half, other, route, order, w_gate, w_up, w_down, early):
     experts, units, width = w_down.shape
     rows = 2 * half.shape[0]
-    columns = blocks * units
-    depth = experts * units
-    h, keep, send, _ = pl.pallas_call(
-        functools.partial(experts_kernel, blocks),
-        in_specs=[VMEM] * 5 + [ANY] * 2 + [VMEM],
-        out_specs=[VMEM] * 4,
-        out_shape=[
-            pltpu.VMEM((rows, depth), BF16),
-            pltpu.VMEM((rows // 2, columns), F32),
-            pltpu.VMEM((rows // 2, columns), BF16),
-            pltpu.VMEM(first_up.shape, first_up.dtype),
-        ],
+    keep, send, *_ = pl.pallas_call(
+        experts_kernel,
+        in_specs=[VMEM] * 5 + [ANY] * 2 + [VMEM] * len(early),
+        out_specs=[VMEM] * (2 + len(early)),
+        out_shape=[pltpu.VMEM((rows // 2, width), F32), pltpu.VMEM((rows // 2, width), BF16)]
+        + [pltpu.VMEM(w.shape, w.dtype) for w in early],
         scratch_shapes=[
             pltpu.VMEM((rows, width), BF16),
-            pltpu.VMEM((2, width // units, units, units), BF16),
+            pltpu.VMEM((rows, experts * units), BF16),
+            pltpu.VMEM(early[0].shape, BF16),
             pltpu.SemaphoreType.DMA((experts,)),
-            pltpu.SemaphoreType.DMA((blocks,)),
+            pltpu.SemaphoreType.DMA((width // units,)),
         ],
-        input_output_aliases={7: 3},
+        input_output_aliases={7 + i: 2 + i for i in range(len(early))},
         compiler_params=pltpu.CompilerParams(vmem_limit_bytes=SCOPED * MIB),
         cost_estimate=cost(0, 8 * w_down.size),
         name="experts",
     )(
-        in_vmem(half), in_vmem(other), in_vmem(route), in_vmem(order),
-        in_vmem(w_gate), in_hbm(w_up), in_hbm(w_down), in_vmem(first_up),
+        in_vmem(half), in_vmem(other), in_vmem(route), in_vmem(order), in_vmem(w_gate), in_hbm(w_up), in_hbm(w_down),
+        *[in_vmem(w) for w in early],
     )
-    return h, keep, send
-
-
-def down_kernel(first, h_ref, down_ref, keep_ref, send_ref, w_ref, sem):
-    half = keep_ref.shape[0]
-    experts, units, _ = down_ref.shape
-    blocks = w_ref.shape[0]
-    copies = [
-        [
-            pltpu.make_async_copy(
-                down_ref.at[e, :, pl.ds((first + b) * units, units)], w_ref.at[b, pl.ds(e * units, units)], sem.at[b, e]
-            )
-            for e in range(experts)
-        ]
-        for b in range(blocks)
-    ]
-    for block in copies:
-        for copy in block:
-            copy.start()
-    for b, block in enumerate(copies):
-        for copy in block:
-            copy.wait()
-        total = jnp.dot(h_ref[...], w_ref[b], preferred_element_type=F32)
-        keep_ref[:, b * units : (b + 1) * units] = total[:half]
-        send_ref[:, b * units : (b + 1) * units] = total[half:].astype(BF16)
-
-
-def down(h, w_down, first, blocks):
-    experts, units, _ = w_down.shape
-    rows, depth = h.shape
-    half, columns = rows // 2, blocks * units
-    return pl.pallas_call(
-        functools.partial(down_kernel, first),
-        in_specs=[VMEM, ANY],
-        out_specs=[VMEM] * 2,
-        out_shape=[pltpu.VMEM((half, columns), F32), pltpu.VMEM((half, columns), BF16)],
-        scratch_shapes=[pltpu.VMEM((blocks, depth, units), BF16), pltpu.SemaphoreType.DMA((blocks, experts))],
-        compiler_params=pltpu.CompilerParams(vmem_limit_bytes=16 * MIB),
-        cost_estimate=cost(2 * rows * depth * columns, 2 * depth * columns),
-        name="down",
-    )(in_vmem(h), in_hbm(w_down))
-
-
-def add_kernel(groups, keep_ref, got_ref, *out_refs):
-    count = sum(len(group) for group in groups)
-    per = keep_ref.shape[0] // count
+    return keep, send
+
+
+def add_kernel(first, groups, keep_ref, *refs):
+    got_refs, out_refs = refs[: -len(groups)], refs[-len(groups) :]
+    per = out_refs[0].shape[0] // len(groups[0])
+    columns = slice(first, first + out_refs[0].shape[1])
     for group, out_ref in zip(groups, out_refs):
         for i, block in enumerate(group):
             rows = slice(block * per, (block + 1) * per)
-            total = keep_ref[rows] + got_ref[rows].astype(F32)
+            total = keep_ref[rows, columns]
+            for got_ref in got_refs:
+                total = total + got_ref[rows, columns].astype(F32)
             out_ref[i * per : (i + 1) * per] = total.astype(out_ref.dtype)
 
 
-def add(keep, got, groups):
+def add(keep, gots, first, columns, groups):
     per = keep.shape[0] // sum(len(group) for group in groups)
-    columns = keep.shape[1]
-    return pl.pallas_call(
-        functools.partial(add_kernel, groups),
-        in_specs=[VMEM, VMEM],
+    return pl.pallas_call(
+        functools.partial(add_kernel, first, groups),
+        in_specs=[VMEM] * (1 + len(gots)),
         out_specs=[VMEM] * len(groups),
         out_shape=[pltpu.VMEM((per * len(g), columns), BF16 if i else F32) for i, g in enumerate(groups)],
         compiler_params=pltpu.CompilerParams(vmem_limit_bytes=2 * MIB),
-        cost_estimate=cost(0, 8 * keep.size),
+        cost_estimate=cost(0, 8 * keep.shape[0] * columns),
         name="add",
-    )(in_vmem(keep), in_vmem(got))
+    )(in_vmem(keep), *[in_vmem(got) for got in gots])
 
 
 def sum_kernel(far, *refs):
@@ -311,12 +274,13 @@
     za = [swap(xa, 4 * z) for z in range(1, far)]
     yb = swap(xb, 2)
     w_up = w_up.reshape(experts, blocks, units, units)
-    first_up, ready = load(w_up, xa)
+    up0, ready = load(w_up, 0, xa)
     xb = stack([xb, yb], [(0, [0]), (0, [1])], (2 * per, b), ready)
     zb = [swap(xb, 4 * z) for z in range(1, far)]
     xa = stack([xa] + za, [(0, [z]) for z in range(far)], (far * per, a), xb)
     ya = swap(xa, 2)
-    route, order = plan(expert_ids, gate_weights, return_order, experts, n, own, xa)
+    up1, ready = load(w_up, 1, xa)
+    route, order = plan(expert_ids, gate_weights, return_order, experts, n, own, ready)
     half = stack(
         [xa, ya, xb] + zb,
         [(0, [0]), (0, [1])] + [(a, [z, far + z]) for z in range(far)],
@@ -324,20 +288,16 @@
         order,
     )
     other = swap(half, 1)
-    h, keep_a, send_a = experts_of(half, other, route, order, w_gate, w_up, w_down, first_up, lead)
-    got_a = swap(send_a, 1)
-    keep_b, send_b = down(h, w_down, lead, blocks - lead)
-    got_b = swap(send_b, 1)
-    keep_a, send_a = add(keep_a, got_a, [list(range(far)), list(range(far, 2 * far))])
+    keep, send = experts_of(half, other, route, order, w_gate, w_up, w_down, [up0, up1])
+
+    got = swap(send, 1)
+    keep_a, send_a = add(keep, [got], 0, a, [list(range(far)), list(range(far, 2 * far))])
     got_a = swap(send_a, 2)
-    keep_b, *send_b = add(keep_b, got_b, [[z, far + z] for z in range(far)])
+    keep_b, *send_b = add(keep, [got], a, b, [[z, far + z] for z in range(far)])
     got_b = [swap(send, 4 * (z + 1)) for z, send in enumerate(send_b)]
-    keep_a, *send_a = add(keep_a, got_a, [[z] for z in range(far)])
+    keep_a, *send_a = add(keep_a, [got_a], 0, a, [[z] for z in range(far)])
     got_a = [swap(send, 4 * (z + 1)) for z, send in enumerate(send_a)]
-    total_b = keep_b
-    for got in got_b:
-        total_b = total_b + got.astype(F32)
-    keep_b, send_b = total_b[:per], total_b[per:].astype(BF16)
+    keep_b, send_b = add(keep_b, got_b, 0, b, [[0], [1]])
     parts = [keep_a, *got_a, keep_b, swap(send_b, 2)]
     return pl.pallas_call(
         functools.partial(sum_kernel, far),

time: 59.3 us -> 58.5 us (0.987)
  starting transfers between devices: 24.6 us -> 23.5 us
    ppermute x19 -> x18, starting transfers between devices: 24.6 us -> 23.5 us  [swap(): return lax.ppermute(x, 'hid', [(i, i ^ mask) for i in range(n)])]
    ppermute x19 -> x18, waiting for transfers between devices: 13.3 us -> 13.4 us  [swap(): return lax.ppermute(x, 'hid', [(i, i ^ mask) for i in range(n)])]
    pallas_call x6 -> x7, Pallas kernels: 19.1 us -> 19.1 us  [the longest x1 13.2 us: experts_of(): pl.pallas_call(experts_kernel, in_specs=[VMEM] * 5 + [ANY] * 2 + [VMEM] *...]
  transfers between devices with their start and end apart: 19 -> 18, of which waited for: 8 -> 7; matrix products, arithmetic and copies ran while one was open for 0% -> 0% of each run, Pallas kernels for 12% -> 11%
where the time goes in v3:
time: 58.5 us; the launch traced here: 58.3 us
  starting transfers between devices  23.5 us (40%)
  Pallas kernels  20.3 us (35%)
  waiting for transfers between devices  13.4 us (23%)
  local copies, waits for them, and re-layouts  0.94 us (2%)
    ppermute x18, starting transfers between devices, swap(): return lax.ppermute(x, 'hid', [(i, i ^ mask) for i in range(n)])  23.5 us
    ppermute x18, waiting for transfers between devices, swap(): return lax.ppermute(x, 'hid', [(i, i ^ mask) for i in range(n)])  13.4 us
    pallas_call x1, Pallas kernels, experts_of(): pl.pallas_call(experts_kernel, in_specs=[VMEM] * 5 + [ANY] * 2 + [VMEM] *...  13.2 us
    pallas_call x2, Pallas kernels, load(): pl.pallas_call(functools.partial(load_kernel, e), in_specs=[ANY, ANY], ou...  5.75 us
  transfers between devices with their start and end apart: 18, of which 7 were waited for; matrix products, arithmetic and copies ran while one was open for 0% of the time, Pallas kernels for 11%

profile of v3, /device:TPU:0, one launch (start us, length us, event | category | flops | bytes accessed | tf_op | source)
XLA Modules:
  0.0 58.3 jit_solution(294668312480090085)
XLA Ops:
  0.0 0.9 %copy-done = bf16[4,2,6144]{2,1,0:T(2,128)(2,1)S(1)} copy-done((bf16[4,2,6144]{2,1,0:T(2,128)(2,1)S(1)}, bf16[4,2,6144]{2,1,0:T(2,128)(2,1)}, u32[]{:S(2)}) %copy-start) | copy-done | bytes 98328
  1.0 5.1 %collective-permute-start.2 = (bf16[8,4096]{1,0:T(8,128)(2,1)S(1)}, bf16[8,4096]{1,0:T(8,128)(2,1)S(1)}, u32[]{:S(2)}, u32[]{:S(2)}) collective-permute-start(bf16[8,4096]{1,0:T(8,128)(2,1)S(1)} %get-tuple-element.27.after_ref.refs_0_), channel_id=1, source_target_pairs={{0,12},{1,13},{2,14},{3,15},{4,8},{5,9},{6,10},{7,11},{8,4},{9,5},... | collective-permute-start | bytes 196616 | tf_op jit(solution)/shard_map/ppermute | solution.py:31
  6.1 0.6 %collective-permute-start = (bf16[8,4096]{1,0:T(8,128)(2,1)S(1)}, bf16[8,4096]{1,0:T(8,128)(2,1)S(1)}, u32[]{:S(2)}, u32[]{:S(2)}) collective-permute-start(bf16[8,4096]{1,0:T(8,128)(2,1)S(1)} %get-tuple-element.27.after_ref.refs_0_), channel_id=1, source_target_pairs={{0,4},{1,5},{2,6},{3,7},{4,0},{5,1},{6,2},{7,3},{8,12},{9,13},{10,... | collective-permute-start | bytes 196616 | tf_op jit(solution)/shard_map/ppermute | solution.py:31
  6.7 1.7 %collective-permute-start.3 = (bf16[8,2048]{1,0:T(8,128)(2,1)S(1)}, bf16[8,2048]{1,0:T(8,128)(2,1)S(1)}, u32[]{:S(2)}, u32[]{:S(2)}) collective-permute-start(bf16[8,2048]{1,0:T(8,128)(2,1)S(1)} %get-tuple-element.28.refs_0_), channel_id=1, source_target_pairs={{0,2},{1,3},{2,0},{3,1},{4,6},{5,7},{6,4},{7,5},{8,10},{9,11},{10,... | collective-permute-start | bytes 98312 | tf_op jit(solution)/shard_map/ppermute | solution.py:31
  8.4 2.9 %load.2 = (bf16[12,512,512]{2,1,0:T(8,128)(2,1)S(1)}, f32[8,128]{1,0:T(8,128)S(1)}) custom-call(bf16[4,12,512,512]{3,2,1,0:T(8,128)(2,1)} %bitcast.7, bf16[8,4096]{1,0:T(8,128)(2,1)S(1)} %get-tuple-element.27.after_ref.refs_0_), custom_call_target="tpu_custom_call" | custom-call | bytes 6291456 | tf_op jit(solution)/shard_map/load/pallas_call | solution.py:86
  11.8 1.6 %collective-permute-start.4 = (bf16[32,4096]{1,0:T(8,128)(2,1)S(1)}, bf16[32,4096]{1,0:T(8,128)(2,1)S(1)}, u32[]{:S(2)}, u32[]{:S(2)}) collective-permute-start(bf16[32,4096]{1,0:T(8,128)(2,1)S(1)} %stack.4.after_ref.refs_0_), channel_id=1, source_target_pairs={{0,2},{1,3},{2,0},{3,1},{4,6},{5,7},{6,4},{7,5},{8,10},{9,11},{10,... | collective-permute-start | bytes 786440 | tf_op jit(solution)/shard_map/ppermute | solution.py:31
  13.4 2.7 %collective-permute-start.7 = (bf16[16,2048]{1,0:T(8,128)(2,1)S(1)}, bf16[16,2048]{1,0:T(8,128)(2,1)S(1)}, u32[]{:S(2)}, u32[]{:S(2)}) collective-permute-start(bf16[16,2048]{1,0:T(8,128)(2,1)S(1)} %stack.3.refs_4_.refs_2_), channel_id=1, source_target_pairs={{0,12},{1,13},{2,14},{3,15},{4,8},{5,9},{6,10},{7,11},{8,4},{9,5},... | collective-permute-start | bytes 196616 | tf_op jit(solution)/shard_map/ppermute | solution.py:31
  16.1 1.7 %collective-permute-start.5 = (bf16[16,2048]{1,0:T(8,128)(2,1)S(1)}, bf16[16,2048]{1,0:T(8,128)(2,1)S(1)}, u32[]{:S(2)}, u32[]{:S(2)}) collective-permute-start(bf16[16,2048]{1,0:T(8,128)(2,1)S(1)} %stack.3.refs_4_.refs_2_), channel_id=1, source_target_pairs={{0,4},{1,5},{2,6},{3,7},{4,0},{5,1},{6,2},{7,3},{8,12},{9,13},{10,... | collective-permute-start | bytes 196616 | tf_op jit(solution)/shard_map/ppermute | solution.py:31
  17.7 2.8 %load.3 = (bf16[12,512,512]{2,1,0:T(8,128)(2,1)S(1)}, f32[8,128]{1,0:T(8,128)S(1)}) custom-call(bf16[4,12,512,512]{3,2,1,0:T(8,128)(2,1)} %bitcast.8, bf16[32,4096]{1,0:T(8,128)(2,1)S(1)} %stack.4.after_ref.refs_0_), custom_call_target="tpu_custom_call" | custom-call | bytes 6291456 | tf_op jit(solution)/shard_map/load/pallas_call | solution.py:86
  20.9 1.3 %collective-permute-done.6.refs_4_ = bf16[16,2048]{1,0:T(8,128)(2,1)S(1)} collective-permute-done((bf16[16,2048]{1,0:T(8,128)(2,1)S(1)}, bf16[16,2048]{1,0:T(8,128)(2,1)S(1)}, u32[]{:S(2)}, u32[]{:S(2)}) %collective-permute-start.6) | collective-permute-done | bytes 65568 | tf_op jit(solution)/shard_map/ppermute | solution.py:31
  22.4 2.3 %collective-permute-done.8.other_ref = bf16[64,6144]{1,0:T(8,128)(2,1)S(1)} collective-permute-done((bf16[64,6144]{1,0:T(8,128)(2,1)S(1)}, bf16[64,6144]{1,0:T(8,128)(2,1)S(1)}, u32[]{:S(2)}, u32[]{:S(2)}) %collective-permute-start.8) | collective-permute-done | bytes 786464 | tf_op jit(solution)/shard_map/ppermute | solution.py:31
  24.7 13.2 %experts.1 = (f32[64,6144]{1,0:T(8,128)S(1)}, bf16[64,6144]{1,0:T(8,128)(2,1)S(1)}, bf16[12,512,512]{2,1,0:T(8,128)(2,1)S(1)}, bf16[12,512,512]{2,1,0:T(8,128)(2,1)S(1)}) custom-call(bf16[64,6144]{1,0:T(8,128)(2,1)S(1)} %stack.5.half_ref, bf16[64,6144]{1,0:T(8,128)(2,1)S(1)} %collective-permute-done.8.other_ref, ...), custom_call_target="tpu_custom_call", output_to_operand_aliasing={{2}: (7, {}), {3}: (8, {})} | custom-call | bytes 100663296 | tf_op jit(solution)/shard_map/experts/pallas_call | solution.py:197
  38.1 2.2 %collective-permute-done.9.refs_0_ = bf16[64,6144]{1,0:T(8,128)(2,1)S(1)} collective-permute-done((bf16[64,6144]{1,0:T(8,128)(2,1)S(1)}, bf16[64,6144]{1,0:T(8,128)(2,1)S(1)}, u32[]{:S(2)}, u32[]{:S(2)}) %collective-permute-start.9) | collective-permute-done | bytes 786464 | tf_op jit(solution)/shard_map/ppermute | solution.py:31
  40.3 0.5 collective-permute-start.10
  40.8 0.4 collective-permute-start.14
  41.2 2.6 %collective-permute-start.15 = (bf16[16,2048]{1,0:T(8,128)(2,1)S(1)}, bf16[16,2048]{1,0:T(8,128)(2,1)S(1)}, u32[]{:S(2)}, u32[]{:S(2)}) collective-permute-start(bf16[16,2048]{1,0:T(8,128)(2,1)S(1)} %get-tuple-element.45), channel_id=1, source_target_pairs={{0,8},{1,9},{2,10},{3,11},{4,12},{5,13},{6,14},{7,15},{8,0},{9,1},... | collective-permute-start | bytes 196616 | tf_op jit(solution)/shard_map/ppermute | solution.py:31
  43.8 1.5 %collective-permute-start.16 = (bf16[16,2048]{1,0:T(8,128)(2,1)S(1)}, bf16[16,2048]{1,0:T(8,128)(2,1)S(1)}, u32[]{:S(2)}, u32[]{:S(2)}) collective-permute-start(bf16[16,2048]{1,0:T(8,128)(2,1)S(1)} %get-tuple-element.46), channel_id=1, source_target_pairs={{0,12},{1,13},{2,14},{3,15},{4,8},{5,9},{6,10},{7,11},{8,4},{9,5},... | collective-permute-start | bytes 196616 | tf_op jit(solution)/shard_map/ppermute | solution.py:31
  45.3 3.5 %collective-permute-done.10.refs_0_ = bf16[32,4096]{1,0:T(8,128)(2,1)S(1)} collective-permute-done((bf16[32,4096]{1,0:T(8,128)(2,1)S(1)}, bf16[32,4096]{1,0:T(8,128)(2,1)S(1)}, u32[]{:S(2)}, u32[]{:S(2)}) %collective-permute-start.10) | collective-permute-done | bytes 262176 | tf_op jit(solution)/shard_map/ppermute | solution.py:31
  48.9 2.6 %collective-permute-start.12 = (bf16[8,4096]{1,0:T(8,128)(2,1)S(1)}, bf16[8,4096]{1,0:T(8,128)(2,1)S(1)}, u32[]{:S(2)}, u32[]{:S(2)}) collective-permute-start(bf16[8,4096]{1,0:T(8,128)(2,1)S(1)} %get-tuple-element.41), channel_id=1, source_target_pairs={{0,8},{1,9},{2,10},{3,11},{4,12},{5,13},{6,14},{7,15},{8,0},{9,1},... | collective-permute-start | bytes 196616 | tf_op jit(solution)/shard_map/ppermute | solution.py:31
  51.4 1.8 %collective-permute-start.13 = (bf16[8,4096]{1,0:T(8,128)(2,1)S(1)}, bf16[8,4096]{1,0:T(8,128)(2,1)S(1)}, u32[]{:S(2)}, u32[]{:S(2)}) collective-permute-start(bf16[8,4096]{1,0:T(8,128)(2,1)S(1)} %get-tuple-element.42), channel_id=1, source_target_pairs={{0,12},{1,13},{2,14},{3,15},{4,8},{5,9},{6,10},{7,11},{8,4},{9,5},... | collective-permute-start | bytes 196616 | tf_op jit(solution)/shard_map/ppermute | solution.py:31
  53.3 0.5 collective-permute-start.17
  53.7 3.5 %collective-permute-done.17.refs_5_ = bf16[8,2048]{1,0:T(8,128)(2,1)S(1)} collective-permute-done((bf16[8,2048]{1,0:T(8,128)(2,1)S(1)}, bf16[8,2048]{1,0:T(8,128)(2,1)S(1)}, u32[]{:S(2)}, u32[]{:S(2)}) %collective-permute-start.17) | collective-permute-done | bytes 32800 | tf_op jit(solution)/shard_map/ppermute | solution.py:31
  57.3 0.3 collective-permute-done.13.refs_3_
  57.6 0.7 %sum.1 = bf16[4,2,6144]{2,1,0:T(2,128)(2,1)} custom-call(f32[8,4096]{1,0:T(8,128)S(1)} %get-tuple-element.39.refs_0_, bf16[8,4096]{1,0:T(8,128)(2,1)S(1)} %collective-permute-done.11.refs_1_, bf16[8,4096]{1,0:T(8,128)(2,1)S(1)} %collective-permute-done.12.refs_2_, bf16[8,4096]{1,0:T(8,128)(2,1)S(1)} %collective-permute-done.13.refs_3_, ...), custom_call_target="tpu_custom_call" | custom-call | bytes 196608 | tf_op jit(solution)/shard_map/sum/pallas_call | solution.py:302
  (46 shorter events, 1.4 us)
Async XLA Ops:
  1.0 10.4 %collective-permute-start.2 = (bf16[8,4096]{1,0:T(8,128)(2,1)S(1)}, bf16[8,4096]{1,0:T(8,128)(2,1)S(1)}, u32[]{:S(2)}, u32[]{:S(2)}) collective-permute-start(bf16[8,4096]{1,0:T(8,128)(2,1)S(1)} %get-tuple-element.27.after_ref.refs_0_), channel_id=1, source_target_pairs={{0,12},{1,13},{2,14},{3,15},{4,8},{5,9},{6,10},{7,11},{8,4},{9,5},... | collective-permute-start | bytes 196616 | tf_op jit(solution)/shard_map/ppermute | solution.py:31
  6.1 5.6 %collective-permute-start.1 = (bf16[8,4096]{1,0:T(8,128)(2,1)S(1)}, bf16[8,4096]{1,0:T(8,128)(2,1)S(1)}, u32[]{:S(2)}, u32[]{:S(2)}) collective-permute-start(bf16[8,4096]{1,0:T(8,128)(2,1)S(1)} %get-tuple-element.27.after_ref.refs_0_), channel_id=1, source_target_pairs={{0,8},{1,9},{2,10},{3,11},{4,12},{5,13},{6,14},{7,15},{8,0},{9,1},... | collective-permute-start | bytes 196616 | tf_op jit(solution)/shard_map/ppermute | solution.py:31
  6.1 5.6 %collective-permute-start = (bf16[8,4096]{1,0:T(8,128)(2,1)S(1)}, bf16[8,4096]{1,0:T(8,128)(2,1)S(1)}, u32[]{:S(2)}, u32[]{:S(2)}) collective-permute-start(bf16[8,4096]{1,0:T(8,128)(2,1)S(1)} %get-tuple-element.27.after_ref.refs_0_), channel_id=1, source_target_pairs={{0,4},{1,5},{2,6},{3,7},{4,0},{5,1},{6,2},{7,3},{8,12},{9,13},{10,... | collective-permute-start | bytes 196616 | tf_op jit(solution)/shard_map/ppermute | solution.py:31
  6.7 4.6 %collective-permute-start.3 = (bf16[8,2048]{1,0:T(8,128)(2,1)S(1)}, bf16[8,2048]{1,0:T(8,128)(2,1)S(1)}, u32[]{:S(2)}, u32[]{:S(2)}) collective-permute-start(bf16[8,2048]{1,0:T(8,128)(2,1)S(1)} %get-tuple-element.28.refs_0_), channel_id=1, source_target_pairs={{0,2},{1,3},{2,0},{3,1},{4,6},{5,7},{6,4},{7,5},{8,10},{9,11},{10,... | collective-permute-start | bytes 98312 | tf_op jit(solution)/shard_map/ppermute | solution.py:31
  8.4 16.3 %slice-start = ((s8[25165824]{0:T(1024)(128)(4,1)}), s8[4194304]{0:T(1024)(128)(4,1)S(1)}, s32[]{:S(2)}) async-start(s8[25165824]{0:T(1024)(128)(4,1)} %bitcast.3), calls=%async_computation | async-start | bytes 8388608
  8.4 16.3 %slice-start.1 = ((s8[25165824]{0:T(1024)(128)(4,1)}), s8[4194304]{0:T(1024)(128)(4,1)S(1)}, s32[]{:S(2)}) async-start(s8[25165824]{0:T(1024)(128)(4,1)} %bitcast.3), calls=%async_computation.1 | async-start | bytes 8388608
  8.4 16.3 %slice-start.2 = ((s8[25165824]{0:T(1024)(128)(4,1)}), s8[4194304]{0:T(1024)(128)(4,1)S(1)}, s32[]{:S(2)}) async-start(s8[25165824]{0:T(1024)(128)(4,1)} %bitcast.3), calls=%async_computation.2 | async-start | bytes 8388608
  11.7 12.9 %slice-start.3 = ((s8[25165824]{0:T(1024)(128)(4,1)}), s8[4194304]{0:T(1024)(128)(4,1)S(1)}, s32[]{:S(2)}) async-start(s8[25165824]{0:T(1024)(128)(4,1)} %bitcast.3), calls=%async_computation.3 | async-start | bytes 8388608
  11.7 12.9 %slice-start.4 = ((s8[25165824]{0:T(1024)(128)(4,1)}), s8[4194304]{0:T(1024)(128)(4,1)S(1)}, s32[]{:S(2)}) async-start(s8[25165824]{0:T(1024)(128)(4,1)} %bitcast.3), calls=%async_computation.4 | async-start | bytes 8388608
  11.8 12.9 %slice-start.5 = ((s8[25165824]{0:T(1024)(128)(4,1)}), s8[4194304]{0:T(1024)(128)(4,1)S(1)}, s32[]{:S(2)}) async-start(s8[25165824]{0:T(1024)(128)(4,1)} %bitcast.3), calls=%async_computation.5 | async-start | bytes 8388608
  11.8 10.5 %collective-permute-start.4 = (bf16[32,4096]{1,0:T(8,128)(2,1)S(1)}, bf16[32,4096]{1,0:T(8,128)(2,1)S(1)}, u32[]{:S(2)}, u32[]{:S(2)}) collective-permute-start(bf16[32,4096]{1,0:T(8,128)(2,1)S(1)} %stack.4.after_ref.refs_0_), channel_id=1, source_target_pairs={{0,2},{1,3},{2,0},{3,1},{4,6},{5,7},{6,4},{7,5},{8,10},{9,11},{10,... | collective-permute-start | bytes 786440 | tf_op jit(solution)/shard_map/ppermute | solution.py:31
  13.4 7.5 %collective-permute-start.7 = (bf16[16,2048]{1,0:T(8,128)(2,1)S(1)}, bf16[16,2048]{1,0:T(8,128)(2,1)S(1)}, u32[]{:S(2)}, u32[]{:S(2)}) collective-permute-start(bf16[16,2048]{1,0:T(8,128)(2,1)S(1)} %stack.3.refs_4_.refs_2_), channel_id=1, source_target_pairs={{0,12},{1,13},{2,14},{3,15},{4,8},{5,9},{6,10},{7,11},{8,4},{9,5},... | collective-permute-start | bytes 196616 | tf_op jit(solution)/shard_map/ppermute | solution.py:31
  16.1 6.1 %collective-permute-start.6 = (bf16[16,2048]{1,0:T(8,128)(2,1)S(1)}, bf16[16,2048]{1,0:T(8,128)(2,1)S(1)}, u32[]{:S(2)}, u32[]{:S(2)}) collective-permute-start(bf16[16,2048]{1,0:T(8,128)(2,1)S(1)} %stack.3.refs_4_.refs_2_), channel_id=1, source_target_pairs={{0,8},{1,9},{2,10},{3,11},{4,12},{5,13},{6,14},{7,15},{8,0},{9,1},... | collective-permute-start | bytes 196616 | tf_op jit(solution)/shard_map/ppermute | solution.py:31
  16.1 6.1 %collective-permute-start.5 = (bf16[16,2048]{1,0:T(8,128)(2,1)S(1)}, bf16[16,2048]{1,0:T(8,128)(2,1)S(1)}, u32[]{:S(2)}, u32[]{:S(2)}) collective-permute-start(bf16[16,2048]{1,0:T(8,128)(2,1)S(1)} %stack.3.refs_4_.refs_2_), channel_id=1, source_target_pairs={{0,4},{1,5},{2,6},{3,7},{4,0},{5,1},{6,2},{7,3},{8,12},{9,13},{10,... | collective-permute-start | bytes 196616 | tf_op jit(solution)/shard_map/ppermute | solution.py:31
  22.3 2.4 %collective-permute-start.8 = (bf16[64,6144]{1,0:T(8,128)(2,1)S(1)}, bf16[64,6144]{1,0:T(8,128)(2,1)S(1)}, u32[]{:S(2)}, u32[]{:S(2)}) collective-permute-start(bf16[64,6144]{1,0:T(8,128)(2,1)S(1)} %stack.5.half_ref), channel_id=1, source_target_pairs={{0,1},{1,0},{2,3},{3,2},{4,5},{5,4},{6,7},{7,6},{8,9},{9,8},{10,11... | collective-permute-start | bytes 2359304 | tf_op jit(solution)/shard_map/ppermute | solution.py:31
  37.9 2.4 %collective-permute-start.9 = (bf16[64,6144]{1,0:T(8,128)(2,1)S(1)}, bf16[64,6144]{1,0:T(8,128)(2,1)S(1)}, u32[]{:S(2)}, u32[]{:S(2)}) collective-permute-start(bf16[64,6144]{1,0:T(8,128)(2,1)S(1)} %get-tuple-element.36), channel_id=1, source_target_pairs={{0,1},{1,0},{2,3},{3,2},{4,5},{5,4},{6,7},{7,6},{8,9},{9,8},{10,11... | collective-permute-start | bytes 2359304 | tf_op jit(solution)/shard_map/ppermute | solution.py:31
  40.3 8.4 %collective-permute-start.10 = (bf16[32,4096]{1,0:T(8,128)(2,1)S(1)}, bf16[32,4096]{1,0:T(8,128)(2,1)S(1)}, u32[]{:S(2)}, u32[]{:S(2)}) collective-permute-start(bf16[32,4096]{1,0:T(8,128)(2,1)S(1)} %get-tuple-element.38), channel_id=1, source_target_pairs={{0,2},{1,3},{2,0},{3,1},{4,6},{5,7},{6,4},{7,5},{8,10},{9,11},{10,... | collective-permute-start | bytes 786440 | tf_op jit(solution)/shard_map/ppermute | solution.py:31
  40.8 10.6 %collective-permute-start.14 = (bf16[16,2048]{1,0:T(8,128)(2,1)S(1)}, bf16[16,2048]{1,0:T(8,128)(2,1)S(1)}, u32[]{:S(2)}, u32[]{:S(2)}) collective-permute-start(bf16[16,2048]{1,0:T(8,128)(2,1)S(1)} %get-tuple-element.44), channel_id=1, source_target_pairs={{0,4},{1,5},{2,6},{3,7},{4,0},{5,1},{6,2},{7,3},{8,12},{9,13},{10,... | collective-permute-start | bytes 196616 | tf_op jit(solution)/shard_map/ppermute | solution.py:31
  41.2 12.0 %collective-permute-start.15 = (bf16[16,2048]{1,0:T(8,128)(2,1)S(1)}, bf16[16,2048]{1,0:T(8,128)(2,1)S(1)}, u32[]{:S(2)}, u32[]{:S(2)}) collective-permute-start(bf16[16,2048]{1,0:T(8,128)(2,1)S(1)} %get-tuple-element.45), channel_id=1, source_target_pairs={{0,8},{1,9},{2,10},{3,11},{4,12},{5,13},{6,14},{7,15},{8,0},{9,1},... | collective-permute-start | bytes 196616 | tf_op jit(solution)/shard_map/ppermute | solution.py:31
  43.8 9.5 %collective-permute-start.16 = (bf16[16,2048]{1,0:T(8,128)(2,1)S(1)}, bf16[16,2048]{1,0:T(8,128)(2,1)S(1)}, u32[]{:S(2)}, u32[]{:S(2)}) collective-permute-start(bf16[16,2048]{1,0:T(8,128)(2,1)S(1)} %get-tuple-element.46), channel_id=1, source_target_pairs={{0,12},{1,13},{2,14},{3,15},{4,8},{5,9},{6,10},{7,11},{8,4},{9,5},... | collective-permute-start | bytes 196616 | tf_op jit(solution)/shard_map/ppermute | solution.py:31
  48.8 8.5 %collective-permute-start.11 = (bf16[8,4096]{1,0:T(8,128)(2,1)S(1)}, bf16[8,4096]{1,0:T(8,128)(2,1)S(1)}, u32[]{:S(2)}, u32[]{:S(2)}) collective-permute-start(bf16[8,4096]{1,0:T(8,128)(2,1)S(1)} %get-tuple-element.40), channel_id=1, source_target_pairs={{0,4},{1,5},{2,6},{3,7},{4,0},{5,1},{6,2},{7,3},{8,12},{9,13},{10,... | collective-permute-start | bytes 196616 | tf_op jit(solution)/shard_map/ppermute | solution.py:31
  48.9 8.4 %collective-permute-start.12 = (bf16[8,4096]{1,0:T(8,128)(2,1)S(1)}, bf16[8,4096]{1,0:T(8,128)(2,1)S(1)}, u32[]{:S(2)}, u32[]{:S(2)}) collective-permute-start(bf16[8,4096]{1,0:T(8,128)(2,1)S(1)} %get-tuple-element.41), channel_id=1, source_target_pairs={{0,8},{1,9},{2,10},{3,11},{4,12},{5,13},{6,14},{7,15},{8,0},{9,1},... | collective-permute-start | bytes 196616 | tf_op jit(solution)/shard_map/ppermute | solution.py:31
  51.4 6.2 %collective-permute-start.13 = (bf16[8,4096]{1,0:T(8,128)(2,1)S(1)}, bf16[8,4096]{1,0:T(8,128)(2,1)S(1)}, u32[]{:S(2)}, u32[]{:S(2)}) collective-permute-start(bf16[8,4096]{1,0:T(8,128)(2,1)S(1)} %get-tuple-element.42), channel_id=1, source_target_pairs={{0,12},{1,13},{2,14},{3,15},{4,8},{5,9},{6,10},{7,11},{8,4},{9,5},... | collective-permute-start | bytes 196616 | tf_op jit(solution)/shard_map/ppermute | solution.py:31
  53.3 4.0 %collective-permute-start.17 = (bf16[8,2048]{1,0:T(8,128)(2,1)S(1)}, bf16[8,2048]{1,0:T(8,128)(2,1)S(1)}, u32[]{:S(2)}, u32[]{:S(2)}) collective-permute-start(bf16[8,2048]{1,0:T(8,128)(2,1)S(1)} %get-tuple-element.48), channel_id=1, source_target_pairs={{0,2},{1,3},{2,0},{3,1},{4,6},{5,7},{6,4},{7,5},{8,10},{9,11},{10,... | collective-permute-start | bytes 98312 | tf_op jit(solution)/shard_map/ppermute | solution.py:31
  (4 other events, 27.5 us)

commit v4 on v3

--- a/solution.py
+++ b/solution.py
@@ -266,14 +266,12 @@
     far = n // 4
     per = steps * own
     rows = per * n
-    blocks = width // units
-    lead = (2 * blocks + 2) // 3
-    a = lead * units
+    a = width * 3 // 4
     b = width - a
     xa, xb = split(tokens, [a, b])
     za = [swap(xa, 4 * z) for z in range(1, far)]
     yb = swap(xb, 2)
-    w_up = w_up.reshape(experts, blocks, units, units)
+    w_up = w_up.reshape(experts, width // units, units, units)
     up0, ready = load(w_up, 0, xa)
     xb = stack([xb, yb], [(0, [0]), (0, [1])], (2 * per, b), ready)
     zb = [swap(xb, 4 * z) for z in range(1, far)]
@@ -290,6 +288,8 @@
     other = swap(half, 1)
     keep, send = experts_of(half, other, route, order, w_gate, w_up, w_down, [up0, up1])
 
+    a = width * 7 // 12
+    b = width - a
     got = swap(send, 1)
     keep_a, send_a = add(keep, [got], 0, a, [list(range(far)), list(range(far, 2 * far))])
     got_a = swap(send_a, 2)

time: 58.5 us -> 57.6 us (0.985)
  waiting for transfers between devices: 13.4 us -> 11.6 us
  starting transfers between devices: 23.5 us -> 24.4 us
    ppermute x18, waiting for transfers between devices: 13.4 us -> 11.6 us  [swap(): return lax.ppermute(x, 'hid', [(i, i ^ mask) for i in range(n)])]
    ppermute x18, starting transfers between devices: 23.5 us -> 24.4 us  [swap(): return lax.ppermute(x, 'hid', [(i, i ^ mask) for i in range(n)])]
where the time goes in v4:
time: 57.6 us; the launch traced here: 57.4 us
  starting transfers between devices  24.4 us (42%)
  Pallas kernels  20.3 us (35%)
  waiting for transfers between devices  11.6 us (20%)
  local copies, waits for them, and re-layouts  0.94 us (2%)
    ppermute x18, starting transfers between devices, swap(): return lax.ppermute(x, 'hid', [(i, i ^ mask) for i in range(n)])  24.4 us
    pallas_call x1, Pallas kernels, experts_of(): pl.pallas_call(experts_kernel, in_specs=[VMEM] * 5 + [ANY] * 2 + [VMEM] *...  13.2 us
    ppermute x18, waiting for transfers between devices, swap(): return lax.ppermute(x, 'hid', [(i, i ^ mask) for i in range(n)])  11.6 us
    pallas_call x2, Pallas kernels, load(): pl.pallas_call(functools.partial(load_kernel, e), in_specs=[ANY, ANY], ou...  5.75 us
  transfers between devices with their start and end apart: 18, of which 7 were waited for; matrix products, arithmetic and copies ran while one was open for 0% of the time, Pallas kernels for 11%

profile of v4, /device:TPU:0, one launch (start us, length us, event | category | flops | bytes accessed | tf_op | source)
XLA Modules:
  0.0 57.4 jit_solution(2610107243790586913)
XLA Ops:
  0.0 0.9 %copy-done = bf16[4,2,6144]{2,1,0:T(2,128)(2,1)S(1)} copy-done((bf16[4,2,6144]{2,1,0:T(2,128)(2,1)S(1)}, bf16[4,2,6144]{2,1,0:T(2,128)(2,1)}, u32[]{:S(2)}) %copy-start) | copy-done | bytes 98328
  0.9 5.1 %collective-permute-start.2 = (bf16[8,4608]{1,0:T(8,128)(2,1)S(1)}, bf16[8,4608]{1,0:T(8,128)(2,1)S(1)}, u32[]{:S(2)}, u32[]{:S(2)}) collective-permute-start(bf16[8,4608]{1,0:T(8,128)(2,1)S(1)} %get-tuple-element.27.after_ref.refs_0_), channel_id=1, source_target_pairs={{0,12},{1,13},{2,14},{3,15},{4,8},{5,9},{6,10},{7,11},{8,4},{9,5},... | collective-permute-start | bytes 221192 | tf_op jit(solution)/shard_map/ppermute | solution.py:31
  6.1 0.6 %collective-permute-start = (bf16[8,4608]{1,0:T(8,128)(2,1)S(1)}, bf16[8,4608]{1,0:T(8,128)(2,1)S(1)}, u32[]{:S(2)}, u32[]{:S(2)}) collective-permute-start(bf16[8,4608]{1,0:T(8,128)(2,1)S(1)} %get-tuple-element.27.after_ref.refs_0_), channel_id=1, source_target_pairs={{0,4},{1,5},{2,6},{3,7},{4,0},{5,1},{6,2},{7,3},{8,12},{9,13},{10,... | collective-permute-start | bytes 221192 | tf_op jit(solution)/shard_map/ppermute | solution.py:31
  6.7 1.7 %collective-permute-start.3 = (bf16[8,1536]{1,0:T(8,128)(2,1)S(1)}, bf16[8,1536]{1,0:T(8,128)(2,1)S(1)}, u32[]{:S(2)}, u32[]{:S(2)}) collective-permute-start(bf16[8,1536]{1,0:T(8,128)(2,1)S(1)} %get-tuple-element.28.refs_0_), channel_id=1, source_target_pairs={{0,2},{1,3},{2,0},{3,1},{4,6},{5,7},{6,4},{7,5},{8,10},{9,11},{10,... | collective-permute-start | bytes 73736 | tf_op jit(solution)/shard_map/ppermute | solution.py:31
  8.4 2.9 %load.2 = (bf16[12,512,512]{2,1,0:T(8,128)(2,1)S(1)}, f32[8,128]{1,0:T(8,128)S(1)}) custom-call(bf16[4,12,512,512]{3,2,1,0:T(8,128)(2,1)} %bitcast.7, bf16[8,4608]{1,0:T(8,128)(2,1)S(1)} %get-tuple-element.27.after_ref.refs_0_), custom_call_target="tpu_custom_call" | custom-call | bytes 6291456 | tf_op jit(solution)/shard_map/load/pallas_call | solution.py:86
  11.4 0.9 %collective-permute-done.1.refs_2_ = bf16[8,4608]{1,0:T(8,128)(2,1)S(1)} collective-permute-done((bf16[8,4608]{1,0:T(8,128)(2,1)S(1)}, bf16[8,4608]{1,0:T(8,128)(2,1)S(1)}, u32[]{:S(2)}, u32[]{:S(2)}) %collective-permute-start.1) | collective-permute-done | bytes 73760 | tf_op jit(solution)/shard_map/ppermute | solution.py:31
  12.4 1.6 %collective-permute-start.4 = (bf16[32,4608]{1,0:T(8,128)(2,1)S(1)}, bf16[32,4608]{1,0:T(8,128)(2,1)S(1)}, u32[]{:S(2)}, u32[]{:S(2)}) collective-permute-start(bf16[32,4608]{1,0:T(8,128)(2,1)S(1)} %stack.4.after_ref.refs_0_), channel_id=1, source_target_pairs={{0,2},{1,3},{2,0},{3,1},{4,6},{5,7},{6,4},{7,5},{8,10},{9,11},{10,... | collective-permute-start | bytes 884744 | tf_op jit(solution)/shard_map/ppermute | solution.py:31
  14.0 2.7 %collective-permute-start.7 = (bf16[16,1536]{1,0:T(8,128)(2,1)S(1)}, bf16[16,1536]{1,0:T(8,128)(2,1)S(1)}, u32[]{:S(2)}, u32[]{:S(2)}) collective-permute-start(bf16[16,1536]{1,0:T(8,128)(2,1)S(1)} %stack.3.refs_4_.refs_2_), channel_id=1, source_target_pairs={{0,12},{1,13},{2,14},{3,15},{4,8},{5,9},{6,10},{7,11},{8,4},{9,5},... | collective-permute-start | bytes 147464 | tf_op jit(solution)/shard_map/ppermute | solution.py:31
  16.7 1.7 %collective-permute-start.5 = (bf16[16,1536]{1,0:T(8,128)(2,1)S(1)}, bf16[16,1536]{1,0:T(8,128)(2,1)S(1)}, u32[]{:S(2)}, u32[]{:S(2)}) collective-permute-start(bf16[16,1536]{1,0:T(8,128)(2,1)S(1)} %stack.3.refs_4_.refs_2_), channel_id=1, source_target_pairs={{0,4},{1,5},{2,6},{3,7},{4,0},{5,1},{6,2},{7,3},{8,12},{9,13},{10,... | collective-permute-start | bytes 147464 | tf_op jit(solution)/shard_map/ppermute | solution.py:31
  18.4 2.8 %load.3 = (bf16[12,512,512]{2,1,0:T(8,128)(2,1)S(1)}, f32[8,128]{1,0:T(8,128)S(1)}) custom-call(bf16[4,12,512,512]{3,2,1,0:T(8,128)(2,1)} %bitcast.8, bf16[32,4608]{1,0:T(8,128)(2,1)S(1)} %stack.4.after_ref.refs_0_), custom_call_target="tpu_custom_call" | custom-call | bytes 6291456 | tf_op jit(solution)/shard_map/load/pallas_call | solution.py:86
  21.8 2.3 %collective-permute-done.8.other_ref = bf16[64,6144]{1,0:T(8,128)(2,1)S(1)} collective-permute-done((bf16[64,6144]{1,0:T(8,128)(2,1)S(1)}, bf16[64,6144]{1,0:T(8,128)(2,1)S(1)}, u32[]{:S(2)}, u32[]{:S(2)}) %collective-permute-start.8) | collective-permute-done | bytes 786464 | tf_op jit(solution)/shard_map/ppermute | solution.py:31
  24.1 13.2 %experts.1 = (f32[64,6144]{1,0:T(8,128)S(1)}, bf16[64,6144]{1,0:T(8,128)(2,1)S(1)}, bf16[12,512,512]{2,1,0:T(8,128)(2,1)S(1)}, bf16[12,512,512]{2,1,0:T(8,128)(2,1)S(1)}) custom-call(bf16[64,6144]{1,0:T(8,128)(2,1)S(1)} %stack.5.half_ref, bf16[64,6144]{1,0:T(8,128)(2,1)S(1)} %collective-permute-done.8.other_ref, ...), custom_call_target="tpu_custom_call", output_to_operand_aliasing={{2}: (7, {}), {3}: (8, {})} | custom-call | bytes 100663296 | tf_op jit(solution)/shard_map/experts/pallas_call | solution.py:197
  37.5 2.2 %collective-permute-done.9.refs_0_ = bf16[64,6144]{1,0:T(8,128)(2,1)S(1)} collective-permute-done((bf16[64,6144]{1,0:T(8,128)(2,1)S(1)}, bf16[64,6144]{1,0:T(8,128)(2,1)S(1)}, u32[]{:S(2)}, u32[]{:S(2)}) %collective-permute-start.9) | collective-permute-done | bytes 786464 | tf_op jit(solution)/shard_map/ppermute | solution.py:31
  39.8 0.9 %collective-permute-start.10 = (bf16[32,3584]{1,0:T(8,128)(2,1)S(1)}, bf16[32,3584]{1,0:T(8,128)(2,1)S(1)}, u32[]{:S(2)}, u32[]{:S(2)}) collective-permute-start(bf16[32,3584]{1,0:T(8,128)(2,1)S(1)} %get-tuple-element.38), channel_id=1, source_target_pairs={{0,2},{1,3},{2,0},{3,1},{4,6},{5,7},{6,4},{7,5},{8,10},{9,11},{10,... | collective-permute-start | bytes 688136 | tf_op jit(solution)/shard_map/ppermute | solution.py:31
  41.2 2.4 %collective-permute-start.15 = (bf16[16,2560]{1,0:T(8,128)(2,1)S(1)}, bf16[16,2560]{1,0:T(8,128)(2,1)S(1)}, u32[]{:S(2)}, u32[]{:S(2)}) collective-permute-start(bf16[16,2560]{1,0:T(8,128)(2,1)S(1)} %get-tuple-element.45), channel_id=1, source_target_pairs={{0,8},{1,9},{2,10},{3,11},{4,12},{5,13},{6,14},{7,15},{8,0},{9,1},... | collective-permute-start | bytes 245768 | tf_op jit(solution)/shard_map/ppermute | solution.py:31
  43.6 1.6 %collective-permute-start.16 = (bf16[16,2560]{1,0:T(8,128)(2,1)S(1)}, bf16[16,2560]{1,0:T(8,128)(2,1)S(1)}, u32[]{:S(2)}, u32[]{:S(2)}) collective-permute-start(bf16[16,2560]{1,0:T(8,128)(2,1)S(1)} %get-tuple-element.46), channel_id=1, source_target_pairs={{0,12},{1,13},{2,14},{3,15},{4,8},{5,9},{6,10},{7,11},{8,4},{9,5},... | collective-permute-start | bytes 245768 | tf_op jit(solution)/shard_map/ppermute | solution.py:31
  45.2 2.3 %collective-permute-done.10.refs_0_ = bf16[32,3584]{1,0:T(8,128)(2,1)S(1)} collective-permute-done((bf16[32,3584]{1,0:T(8,128)(2,1)S(1)}, bf16[32,3584]{1,0:T(8,128)(2,1)S(1)}, u32[]{:S(2)}, u32[]{:S(2)}) %collective-permute-start.10) | collective-permute-done | bytes 229408 | tf_op jit(solution)/shard_map/ppermute | solution.py:31
  47.5 0.8 %collective-permute-start.11 = (bf16[8,3584]{1,0:T(8,128)(2,1)S(1)}, bf16[8,3584]{1,0:T(8,128)(2,1)S(1)}, u32[]{:S(2)}, u32[]{:S(2)}) collective-permute-start(bf16[8,3584]{1,0:T(8,128)(2,1)S(1)} %get-tuple-element.40), channel_id=1, source_target_pairs={{0,4},{1,5},{2,6},{3,7},{4,0},{5,1},{6,2},{7,3},{8,12},{9,13},{10,... | collective-permute-start | bytes 172040 | tf_op jit(solution)/shard_map/ppermute | solution.py:31
  48.4 2.4 %collective-permute-start.12 = (bf16[8,3584]{1,0:T(8,128)(2,1)S(1)}, bf16[8,3584]{1,0:T(8,128)(2,1)S(1)}, u32[]{:S(2)}, u32[]{:S(2)}) collective-permute-start(bf16[8,3584]{1,0:T(8,128)(2,1)S(1)} %get-tuple-element.41), channel_id=1, source_target_pairs={{0,8},{1,9},{2,10},{3,11},{4,12},{5,13},{6,14},{7,15},{8,0},{9,1},... | collective-permute-start | bytes 172040 | tf_op jit(solution)/shard_map/ppermute | solution.py:31
  50.7 1.3 %collective-permute-start.13 = (bf16[8,3584]{1,0:T(8,128)(2,1)S(1)}, bf16[8,3584]{1,0:T(8,128)(2,1)S(1)}, u32[]{:S(2)}, u32[]{:S(2)}) collective-permute-start(bf16[8,3584]{1,0:T(8,128)(2,1)S(1)} %get-tuple-element.42), channel_id=1, source_target_pairs={{0,12},{1,13},{2,14},{3,15},{4,8},{5,9},{6,10},{7,11},{8,4},{9,5},... | collective-permute-start | bytes 172040 | tf_op jit(solution)/shard_map/ppermute | solution.py:31
  52.1 0.9 %collective-permute-start.17 = (bf16[8,2560]{1,0:T(8,128)(2,1)S(1)}, bf16[8,2560]{1,0:T(8,128)(2,1)S(1)}, u32[]{:S(2)}, u32[]{:S(2)}) collective-permute-start(bf16[8,2560]{1,0:T(8,128)(2,1)S(1)} %get-tuple-element.48), channel_id=1, source_target_pairs={{0,2},{1,3},{2,0},{3,1},{4,6},{5,7},{6,4},{7,5},{8,10},{9,11},{10,... | collective-permute-start | bytes 122888 | tf_op jit(solution)/shard_map/ppermute | solution.py:31
  53.0 3.2 %collective-permute-done.17.refs_5_ = bf16[8,2560]{1,0:T(8,128)(2,1)S(1)} collective-permute-done((bf16[8,2560]{1,0:T(8,128)(2,1)S(1)}, bf16[8,2560]{1,0:T(8,128)(2,1)S(1)}, u32[]{:S(2)}, u32[]{:S(2)}) %collective-permute-start.17) | collective-permute-done | bytes 40992 | tf_op jit(solution)/shard_map/ppermute | solution.py:31
  56.1 0.6 %collective-permute-done.13.refs_3_ = bf16[8,3584]{1,0:T(8,128)(2,1)S(1)} collective-permute-done((bf16[8,3584]{1,0:T(8,128)(2,1)S(1)}, bf16[8,3584]{1,0:T(8,128)(2,1)S(1)}, u32[]{:S(2)}, u32[]{:S(2)}) %collective-permute-start.13) | collective-permute-done | bytes 57376 | tf_op jit(solution)/shard_map/ppermute | solution.py:31
  56.7 0.7 %sum.1 = bf16[4,2,6144]{2,1,0:T(2,128)(2,1)} custom-call(f32[8,3584]{1,0:T(8,128)S(1)} %get-tuple-element.39.refs_0_, bf16[8,3584]{1,0:T(8,128)(2,1)S(1)} %collective-permute-done.11.refs_1_, bf16[8,3584]{1,0:T(8,128)(2,1)S(1)} %collective-permute-done.12.refs_2_, bf16[8,3584]{1,0:T(8,128)(2,1)S(1)} %collective-permute-done.13.refs_3_, ...), custom_call_target="tpu_custom_call" | custom-call | bytes 196608 | tf_op jit(solution)/shard_map/sum/pallas_call | solution.py:302
  (46 shorter events, 1.6 us)
Async XLA Ops:
  0.9 10.4 %collective-permute-start.2 = (bf16[8,4608]{1,0:T(8,128)(2,1)S(1)}, bf16[8,4608]{1,0:T(8,128)(2,1)S(1)}, u32[]{:S(2)}, u32[]{:S(2)}) collective-permute-start(bf16[8,4608]{1,0:T(8,128)(2,1)S(1)} %get-tuple-element.27.after_ref.refs_0_), channel_id=1, source_target_pairs={{0,12},{1,13},{2,14},{3,15},{4,8},{5,9},{6,10},{7,11},{8,4},{9,5},... | collective-permute-start | bytes 221192 | tf_op jit(solution)/shard_map/ppermute | solution.py:31
  6.1 6.2 %collective-permute-start.1 = (bf16[8,4608]{1,0:T(8,128)(2,1)S(1)}, bf16[8,4608]{1,0:T(8,128)(2,1)S(1)}, u32[]{:S(2)}, u32[]{:S(2)}) collective-permute-start(bf16[8,4608]{1,0:T(8,128)(2,1)S(1)} %get-tuple-element.27.after_ref.refs_0_), channel_id=1, source_target_pairs={{0,8},{1,9},{2,10},{3,11},{4,12},{5,13},{6,14},{7,15},{8,0},{9,1},... | collective-permute-start | bytes 221192 | tf_op jit(solution)/shard_map/ppermute | solution.py:31
  6.1 6.2 %collective-permute-start = (bf16[8,4608]{1,0:T(8,128)(2,1)S(1)}, bf16[8,4608]{1,0:T(8,128)(2,1)S(1)}, u32[]{:S(2)}, u32[]{:S(2)}) collective-permute-start(bf16[8,4608]{1,0:T(8,128)(2,1)S(1)} %get-tuple-element.27.after_ref.refs_0_), channel_id=1, source_target_pairs={{0,4},{1,5},{2,6},{3,7},{4,0},{5,1},{6,2},{7,3},{8,12},{9,13},{10,... | collective-permute-start | bytes 221192 | tf_op jit(solution)/shard_map/ppermute | solution.py:31
  6.7 4.6 %collective-permute-start.3 = (bf16[8,1536]{1,0:T(8,128)(2,1)S(1)}, bf16[8,1536]{1,0:T(8,128)(2,1)S(1)}, u32[]{:S(2)}, u32[]{:S(2)}) collective-permute-start(bf16[8,1536]{1,0:T(8,128)(2,1)S(1)} %get-tuple-element.28.refs_0_), channel_id=1, source_target_pairs={{0,2},{1,3},{2,0},{3,1},{4,6},{5,7},{6,4},{7,5},{8,10},{9,11},{10,... | collective-permute-start | bytes 73736 | tf_op jit(solution)/shard_map/ppermute | solution.py:31
  8.4 15.7 %slice-start = ((s8[25165824]{0:T(1024)(128)(4,1)}), s8[4194304]{0:T(1024)(128)(4,1)S(1)}, s32[]{:S(2)}) async-start(s8[25165824]{0:T(1024)(128)(4,1)} %bitcast.3), calls=%async_computation | async-start | bytes 8388608
  8.4 15.7 %slice-start.1 = ((s8[25165824]{0:T(1024)(128)(4,1)}), s8[4194304]{0:T(1024)(128)(4,1)S(1)}, s32[]{:S(2)}) async-start(s8[25165824]{0:T(1024)(128)(4,1)} %bitcast.3), calls=%async_computation.1 | async-start | bytes 8388608
  8.4 15.7 %slice-start.2 = ((s8[25165824]{0:T(1024)(128)(4,1)}), s8[4194304]{0:T(1024)(128)(4,1)S(1)}, s32[]{:S(2)}) async-start(s8[25165824]{0:T(1024)(128)(4,1)} %bitcast.3), calls=%async_computation.2 | async-start | bytes 8388608
  12.3 11.8 %slice-start.3 = ((s8[25165824]{0:T(1024)(128)(4,1)}), s8[4194304]{0:T(1024)(128)(4,1)S(1)}, s32[]{:S(2)}) async-start(s8[25165824]{0:T(1024)(128)(4,1)} %bitcast.3), calls=%async_computation.3 | async-start | bytes 8388608
  12.4 11.8 %slice-start.4 = ((s8[25165824]{0:T(1024)(128)(4,1)}), s8[4194304]{0:T(1024)(128)(4,1)S(1)}, s32[]{:S(2)}) async-start(s8[25165824]{0:T(1024)(128)(4,1)} %bitcast.3), calls=%async_computation.4 | async-start | bytes 8388608
  12.4 11.8 %slice-start.5 = ((s8[25165824]{0:T(1024)(128)(4,1)}), s8[4194304]{0:T(1024)(128)(4,1)S(1)}, s32[]{:S(2)}) async-start(s8[25165824]{0:T(1024)(128)(4,1)} %bitcast.3), calls=%async_computation.5 | async-start | bytes 8388608
  12.4 9.3 %collective-permute-start.4 = (bf16[32,4608]{1,0:T(8,128)(2,1)S(1)}, bf16[32,4608]{1,0:T(8,128)(2,1)S(1)}, u32[]{:S(2)}, u32[]{:S(2)}) collective-permute-start(bf16[32,4608]{1,0:T(8,128)(2,1)S(1)} %stack.4.after_ref.refs_0_), channel_id=1, source_target_pairs={{0,2},{1,3},{2,0},{3,1},{4,6},{5,7},{6,4},{7,5},{8,10},{9,11},{10,... | collective-permute-start | bytes 884744 | tf_op jit(solution)/shard_map/ppermute | solution.py:31
  14.0 7.5 %collective-permute-start.7 = (bf16[16,1536]{1,0:T(8,128)(2,1)S(1)}, bf16[16,1536]{1,0:T(8,128)(2,1)S(1)}, u32[]{:S(2)}, u32[]{:S(2)}) collective-permute-start(bf16[16,1536]{1,0:T(8,128)(2,1)S(1)} %stack.3.refs_4_.refs_2_), channel_id=1, source_target_pairs={{0,12},{1,13},{2,14},{3,15},{4,8},{5,9},{6,10},{7,11},{8,4},{9,5},... | collective-permute-start | bytes 147464 | tf_op jit(solution)/shard_map/ppermute | solution.py:31
  16.7 5.0 %collective-permute-start.6 = (bf16[16,1536]{1,0:T(8,128)(2,1)S(1)}, bf16[16,1536]{1,0:T(8,128)(2,1)S(1)}, u32[]{:S(2)}, u32[]{:S(2)}) collective-permute-start(bf16[16,1536]{1,0:T(8,128)(2,1)S(1)} %stack.3.refs_4_.refs_2_), channel_id=1, source_target_pairs={{0,8},{1,9},{2,10},{3,11},{4,12},{5,13},{6,14},{7,15},{8,0},{9,1},... | collective-permute-start | bytes 147464 | tf_op jit(solution)/shard_map/ppermute | solution.py:31
  16.7 5.0 %collective-permute-start.5 = (bf16[16,1536]{1,0:T(8,128)(2,1)S(1)}, bf16[16,1536]{1,0:T(8,128)(2,1)S(1)}, u32[]{:S(2)}, u32[]{:S(2)}) collective-permute-start(bf16[16,1536]{1,0:T(8,128)(2,1)S(1)} %stack.3.refs_4_.refs_2_), channel_id=1, source_target_pairs={{0,4},{1,5},{2,6},{3,7},{4,0},{5,1},{6,2},{7,3},{8,12},{9,13},{10,... | collective-permute-start | bytes 147464 | tf_op jit(solution)/shard_map/ppermute | solution.py:31
  21.7 2.4 %collective-permute-start.8 = (bf16[64,6144]{1,0:T(8,128)(2,1)S(1)}, bf16[64,6144]{1,0:T(8,128)(2,1)S(1)}, u32[]{:S(2)}, u32[]{:S(2)}) collective-permute-start(bf16[64,6144]{1,0:T(8,128)(2,1)S(1)} %stack.5.half_ref), channel_id=1, source_target_pairs={{0,1},{1,0},{2,3},{3,2},{4,5},{5,4},{6,7},{7,6},{8,9},{9,8},{10,11... | collective-permute-start | bytes 2359304 | tf_op jit(solution)/shard_map/ppermute | solution.py:31
  37.4 2.4 %collective-permute-start.9 = (bf16[64,6144]{1,0:T(8,128)(2,1)S(1)}, bf16[64,6144]{1,0:T(8,128)(2,1)S(1)}, u32[]{:S(2)}, u32[]{:S(2)}) collective-permute-start(bf16[64,6144]{1,0:T(8,128)(2,1)S(1)} %get-tuple-element.36), channel_id=1, source_target_pairs={{0,1},{1,0},{2,3},{3,2},{4,5},{5,4},{6,7},{7,6},{8,9},{9,8},{10,11... | collective-permute-start | bytes 2359304 | tf_op jit(solution)/shard_map/ppermute | solution.py:31
  39.8 7.7 %collective-permute-start.10 = (bf16[32,3584]{1,0:T(8,128)(2,1)S(1)}, bf16[32,3584]{1,0:T(8,128)(2,1)S(1)}, u32[]{:S(2)}, u32[]{:S(2)}) collective-permute-start(bf16[32,3584]{1,0:T(8,128)(2,1)S(1)} %get-tuple-element.38), channel_id=1, source_target_pairs={{0,2},{1,3},{2,0},{3,1},{4,6},{5,7},{6,4},{7,5},{8,10},{9,11},{10,... | collective-permute-start | bytes 688136 | tf_op jit(solution)/shard_map/ppermute | solution.py:31
  40.8 10.0 %collective-permute-start.14 = (bf16[16,2560]{1,0:T(8,128)(2,1)S(1)}, bf16[16,2560]{1,0:T(8,128)(2,1)S(1)}, u32[]{:S(2)}, u32[]{:S(2)}) collective-permute-start(bf16[16,2560]{1,0:T(8,128)(2,1)S(1)} %get-tuple-element.44), channel_id=1, source_target_pairs={{0,4},{1,5},{2,6},{3,7},{4,0},{5,1},{6,2},{7,3},{8,12},{9,13},{10,... | collective-permute-start | bytes 245768 | tf_op jit(solution)/shard_map/ppermute | solution.py:31
  41.2 10.8 %collective-permute-start.15 = (bf16[16,2560]{1,0:T(8,128)(2,1)S(1)}, bf16[16,2560]{1,0:T(8,128)(2,1)S(1)}, u32[]{:S(2)}, u32[]{:S(2)}) collective-permute-start(bf16[16,2560]{1,0:T(8,128)(2,1)S(1)} %get-tuple-element.45), channel_id=1, source_target_pairs={{0,8},{1,9},{2,10},{3,11},{4,12},{5,13},{6,14},{7,15},{8,0},{9,1},... | collective-permute-start | bytes 245768 | tf_op jit(solution)/shard_map/ppermute | solution.py:31
  43.6 8.4 %collective-permute-start.16 = (bf16[16,2560]{1,0:T(8,128)(2,1)S(1)}, bf16[16,2560]{1,0:T(8,128)(2,1)S(1)}, u32[]{:S(2)}, u32[]{:S(2)}) collective-permute-start(bf16[16,2560]{1,0:T(8,128)(2,1)S(1)} %get-tuple-element.46), channel_id=1, source_target_pairs={{0,12},{1,13},{2,14},{3,15},{4,8},{5,9},{6,10},{7,11},{8,4},{9,5},... | collective-permute-start | bytes 245768 | tf_op jit(solution)/shard_map/ppermute | solution.py:31
  47.5 8.6 %collective-permute-start.11 = (bf16[8,3584]{1,0:T(8,128)(2,1)S(1)}, bf16[8,3584]{1,0:T(8,128)(2,1)S(1)}, u32[]{:S(2)}, u32[]{:S(2)}) collective-permute-start(bf16[8,3584]{1,0:T(8,128)(2,1)S(1)} %get-tuple-element.40), channel_id=1, source_target_pairs={{0,4},{1,5},{2,6},{3,7},{4,0},{5,1},{6,2},{7,3},{8,12},{9,13},{10,... | collective-permute-start | bytes 172040 | tf_op jit(solution)/shard_map/ppermute | solution.py:31
  48.4 7.8 %collective-permute-start.12 = (bf16[8,3584]{1,0:T(8,128)(2,1)S(1)}, bf16[8,3584]{1,0:T(8,128)(2,1)S(1)}, u32[]{:S(2)}, u32[]{:S(2)}) collective-permute-start(bf16[8,3584]{1,0:T(8,128)(2,1)S(1)} %get-tuple-element.41), channel_id=1, source_target_pairs={{0,8},{1,9},{2,10},{3,11},{4,12},{5,13},{6,14},{7,15},{8,0},{9,1},... | collective-permute-start | bytes 172040 | tf_op jit(solution)/shard_map/ppermute | solution.py:31
  50.7 6.0 %collective-permute-start.13 = (bf16[8,3584]{1,0:T(8,128)(2,1)S(1)}, bf16[8,3584]{1,0:T(8,128)(2,1)S(1)}, u32[]{:S(2)}, u32[]{:S(2)}) collective-permute-start(bf16[8,3584]{1,0:T(8,128)(2,1)S(1)} %get-tuple-element.42), channel_id=1, source_target_pairs={{0,12},{1,13},{2,14},{3,15},{4,8},{5,9},{6,10},{7,11},{8,4},{9,5},... | collective-permute-start | bytes 172040 | tf_op jit(solution)/shard_map/ppermute | solution.py:31
  52.1 4.1 %collective-permute-start.17 = (bf16[8,2560]{1,0:T(8,128)(2,1)S(1)}, bf16[8,2560]{1,0:T(8,128)(2,1)S(1)}, u32[]{:S(2)}, u32[]{:S(2)}) collective-permute-start(bf16[8,2560]{1,0:T(8,128)(2,1)S(1)} %get-tuple-element.48), channel_id=1, source_target_pairs={{0,2},{1,3},{2,0},{3,1},{4,6},{5,7},{6,4},{7,5},{8,10},{9,11},{10,... | collective-permute-start | bytes 122888 | tf_op jit(solution)/shard_map/ppermute | solution.py:31
  (4 other events, 27.5 us)

commit v5 on v4

--- a/solution.py
+++ b/solution.py
@@ -141,10 +141,10 @@
 def experts_kernel(
     half_ref, other_ref, route_ref, order_ref, gate_ref, up_ref, down_ref, *refs
 ):
-    early = len(refs) // 2 - 3
-    keep_ref, send_ref = refs[early : early + 2]
-    homes = list(refs[early + 2 : 2 * early + 2])
-    x_ref, h_ref, up_buf, up_sem, down_sem = refs[2 * early + 2 :]
+    early = len(refs) // 2 - 4
+    keep_ref, *send_refs = refs[early : early + 3]
+    homes = list(refs[early + 3 : 2 * early + 3])
+    x_ref, h_ref, up_buf, up_sem, down_sem = refs[2 * early + 3 :]
     half, width = half_ref.shape
     experts, units, _ = down_ref.shape
     depth = experts * units
@@ -188,17 +188,21 @@
         total = jnp.dot(h_ref[...], w[...], preferred_element_type=F32)
         start_blocks(b + slots, b + slots + 1)
         keep_ref[:, b * units : (b + 1) * units] = total[:half]
-        send_ref[:, b * units : (b + 1) * units] = total[half:].astype(BF16)
-
-
-def experts_of(half, other, route, order, w_gate, w_up, w_down, early):
+        send_ref, at = send_refs[0], b * units
+        if at >= send_ref.shape[1]:
+            send_ref, at = send_refs[1], at - send_ref.shape[1]
+        send_ref[:, at : at + units] = total[half:].astype(BF16)
+
+
+def experts_of(half, other, route, order, w_gate, w_up, w_down, early, cut):
     experts, units, width = w_down.shape
     rows = 2 * half.shape[0]
-    keep, send, *_ = pl.pallas_call(
+    keep, first, second, *_ = pl.pallas_call(
         experts_kernel,
         in_specs=[VMEM] * 5 + [ANY] * 2 + [VMEM] * len(early),
-        out_specs=[VMEM] * (2 + len(early)),
-        out_shape=[pltpu.VMEM((rows // 2, width), F32), pltpu.VMEM((rows // 2, width), BF16)]
+        out_specs=[VMEM] * (3 + len(early)),
+        out_shape=[pltpu.VMEM((rows // 2, width), F32)]
+        + [pltpu.VMEM((rows // 2, columns), BF16) for columns in (cut, width - cut)]
         + [pltpu.VMEM(w.shape, w.dtype) for w in early],
         scratch_shapes=[
             pltpu.VMEM((rows, width), BF16),
@@ -207,7 +211,7 @@
             pltpu.SemaphoreType.DMA((experts,)),
             pltpu.SemaphoreType.DMA((width // units,)),
         ],
-        input_output_aliases={7 + i: 2 + i for i in range(len(early))},
+        input_output_aliases={7 + i: 3 + i for i in range(len(early))},
         compiler_params=pltpu.CompilerParams(vmem_limit_bytes=SCOPED * MIB),
         cost_estimate=cost(0, 8 * w_down.size),
         name="experts",
@@ -215,7 +219,7 @@
         in_vmem(half), in_vmem(other), in_vmem(route), in_vmem(order), in_vmem(w_gate), in_hbm(w_up), in_hbm(w_down),
         *[in_vmem(w) for w in early],
     )
-    return keep, send
+    return keep, first, second
 
 
 def add_kernel(first, groups, keep_ref, *refs):
@@ -227,7 +231,8 @@
             rows = slice(block * per, (block + 1) * per)
             total = keep_ref[rows, columns]
             for got_ref in got_refs:
-                total = total + got_ref[rows, columns].astype(F32)
+                same = columns if got_ref.shape == keep_ref.shape else slice(None)
+                total = total + got_ref[rows, same].astype(F32)
             out_ref[i * per : (i + 1) * per] = total.astype(out_ref.dtype)
 
 
@@ -286,14 +291,14 @@
         order,
     )
     other = swap(half, 1)
-    keep, send = experts_of(half, other, route, order, w_gate, w_up, w_down, [up0, up1])
-
-    a = width * 7 // 12
-    b = width - a
-    got = swap(send, 1)
-    keep_a, send_a = add(keep, [got], 0, a, [list(range(far)), list(range(far, 2 * far))])
+    cut = units * (width // units * 7 // 12)
+    keep, send_a, send_b = experts_of(half, other, route, order, w_gate, w_up, w_down, [up0, up1], cut)
+
+    a, b = cut, width - cut
+    got_a, got_b = swap(send_a, 1), swap(send_b, 1)
+    keep_a, send_a = add(keep, [got_a], 0, a, [list(range(far)), list(range(far, 2 * far))])
     got_a = swap(send_a, 2)
-    keep_b, *send_b = add(keep, [got], a, b, [[z, far + z] for z in range(far)])
+    keep_b, *send_b = add(keep, [got_b], a, b, [[z, far + z] for z in range(far)])
     got_b = [swap(send, 4 * (z + 1)) for z, send in enumerate(send_b)]
     keep_a, *send_a = add(keep_a, [got_a], 0, a, [[z] for z in range(far)])
     got_a = [swap(send, 4 * (z + 1)) for z, send in enumerate(send_a)]

time: 57.6 us -> 57.1 us (level)
  waiting for transfers between devices: 11.6 us -> 10.7 us
    ppermute x18 -> x19, waiting for transfers between devices: 11.6 us -> 10.7 us  [swap(): return lax.ppermute(x, 'hid', [(i, i ^ mask) for i in range(n)])]
    ppermute x18 -> x19, starting transfers between devices: 24.4 us -> 24.8 us  [swap(): return lax.ppermute(x, 'hid', [(i, i ^ mask) for i in range(n)])]
  transfers between devices with their start and end apart: 18 -> 19, of which waited for: 7 -> 7; matrix products, arithmetic and copies ran while one was open for 0% -> 0% of each run, Pallas kernels for 11% -> 11%
where the time goes in v5:
time: 57.1 us; the launch traced here: 57 us
  starting transfers between devices  24.8 us (43%)
  Pallas kernels  20.3 us (36%)
  waiting for transfers between devices  10.7 us (19%)
  local copies, waits for them, and re-layouts  0.94 us (2%)
    ppermute x19, starting transfers between devices, swap(): return lax.ppermute(x, 'hid', [(i, i ^ mask) for i in range(n)])  24.8 us
    pallas_call x1, Pallas kernels, experts_of(): pl.pallas_call(experts_kernel, in_specs=[VMEM] * 5 + [ANY] * 2 + [VMEM] *...  13.2 us
    ppermute x19, waiting for transfers between devices, swap(): return lax.ppermute(x, 'hid', [(i, i ^ mask) for i in range(n)])  10.7 us
    pallas_call x2, Pallas kernels, load(): pl.pallas_call(functools.partial(load_kernel, e), in_specs=[ANY, ANY], ou...  5.75 us
  transfers between devices with their start and end apart: 19, of which 7 were waited for; matrix products, arithmetic and copies ran while one was open for 0% of the time, Pallas kernels for 11%

profile of v5, /device:TPU:0, one launch (start us, length us, event | category | flops | bytes accessed | tf_op | source)
XLA Modules:
  0.0 57.0 jit_solution(1524460266374997675)
XLA Ops:
  0.0 0.9 %copy-done = bf16[4,2,6144]{2,1,0:T(2,128)(2,1)S(1)} copy-done((bf16[4,2,6144]{2,1,0:T(2,128)(2,1)S(1)}, bf16[4,2,6144]{2,1,0:T(2,128)(2,1)}, u32[]{:S(2)}) %copy-start) | copy-done | bytes 98328
  0.9 5.1 %collective-permute-start.2 = (bf16[8,4608]{1,0:T(8,128)(2,1)S(1)}, bf16[8,4608]{1,0:T(8,128)(2,1)S(1)}, u32[]{:S(2)}, u32[]{:S(2)}) collective-permute-start(bf16[8,4608]{1,0:T(8,128)(2,1)S(1)} %get-tuple-element.28.after_ref.refs_0_), channel_id=1, source_target_pairs={{0,12},{1,13},{2,14},{3,15},{4,8},{5,9},{6,10},{7,11},{8,4},{9,5},... | collective-permute-start | bytes 221192 | tf_op jit(solution)/shard_map/ppermute | solution.py:31
  6.1 0.6 %collective-permute-start = (bf16[8,4608]{1,0:T(8,128)(2,1)S(1)}, bf16[8,4608]{1,0:T(8,128)(2,1)S(1)}, u32[]{:S(2)}, u32[]{:S(2)}) collective-permute-start(bf16[8,4608]{1,0:T(8,128)(2,1)S(1)} %get-tuple-element.28.after_ref.refs_0_), channel_id=1, source_target_pairs={{0,4},{1,5},{2,6},{3,7},{4,0},{5,1},{6,2},{7,3},{8,12},{9,13},{10,... | collective-permute-start | bytes 221192 | tf_op jit(solution)/shard_map/ppermute | solution.py:31
  6.7 1.7 %collective-permute-start.3 = (bf16[8,1536]{1,0:T(8,128)(2,1)S(1)}, bf16[8,1536]{1,0:T(8,128)(2,1)S(1)}, u32[]{:S(2)}, u32[]{:S(2)}) collective-permute-start(bf16[8,1536]{1,0:T(8,128)(2,1)S(1)} %get-tuple-element.29.refs_0_), channel_id=1, source_target_pairs={{0,2},{1,3},{2,0},{3,1},{4,6},{5,7},{6,4},{7,5},{8,10},{9,11},{10,... | collective-permute-start | bytes 73736 | tf_op jit(solution)/shard_map/ppermute | solution.py:31
  8.4 2.9 %load.2 = (bf16[12,512,512]{2,1,0:T(8,128)(2,1)S(1)}, f32[8,128]{1,0:T(8,128)S(1)}) custom-call(bf16[4,12,512,512]{3,2,1,0:T(8,128)(2,1)} %bitcast.7, bf16[8,4608]{1,0:T(8,128)(2,1)S(1)} %get-tuple-element.28.after_ref.refs_0_), custom_call_target="tpu_custom_call" | custom-call | bytes 6291456 | tf_op jit(solution)/shard_map/load/pallas_call | solution.py:86
  11.4 0.9 %collective-permute-done.1.refs_2_ = bf16[8,4608]{1,0:T(8,128)(2,1)S(1)} collective-permute-done((bf16[8,4608]{1,0:T(8,128)(2,1)S(1)}, bf16[8,4608]{1,0:T(8,128)(2,1)S(1)}, u32[]{:S(2)}, u32[]{:S(2)}) %collective-permute-start.1) | collective-permute-done | bytes 73760 | tf_op jit(solution)/shard_map/ppermute | solution.py:31
  12.4 1.6 %collective-permute-start.4 = (bf16[32,4608]{1,0:T(8,128)(2,1)S(1)}, bf16[32,4608]{1,0:T(8,128)(2,1)S(1)}, u32[]{:S(2)}, u32[]{:S(2)}) collective-permute-start(bf16[32,4608]{1,0:T(8,128)(2,1)S(1)} %stack.4.after_ref.refs_0_), channel_id=1, source_target_pairs={{0,2},{1,3},{2,0},{3,1},{4,6},{5,7},{6,4},{7,5},{8,10},{9,11},{10,... | collective-permute-start | bytes 884744 | tf_op jit(solution)/shard_map/ppermute | solution.py:31
  14.0 2.7 %collective-permute-start.7 = (bf16[16,1536]{1,0:T(8,128)(2,1)S(1)}, bf16[16,1536]{1,0:T(8,128)(2,1)S(1)}, u32[]{:S(2)}, u32[]{:S(2)}) collective-permute-start(bf16[16,1536]{1,0:T(8,128)(2,1)S(1)} %stack.3.refs_4_.refs_2_), channel_id=1, source_target_pairs={{0,12},{1,13},{2,14},{3,15},{4,8},{5,9},{6,10},{7,11},{8,4},{9,5},... | collective-permute-start | bytes 147464 | tf_op jit(solution)/shard_map/ppermute | solution.py:31
  16.7 1.7 %collective-permute-start.5 = (bf16[16,1536]{1,0:T(8,128)(2,1)S(1)}, bf16[16,1536]{1,0:T(8,128)(2,1)S(1)}, u32[]{:S(2)}, u32[]{:S(2)}) collective-permute-start(bf16[16,1536]{1,0:T(8,128)(2,1)S(1)} %stack.3.refs_4_.refs_2_), channel_id=1, source_target_pairs={{0,4},{1,5},{2,6},{3,7},{4,0},{5,1},{6,2},{7,3},{8,12},{9,13},{10,... | collective-permute-start | bytes 147464 | tf_op jit(solution)/shard_map/ppermute | solution.py:31
  18.4 2.8 %load.3 = (bf16[12,512,512]{2,1,0:T(8,128)(2,1)S(1)}, f32[8,128]{1,0:T(8,128)S(1)}) custom-call(bf16[4,12,512,512]{3,2,1,0:T(8,128)(2,1)} %bitcast.8, bf16[32,4608]{1,0:T(8,128)(2,1)S(1)} %stack.4.after_ref.refs_0_), custom_call_target="tpu_custom_call" | custom-call | bytes 6291456 | tf_op jit(solution)/shard_map/load/pallas_call | solution.py:86
  21.8 2.3 %collective-permute-done.8.other_ref = bf16[64,6144]{1,0:T(8,128)(2,1)S(1)} collective-permute-done((bf16[64,6144]{1,0:T(8,128)(2,1)S(1)}, bf16[64,6144]{1,0:T(8,128)(2,1)S(1)}, u32[]{:S(2)}, u32[]{:S(2)}) %collective-permute-start.8) | collective-permute-done | bytes 786464 | tf_op jit(solution)/shard_map/ppermute | solution.py:31
  24.1 13.2 %experts.1 = (f32[64,6144]{1,0:T(8,128)S(1)}, bf16[64,3584]{1,0:T(8,128)(2,1)S(1)}, bf16[64,2560]{1,0:T(8,128)(2,1)S(1)}, bf16[12,512,512]{2,1,0:T(8,128)(2,1)S(1)}, bf16[12,512,512]{2,1,0:T(8,128)(2,1)S(1)}) custom-call(bf16[64,6144]{1,0:T(8,128)(2,1)S(1)} %stack.5.half_ref, ...), custom_call_target="tpu_custom_call", output_to_operand_aliasing={{3}: (7, {}), {4}: (8, {})} | custom-call | bytes 100663296 | tf_op jit(solution)/shard_map/experts/pallas_call | solution.py:200
  37.9 1.3 %collective-permute-done.9.refs_0_ = bf16[64,3584]{1,0:T(8,128)(2,1)S(1)} collective-permute-done((bf16[64,3584]{1,0:T(8,128)(2,1)S(1)}, bf16[64,3584]{1,0:T(8,128)(2,1)S(1)}, u32[]{:S(2)}, u32[]{:S(2)}) %collective-permute-start.9) | collective-permute-done | bytes 458784 | tf_op jit(solution)/shard_map/ppermute | solution.py:31
  39.3 0.9 %collective-permute-start.10 = (bf16[32,3584]{1,0:T(8,128)(2,1)S(1)}, bf16[32,3584]{1,0:T(8,128)(2,1)S(1)}, u32[]{:S(2)}, u32[]{:S(2)}) collective-permute-start(bf16[32,3584]{1,0:T(8,128)(2,1)S(1)} %get-tuple-element.39), channel_id=1, source_target_pairs={{0,2},{1,3},{2,0},{3,1},{4,6},{5,7},{6,4},{7,5},{8,10},{9,11},{10,... | collective-permute-start | bytes 688136 | tf_op jit(solution)/shard_map/ppermute | solution.py:31
  40.8 2.4 %collective-permute-start.16 = (bf16[16,2560]{1,0:T(8,128)(2,1)S(1)}, bf16[16,2560]{1,0:T(8,128)(2,1)S(1)}, u32[]{:S(2)}, u32[]{:S(2)}) collective-permute-start(bf16[16,2560]{1,0:T(8,128)(2,1)S(1)} %get-tuple-element.47), channel_id=1, source_target_pairs={{0,8},{1,9},{2,10},{3,11},{4,12},{5,13},{6,14},{7,15},{8,0},{9,1},... | collective-permute-start | bytes 245768 | tf_op jit(solution)/shard_map/ppermute | solution.py:31
  43.1 1.6 %collective-permute-start.17 = (bf16[16,2560]{1,0:T(8,128)(2,1)S(1)}, bf16[16,2560]{1,0:T(8,128)(2,1)S(1)}, u32[]{:S(2)}, u32[]{:S(2)}) collective-permute-start(bf16[16,2560]{1,0:T(8,128)(2,1)S(1)} %get-tuple-element.48), channel_id=1, source_target_pairs={{0,12},{1,13},{2,14},{3,15},{4,8},{5,9},{6,10},{7,11},{8,4},{9,5},... | collective-permute-start | bytes 245768 | tf_op jit(solution)/shard_map/ppermute | solution.py:31
  44.8 2.3 %collective-permute-done.10.refs_0_ = bf16[32,3584]{1,0:T(8,128)(2,1)S(1)} collective-permute-done((bf16[32,3584]{1,0:T(8,128)(2,1)S(1)}, bf16[32,3584]{1,0:T(8,128)(2,1)S(1)}, u32[]{:S(2)}, u32[]{:S(2)}) %collective-permute-start.10) | collective-permute-done | bytes 229408 | tf_op jit(solution)/shard_map/ppermute | solution.py:31
  47.1 0.8 %collective-permute-start.11 = (bf16[8,3584]{1,0:T(8,128)(2,1)S(1)}, bf16[8,3584]{1,0:T(8,128)(2,1)S(1)}, u32[]{:S(2)}, u32[]{:S(2)}) collective-permute-start(bf16[8,3584]{1,0:T(8,128)(2,1)S(1)} %get-tuple-element.41), channel_id=1, source_target_pairs={{0,4},{1,5},{2,6},{3,7},{4,0},{5,1},{6,2},{7,3},{8,12},{9,13},{10,... | collective-permute-start | bytes 172040 | tf_op jit(solution)/shard_map/ppermute | solution.py:31
  47.9 2.4 %collective-permute-start.12 = (bf16[8,3584]{1,0:T(8,128)(2,1)S(1)}, bf16[8,3584]{1,0:T(8,128)(2,1)S(1)}, u32[]{:S(2)}, u32[]{:S(2)}) collective-permute-start(bf16[8,3584]{1,0:T(8,128)(2,1)S(1)} %get-tuple-element.42), channel_id=1, source_target_pairs={{0,8},{1,9},{2,10},{3,11},{4,12},{5,13},{6,14},{7,15},{8,0},{9,1},... | collective-permute-start | bytes 172040 | tf_op jit(solution)/shard_map/ppermute | solution.py:31
  50.3 1.2 %collective-permute-start.13 = (bf16[8,3584]{1,0:T(8,128)(2,1)S(1)}, bf16[8,3584]{1,0:T(8,128)(2,1)S(1)}, u32[]{:S(2)}, u32[]{:S(2)}) collective-permute-start(bf16[8,3584]{1,0:T(8,128)(2,1)S(1)} %get-tuple-element.43), channel_id=1, source_target_pairs={{0,12},{1,13},{2,14},{3,15},{4,8},{5,9},{6,10},{7,11},{8,4},{9,5},... | collective-permute-start | bytes 172040 | tf_op jit(solution)/shard_map/ppermute | solution.py:31
  51.6 0.9 %collective-permute-start.18 = (bf16[8,2560]{1,0:T(8,128)(2,1)S(1)}, bf16[8,2560]{1,0:T(8,128)(2,1)S(1)}, u32[]{:S(2)}, u32[]{:S(2)}) collective-permute-start(bf16[8,2560]{1,0:T(8,128)(2,1)S(1)} %get-tuple-element.50), channel_id=1, source_target_pairs={{0,2},{1,3},{2,0},{3,1},{4,6},{5,7},{6,4},{7,5},{8,10},{9,11},{10,... | collective-permute-start | bytes 122888 | tf_op jit(solution)/shard_map/ppermute | solution.py:31
  52.5 3.1 %collective-permute-done.18.refs_5_ = bf16[8,2560]{1,0:T(8,128)(2,1)S(1)} collective-permute-done((bf16[8,2560]{1,0:T(8,128)(2,1)S(1)}, bf16[8,2560]{1,0:T(8,128)(2,1)S(1)}, u32[]{:S(2)}, u32[]{:S(2)}) %collective-permute-start.18) | collective-permute-done | bytes 40992 | tf_op jit(solution)/shard_map/ppermute | solution.py:31
  55.7 0.6 %collective-permute-done.13.refs_3_ = bf16[8,3584]{1,0:T(8,128)(2,1)S(1)} collective-permute-done((bf16[8,3584]{1,0:T(8,128)(2,1)S(1)}, bf16[8,3584]{1,0:T(8,128)(2,1)S(1)}, u32[]{:S(2)}, u32[]{:S(2)}) %collective-permute-start.13) | collective-permute-done | bytes 57376 | tf_op jit(solution)/shard_map/ppermute | solution.py:31
  56.3 0.7 %sum.1 = bf16[4,2,6144]{2,1,0:T(2,128)(2,1)} custom-call(f32[8,3584]{1,0:T(8,128)S(1)} %get-tuple-element.40.refs_0_, bf16[8,3584]{1,0:T(8,128)(2,1)S(1)} %collective-permute-done.11.refs_1_, bf16[8,3584]{1,0:T(8,128)(2,1)S(1)} %collective-permute-done.12.refs_2_, bf16[8,3584]{1,0:T(8,128)(2,1)S(1)} %collective-permute-done.13.refs_3_, ...), custom_call_target="tpu_custom_call" | custom-call | bytes 196608 | tf_op jit(solution)/shard_map/sum/pallas_call | solution.py:307
  (48 shorter events, 2.0 us)
Async XLA Ops:
  0.9 10.4 %collective-permute-start.2 = (bf16[8,4608]{1,0:T(8,128)(2,1)S(1)}, bf16[8,4608]{1,0:T(8,128)(2,1)S(1)}, u32[]{:S(2)}, u32[]{:S(2)}) collective-permute-start(bf16[8,4608]{1,0:T(8,128)(2,1)S(1)} %get-tuple-element.28.after_ref.refs_0_), channel_id=1, source_target_pairs={{0,12},{1,13},{2,14},{3,15},{4,8},{5,9},{6,10},{7,11},{8,4},{9,5},... | collective-permute-start | bytes 221192 | tf_op jit(solution)/shard_map/ppermute | solution.py:31
  6.1 6.2 %collective-permute-start.1 = (bf16[8,4608]{1,0:T(8,128)(2,1)S(1)}, bf16[8,4608]{1,0:T(8,128)(2,1)S(1)}, u32[]{:S(2)}, u32[]{:S(2)}) collective-permute-start(bf16[8,4608]{1,0:T(8,128)(2,1)S(1)} %get-tuple-element.28.after_ref.refs_0_), channel_id=1, source_target_pairs={{0,8},{1,9},{2,10},{3,11},{4,12},{5,13},{6,14},{7,15},{8,0},{9,1},... | collective-permute-start | bytes 221192 | tf_op jit(solution)/shard_map/ppermute | solution.py:31
  6.1 6.2 %collective-permute-start = (bf16[8,4608]{1,0:T(8,128)(2,1)S(1)}, bf16[8,4608]{1,0:T(8,128)(2,1)S(1)}, u32[]{:S(2)}, u32[]{:S(2)}) collective-permute-start(bf16[8,4608]{1,0:T(8,128)(2,1)S(1)} %get-tuple-element.28.after_ref.refs_0_), channel_id=1, source_target_pairs={{0,4},{1,5},{2,6},{3,7},{4,0},{5,1},{6,2},{7,3},{8,12},{9,13},{10,... | collective-permute-start | bytes 221192 | tf_op jit(solution)/shard_map/ppermute | solution.py:31
  6.7 4.6 %collective-permute-start.3 = (bf16[8,1536]{1,0:T(8,128)(2,1)S(1)}, bf16[8,1536]{1,0:T(8,128)(2,1)S(1)}, u32[]{:S(2)}, u32[]{:S(2)}) collective-permute-start(bf16[8,1536]{1,0:T(8,128)(2,1)S(1)} %get-tuple-element.29.refs_0_), channel_id=1, source_target_pairs={{0,2},{1,3},{2,0},{3,1},{4,6},{5,7},{6,4},{7,5},{8,10},{9,11},{10,... | collective-permute-start | bytes 73736 | tf_op jit(solution)/shard_map/ppermute | solution.py:31
  8.4 15.7 %slice-start = ((s8[25165824]{0:T(1024)(128)(4,1)}), s8[4194304]{0:T(1024)(128)(4,1)S(1)}, s32[]{:S(2)}) async-start(s8[25165824]{0:T(1024)(128)(4,1)} %bitcast.3), calls=%async_computation | async-start | bytes 8388608
  8.4 15.7 %slice-start.1 = ((s8[25165824]{0:T(1024)(128)(4,1)}), s8[4194304]{0:T(1024)(128)(4,1)S(1)}, s32[]{:S(2)}) async-start(s8[25165824]{0:T(1024)(128)(4,1)} %bitcast.3), calls=%async_computation.1 | async-start | bytes 8388608
  8.4 15.7 %slice-start.2 = ((s8[25165824]{0:T(1024)(128)(4,1)}), s8[4194304]{0:T(1024)(128)(4,1)S(1)}, s32[]{:S(2)}) async-start(s8[25165824]{0:T(1024)(128)(4,1)} %bitcast.3), calls=%async_computation.2 | async-start | bytes 8388608
  12.3 11.8 %slice-start.3 = ((s8[25165824]{0:T(1024)(128)(4,1)}), s8[4194304]{0:T(1024)(128)(4,1)S(1)}, s32[]{:S(2)}) async-start(s8[25165824]{0:T(1024)(128)(4,1)} %bitcast.3), calls=%async_computation.3 | async-start | bytes 8388608
  12.4 11.8 %slice-start.4 = ((s8[25165824]{0:T(1024)(128)(4,1)}), s8[4194304]{0:T(1024)(128)(4,1)S(1)}, s32[]{:S(2)}) async-start(s8[25165824]{0:T(1024)(128)(4,1)} %bitcast.3), calls=%async_computation.4 | async-start | bytes 8388608
  12.4 9.3 %collective-permute-start.4 = (bf16[32,4608]{1,0:T(8,128)(2,1)S(1)}, bf16[32,4608]{1,0:T(8,128)(2,1)S(1)}, u32[]{:S(2)}, u32[]{:S(2)}) collective-permute-start(bf16[32,4608]{1,0:T(8,128)(2,1)S(1)} %stack.4.after_ref.refs_0_), channel_id=1, source_target_pairs={{0,2},{1,3},{2,0},{3,1},{4,6},{5,7},{6,4},{7,5},{8,10},{9,11},{10,... | collective-permute-start | bytes 884744 | tf_op jit(solution)/shard_map/ppermute | solution.py:31
  14.0 7.5 %collective-permute-start.7 = (bf16[16,1536]{1,0:T(8,128)(2,1)S(1)}, bf16[16,1536]{1,0:T(8,128)(2,1)S(1)}, u32[]{:S(2)}, u32[]{:S(2)}) collective-permute-start(bf16[16,1536]{1,0:T(8,128)(2,1)S(1)} %stack.3.refs_4_.refs_2_), channel_id=1, source_target_pairs={{0,12},{1,13},{2,14},{3,15},{4,8},{5,9},{6,10},{7,11},{8,4},{9,5},... | collective-permute-start | bytes 147464 | tf_op jit(solution)/shard_map/ppermute | solution.py:31
  16.7 5.0 %collective-permute-start.6 = (bf16[16,1536]{1,0:T(8,128)(2,1)S(1)}, bf16[16,1536]{1,0:T(8,128)(2,1)S(1)}, u32[]{:S(2)}, u32[]{:S(2)}) collective-permute-start(bf16[16,1536]{1,0:T(8,128)(2,1)S(1)} %stack.3.refs_4_.refs_2_), channel_id=1, source_target_pairs={{0,8},{1,9},{2,10},{3,11},{4,12},{5,13},{6,14},{7,15},{8,0},{9,1},... | collective-permute-start | bytes 147464 | tf_op jit(solution)/shard_map/ppermute | solution.py:31
  16.7 5.0 %collective-permute-start.5 = (bf16[16,1536]{1,0:T(8,128)(2,1)S(1)}, bf16[16,1536]{1,0:T(8,128)(2,1)S(1)}, u32[]{:S(2)}, u32[]{:S(2)}) collective-permute-start(bf16[16,1536]{1,0:T(8,128)(2,1)S(1)} %stack.3.refs_4_.refs_2_), channel_id=1, source_target_pairs={{0,4},{1,5},{2,6},{3,7},{4,0},{5,1},{6,2},{7,3},{8,12},{9,13},{10,... | collective-permute-start | bytes 147464 | tf_op jit(solution)/shard_map/ppermute | solution.py:31
  21.7 2.4 %collective-permute-start.8 = (bf16[64,6144]{1,0:T(8,128)(2,1)S(1)}, bf16[64,6144]{1,0:T(8,128)(2,1)S(1)}, u32[]{:S(2)}, u32[]{:S(2)}) collective-permute-start(bf16[64,6144]{1,0:T(8,128)(2,1)S(1)} %stack.5.half_ref), channel_id=1, source_target_pairs={{0,1},{1,0},{2,3},{3,2},{4,5},{5,4},{6,7},{7,6},{8,9},{9,8},{10,11... | collective-permute-start | bytes 2359304 | tf_op jit(solution)/shard_map/ppermute | solution.py:31
  37.3 1.9 %collective-permute-start.9 = (bf16[64,3584]{1,0:T(8,128)(2,1)S(1)}, bf16[64,3584]{1,0:T(8,128)(2,1)S(1)}, u32[]{:S(2)}, u32[]{:S(2)}) collective-permute-start(bf16[64,3584]{1,0:T(8,128)(2,1)S(1)} %get-tuple-element.37), channel_id=1, source_target_pairs={{0,1},{1,0},{2,3},{3,2},{4,5},{5,4},{6,7},{7,6},{8,9},{9,8},{10,11... | collective-permute-start | bytes 1376264 | tf_op jit(solution)/shard_map/ppermute | solution.py:31
  37.5 2.7 %collective-permute-start.14 = (bf16[64,2560]{1,0:T(8,128)(2,1)S(1)}, bf16[64,2560]{1,0:T(8,128)(2,1)S(1)}, u32[]{:S(2)}, u32[]{:S(2)}) collective-permute-start(bf16[64,2560]{1,0:T(8,128)(2,1)S(1)} %get-tuple-element.44), channel_id=1, source_target_pairs={{0,1},{1,0},{2,3},{3,2},{4,5},{5,4},{6,7},{7,6},{8,9},{9,8},{10,11... | collective-permute-start | bytes 983048 | tf_op jit(solution)/shard_map/ppermute | solution.py:31
  39.3 7.7 %collective-permute-start.10 = (bf16[32,3584]{1,0:T(8,128)(2,1)S(1)}, bf16[32,3584]{1,0:T(8,128)(2,1)S(1)}, u32[]{:S(2)}, u32[]{:S(2)}) collective-permute-start(bf16[32,3584]{1,0:T(8,128)(2,1)S(1)} %get-tuple-element.39), channel_id=1, source_target_pairs={{0,2},{1,3},{2,0},{3,1},{4,6},{5,7},{6,4},{7,5},{8,10},{9,11},{10,... | collective-permute-start | bytes 688136 | tf_op jit(solution)/shard_map/ppermute | solution.py:31
  40.3 10.0 %collective-permute-start.15 = (bf16[16,2560]{1,0:T(8,128)(2,1)S(1)}, bf16[16,2560]{1,0:T(8,128)(2,1)S(1)}, u32[]{:S(2)}, u32[]{:S(2)}) collective-permute-start(bf16[16,2560]{1,0:T(8,128)(2,1)S(1)} %get-tuple-element.46), channel_id=1, source_target_pairs={{0,4},{1,5},{2,6},{3,7},{4,0},{5,1},{6,2},{7,3},{8,12},{9,13},{10,... | collective-permute-start | bytes 245768 | tf_op jit(solution)/shard_map/ppermute | solution.py:31
  40.8 10.8 %collective-permute-start.16 = (bf16[16,2560]{1,0:T(8,128)(2,1)S(1)}, bf16[16,2560]{1,0:T(8,128)(2,1)S(1)}, u32[]{:S(2)}, u32[]{:S(2)}) collective-permute-start(bf16[16,2560]{1,0:T(8,128)(2,1)S(1)} %get-tuple-element.47), channel_id=1, source_target_pairs={{0,8},{1,9},{2,10},{3,11},{4,12},{5,13},{6,14},{7,15},{8,0},{9,1},... | collective-permute-start | bytes 245768 | tf_op jit(solution)/shard_map/ppermute | solution.py:31
  43.1 8.4 %collective-permute-start.17 = (bf16[16,2560]{1,0:T(8,128)(2,1)S(1)}, bf16[16,2560]{1,0:T(8,128)(2,1)S(1)}, u32[]{:S(2)}, u32[]{:S(2)}) collective-permute-start(bf16[16,2560]{1,0:T(8,128)(2,1)S(1)} %get-tuple-element.48), channel_id=1, source_target_pairs={{0,12},{1,13},{2,14},{3,15},{4,8},{5,9},{6,10},{7,11},{8,4},{9,5},... | collective-permute-start | bytes 245768 | tf_op jit(solution)/shard_map/ppermute | solution.py:31
  47.1 8.6 %collective-permute-start.11 = (bf16[8,3584]{1,0:T(8,128)(2,1)S(1)}, bf16[8,3584]{1,0:T(8,128)(2,1)S(1)}, u32[]{:S(2)}, u32[]{:S(2)}) collective-permute-start(bf16[8,3584]{1,0:T(8,128)(2,1)S(1)} %get-tuple-element.41), channel_id=1, source_target_pairs={{0,4},{1,5},{2,6},{3,7},{4,0},{5,1},{6,2},{7,3},{8,12},{9,13},{10,... | collective-permute-start | bytes 172040 | tf_op jit(solution)/shard_map/ppermute | solution.py:31
  47.9 7.7 %collective-permute-start.12 = (bf16[8,3584]{1,0:T(8,128)(2,1)S(1)}, bf16[8,3584]{1,0:T(8,128)(2,1)S(1)}, u32[]{:S(2)}, u32[]{:S(2)}) collective-permute-start(bf16[8,3584]{1,0:T(8,128)(2,1)S(1)} %get-tuple-element.42), channel_id=1, source_target_pairs={{0,8},{1,9},{2,10},{3,11},{4,12},{5,13},{6,14},{7,15},{8,0},{9,1},... | collective-permute-start | bytes 172040 | tf_op jit(solution)/shard_map/ppermute | solution.py:31
  50.3 6.0 %collective-permute-start.13 = (bf16[8,3584]{1,0:T(8,128)(2,1)S(1)}, bf16[8,3584]{1,0:T(8,128)(2,1)S(1)}, u32[]{:S(2)}, u32[]{:S(2)}) collective-permute-start(bf16[8,3584]{1,0:T(8,128)(2,1)S(1)} %get-tuple-element.43), channel_id=1, source_target_pairs={{0,12},{1,13},{2,14},{3,15},{4,8},{5,9},{6,10},{7,11},{8,4},{9,5},... | collective-permute-start | bytes 172040 | tf_op jit(solution)/shard_map/ppermute | solution.py:31
  51.6 4.1 %collective-permute-start.18 = (bf16[8,2560]{1,0:T(8,128)(2,1)S(1)}, bf16[8,2560]{1,0:T(8,128)(2,1)S(1)}, u32[]{:S(2)}, u32[]{:S(2)}) collective-permute-start(bf16[8,2560]{1,0:T(8,128)(2,1)S(1)} %get-tuple-element.50), channel_id=1, source_target_pairs={{0,2},{1,3},{2,0},{3,1},{4,6},{5,7},{6,4},{7,5},{8,10},{9,11},{10,... | collective-permute-start | bytes 122888 | tf_op jit(solution)/shard_map/ppermute | solution.py:31
  (5 other events, 39.2 us)
